TPU v7x, 128 devices: a whole 4x4x4 slice. The times are simulated.
128 devices in a mesh: row: 4 (over y), col: 32 (over z, x, core).
Axes of the slice: x: 4, y: 4, z: 4, core: 2. Of those that a mesh axis runs over, the one named last changes fastest.
Arguments:
- top_boundary: bfloat16 [32, 8, 64, 1024], P('col'), may hold values from -6 to 6
- row_transfer: bfloat16 [4, 32, 8, 256, 256], P('row', 'col'), may hold values from -0.375 to 0.375
- proj_in: bfloat16 [4, 32, 8, 64, 1024], P('row', 'col'), may hold values from -3 to 3
- proj_out: bfloat16 [4, 32, 8, 64, 1024], P('row', 'col'), may hold values from -3 to 3
- bottom_boundary: bfloat16 [4, 32, 8, 64, 1024], P('row', 'col'), may hold values from -6 to 6
- environments: bfloat16 [4, 32, 8, 64, 64], P('row', 'col'), may hold values from -0.09375 to 0.09375
- operators: bfloat16 [2, 8, 16, 16], replicated, may hold values from -1.5 to 1.5
- ranks: int32 [4, 8], P('row'), may hold values from 32 to 64, as said below
Outputs:
- boundaries: bfloat16 [4, 32, 8, 64, 1024], P('row', 'col')
- log_norms: float32 [4, 8], P('row')
- observables: float32 [2, 4, 32, 8], P(None, 'row', 'col')
Inputs may be any that keep to these rules, and one draw needn't show every extreme that they name: `ranks`: in every row at least one sector keeps all 64 slots.
All inputs are finite; a program needn't handle non-finite values.
Results may differ from a plain program's by a relative error of at most 0.034.
Values may be sent and summed in bfloat16 or wider, within the bound.
No kernel may reach another device: no remote copies, remote signals or barrier semaphores. Data moves between devices by JAX's collectives and lax.ppermute only.
A program may use at most 256 MiB of HBM per device.

v0:
```python
import math

import jax
import jax.numpy as jnp
from jax import lax
from jax.sharding import PartitionSpec as P

SEC = 8
PAD = 64
KM = 16
DB = 16


epsilon = 1e-06


def passed_along(block, axis, distance):
    devices = range(lax.axis_size(axis))
    route = [((i - distance) % len(devices), i) for i in devices]
    return lax.ppermute(block, axis, route)


def shifted(block, axis, distance):
    devices = range(lax.axis_size(axis))
    route = [(i - distance, i) for i in devices if i - distance in devices]
    return lax.ppermute(block, axis, route)


def absorb_site(site, transfer, left_proj, right_proj, rank):
    upper = site.reshape(PAD, KM, PAD)
    first = jnp.einsum(
        "caw,akb->cwkb", left_proj.reshape(PAD, PAD, DB), upper, preferred_element_type=jnp.float32
    ).astype(jnp.bfloat16)
    second = jnp.einsum(
        "cwkb,wkle->clbe",
        first,
        transfer.reshape(DB, KM, KM, DB),
        preferred_element_type=jnp.float32,
    ).astype(jnp.bfloat16)
    result = jnp.einsum(
        "clbe,dbe->cld",
        second,
        right_proj.reshape(PAD, PAD, DB),
        preferred_element_type=jnp.float32,
    )
    inside = jnp.arange(PAD, dtype=jnp.int32) < rank
    keep = inside[:, None, None] & inside[None, None, :]
    return jnp.where(keep, result, jnp.zeros_like(result))


def observe_site(site, operators, left_env, right_env, lower):
    upper = site.reshape(PAD, KM, PAD)
    inserted = jnp.einsum(
        "akb,qkl->qalb", upper, operators, preferred_element_type=jnp.float32
    ).astype(jnp.bfloat16)
    carried = jnp.einsum(
        "qalb,bd->qald", inserted, right_env, preferred_element_type=jnp.float32
    ).astype(jnp.bfloat16)
    closed = jnp.einsum(
        "qald,cld->qac", carried, lower.reshape(PAD, KM, PAD), preferred_element_type=jnp.float32
    )
    return jnp.einsum("ac,qac->q", left_env.astype(jnp.float32), closed) / math.sqrt(KM)


def on_device(
    top_boundary, row_transfer, proj_in, proj_out, bottom_boundary, environments, operators, ranks
):
    row_count = lax.axis_size("row")
    row_index = lax.axis_index("row")
    columns = top_boundary.shape[0]
    entries = float(columns * lax.axis_size("col") * PAD * KM * PAD)
    transfer = row_transfer[0]
    left_projs = proj_in[0]
    right_projs = proj_out[0]
    lower_sites = bottom_boundary[0]
    envs_here = environments[0]
    rank_row = ranks[0]
    arrived = passed_along((right_projs, envs_here), "col", -1)
    following = jnp.concatenate([right_projs[1:], arrived[0]], axis=0)
    right_envs = jnp.concatenate([envs_here[1:], arrived[1]], axis=0)
    sector_absorb = jax.vmap(absorb_site, in_axes=(0, 0, 0, 0, 0))
    full_shape = (columns, SEC, PAD, KM, PAD)
    current = top_boundary
    kept = jnp.zeros_like(top_boundary)
    logs = jnp.zeros((SEC,), jnp.float32)
    for turn in range(row_count):

        def absorb_turn(current=current):
            return lax.map(
                lambda pieces: sector_absorb(pieces[0], pieces[1], pieces[2], pieces[3], rank_row),
                (current, transfer, left_projs, following),
            )

        absorbed = lax.cond(
            row_index == turn, absorb_turn, lambda: jnp.zeros(full_shape, jnp.float32)
        )
        sums = lax.psum(jnp.sum(absorbed * absorbed, axis=(0, 2, 3, 4)), "col")
        norm = jnp.sqrt(sums / entries + epsilon)
        fresh = (
            (absorbed / norm[None, :, None, None, None])
            .astype(jnp.bfloat16)
            .reshape(top_boundary.shape)
        )
        mine = row_index == turn
        kept = jnp.where(mine, fresh, kept)
        logs = jnp.where(mine, jnp.log(norm), logs)
        if turn + 1 < row_count:
            current = shifted(fresh, "row", 1)
    sector_observe = jax.vmap(observe_site, in_axes=(0, 1, 0, 0, 0))
    values = lax.map(
        lambda pieces: sector_observe(pieces[0], operators, pieces[1], pieces[2], pieces[3]),
        (kept, envs_here, right_envs, lower_sites),
    )
    return (kept[None], logs[None], values.transpose(2, 0, 1)[:, None])


def solution(mesh):
    in_specs = (
        P("col", None, None, None),
        P("row", "col", None, None, None),
        P("row", "col", None, None, None),
        P("row", "col", None, None, None),
        P("row", "col", None, None, None),
        P("row", "col", None, None, None),
        P(),
        P("row", None),
    )
    out_specs = (P("row", "col", None, None, None), P("row", None), P(None, "row", "col", None))
    return jax.shard_map(
        on_device, mesh=mesh, in_specs=in_specs, out_specs=out_specs, check_vma=False
    )
```

profile of v0, /device:TPU:25, one launch (start us, length us, event | category | flops | bytes accessed | tf_op | source)
XLA Modules:
  0.0 1182.5 jit_solution(348159037297192970)
XLA Ops:
  3.4 11.9 %collective-permute-done = bf16[1,8,64,1024]{3,2,1,0:T(8,128)(2,1)} collective-permute-done((bf16[1,8,64,1024]{3,2,1,0:T(8,128)(2,1)}, bf16[1,8,64,1024]{3,2,1,0:T(8,128)(2,1)}, u32[]{:S(2)}, u32[]{:S(2)}) %collective-permute-start) | collective-permute-done | bytes 1048608 | tf_op jit(solution)/shard_map/ppermute | solution.py:20
  15.3 9.0 conditional.4
  27.0 66.6 %psum.28 = f32[8]{0:T(128)S(1)} all-reduce(f32[8]{0:T(128)S(1)} %multiply_reduce_fusion.3), channel_id=1, replica_groups=mesh['row'=4,'col'=32] {'col'}, use_global_device_ids=true, to_apply=%region_3.4 | all-reduce | flops 8 | bytes 64 | tf_op jit(solution)/shard_map/psum | solution.py:97
  100.3 4.1 reshape.388
  105.7 19.9 %collective-permute-done.1 = bf16[1,8,64,1024]{3,2,1,0:T(8,128)(2,1)} collective-permute-done((bf16[1,8,64,1024]{3,2,1,0:T(8,128)(2,1)}, bf16[1,8,64,1024]{3,2,1,0:T(8,128)(2,1)}, u32[]{:S(2)}, u32[]{:S(2)}) %collective-permute-start.1) | collective-permute-done | bytes 1048608 | tf_op jit(solution)/shard_map/ppermute | solution.py:26
  125.6 8.6 conditional.5
  137.0 68.6 %psum.29 = f32[8]{0:T(128)S(1)} all-reduce(f32[8]{0:T(128)S(1)} %multiply_reduce_fusion.2), channel_id=1, replica_groups=mesh['row'=4,'col'=32] {'col'}, use_global_device_ids=true, to_apply=%region_7.8 | all-reduce | flops 8 | bytes 64 | tf_op jit(solution)/shard_map/psum | solution.py:97
  211.3 4.1 reshape.389
  216.6 22.9 %collective-permute-done.2 = bf16[1,8,64,1024]{3,2,1,0:T(8,128)(2,1)} collective-permute-done((bf16[1,8,64,1024]{3,2,1,0:T(8,128)(2,1)}, bf16[1,8,64,1024]{3,2,1,0:T(8,128)(2,1)}, u32[]{:S(2)}, u32[]{:S(2)}) %collective-permute-start.2) | collective-permute-done | bytes 1048608 | tf_op jit(solution)/shard_map/ppermute | solution.py:26
  239.5 9.1 conditional.6
  251.4 65.6 %psum.30 = f32[8]{0:T(128)S(1)} all-reduce(f32[8]{0:T(128)S(1)} %multiply_reduce_fusion.1), channel_id=1, replica_groups=mesh['row'=4,'col'=32] {'col'}, use_global_device_ids=true, to_apply=%region_11.12 | all-reduce | flops 8 | bytes 64 | tf_op jit(solution)/shard_map/psum | solution.py:97
  322.6 4.1 reshape.390
  328.7 570.4 %collective-permute-done.3 = bf16[1,8,64,1024]{3,2,1,0:T(8,128)(2,1)} collective-permute-done((bf16[1,8,64,1024]{3,2,1,0:T(8,128)(2,1)}, bf16[1,8,64,1024]{3,2,1,0:T(8,128)(2,1)}, u32[]{:S(2)}, u32[]{:S(2)}) %collective-permute-start.3) | collective-permute-done | bytes 1048608 | tf_op jit(solution)/shard_map/ppermute | solution.py:26
  899.2 191.5 %conditional.7 = (f32[1,8,64,16,64]{4,2,3,1,0:T(8,128)}) conditional(s32[]{:T(128)} %convert_element_type.81, () %tuple.42, (s32[1,8]{1,0:T(1,128)S(1)}, bf16[1,8,64,1024]{2,3,1,0:T(8,128)(2,1)S(1)}, bf16[1,8,64,1024]{3,2,1,0:T(8,128)(2,1)}, bf16[1,8,256,256]{3,2,1,0:T(8,128)(2,1)S(1)}, bf16[1,8,64,1024]{3,2,1,0:T(8,128)(2,1)}) %tuple.77), branch_computations={%region_12.13_spmd, %region_13.14_spmd} | conditional | flops 6459785728 | bytes 79758376 | solution.py:94
  899.2 4.0 reshape.381
  903.2 15.3 %convert_bitcast_fusion.3 = bf16[8,64,16,16,64,1]{4,1,3,2,0,5:T(8,128)(2,1)} fusion(bf16[8,64,16,64,1]{3,2,1,0,4:T(8,128)(2,1)} %bitcast.185, bf16[8,64,64,16,1]{1,3,2,0,4:T(8,128)(2,1)S(1)} %bitcast.172), kind=kOutput, calls=%fused_computation.51 | convolution fusion | flops 1082130432 | bytes 18874368 | tf_op jit(solution)/shard_map/cond/branch_1_fun/while/body/eval_jaxpr/vmap(caw,akb->cwkb)/dot_general | solution.py:31
  918.5 7.5 reshape.382
  926.0 74.9 %fusion.42 = bf16[8,64,16,64,16]{3,4,2,1,0:T(8,128)(2,1)} fusion(bf16[8,64,16,16,64,1]{4,1,3,2,0,5:T(8,128)(2,1)} %convert_bitcast_fusion.3, bf16[8,16,16,16,16,1]{4,3,2,1,0,5:T(8,128)(2,1)} %bitcast.176), kind=kOutput, calls=%fused_computation.46 | convolution fusion | flops 4303355904 | bytes 34603008 | tf_op jit(solution)/shard_map/cond/branch_1_fun/while/body/eval_jaxpr/vmap(cwkb,wkle->clbe)/dot_general | solution.py:34
  1003.2 80.2 %fusion.50 = f32[1,8,64,16,64]{4,2,3,1,0:T(8,128)} fusion(bf16[8,64,16,64,16]{3,4,2,1,0:T(8,128)(2,1)} %fusion.42, bf16[8,64,64,16,1]{1,3,2,0,4:T(8,128)(2,1)S(1)} %bitcast.190, pred[8,64,64]{2,1,0:T(8,128)(4,1)S(1)} %broadcast_and_fusion.3), kind=kOutput, calls=%fused_computation.54 | convolution fusion | flops 1074266112 | bytes 19955712 | tf_op jit(solution)/shard_map/cond/branch_1_fun/while/body/eval_jaxpr/vmap(clbe,dbe->cld)/dot_general | solution.py:40
  1090.7 2.8 multiply_reduce_fusion
  1095.9 63.2 %psum.31 = f32[8]{0:T(128)S(1)} all-reduce(f32[8]{0:T(128)S(1)} %multiply_reduce_fusion), channel_id=1, replica_groups=mesh['row'=4,'col'=32] {'col'}, use_global_device_ids=true, to_apply=%region_15.16 | all-reduce | flops 8 | bytes 64 | tf_op jit(solution)/shard_map/psum | solution.py:97
  1159.7 7.0 fusion.64
  1166.7 3.7 convert_bitcast_fusion.4
  1171.7 6.8 fusion.67
  (50 shorter events, 51.3 us)
Async XLA Ops:
  0.6 1166.0 %copy-start = (bf16[2,8,16,16]{3,2,1,0:T(8,128)(2,1)S(1)}, bf16[2,8,16,16]{3,2,1,0:T(8,128)(2,1)}, u32[]{:S(2)}) copy-start(bf16[2,8,16,16]{3,2,1,0:T(8,128)(2,1)} %param.22) | copy-start | bytes 24580
  0.6 14.6 %collective-permute-start = (bf16[1,8,64,1024]{3,2,1,0:T(8,128)(2,1)}, bf16[1,8,64,1024]{3,2,1,0:T(8,128)(2,1)}, u32[]{:S(2)}, u32[]{:S(2)}) collective-permute-start(bf16[1,8,64,1024]{3,2,1,0:T(8,128)(2,1)} %bitcast.192), channel_id=1, source_target_pairs={{1,0},{2,1},{3,2},{4,3},{5,4},{6,5},{7,6},{8,7},{9,8},{10,9},{11,1... | collective-permute-start | bytes 3145736 | tf_op jit(solution)/shard_map/ppermute | solution.py:20
  93.6 0.5 copy-start.6
  94.1 0.6 copy-start.4
  97.5 28.1 %copy-start.1 = (bf16[1,1,8,256,256]{4,3,2,1,0:T(8,128)(2,1)S(1)}, bf16[1,1,8,256,256]{4,3,2,1,0:T(8,128)(2,1)}, u32[]{:S(2)}) copy-start(bf16[1,1,8,256,256]{4,3,2,1,0:T(8,128)(2,1)} %param.17) | copy-start | bytes 3145732
  97.6 28.0 %copy-start.9 = (s32[1,8]{1,0:T(1,128)S(1)}, s32[1,8]{1,0:T(1,128)}, u32[]{:S(2)}) copy-start(s32[1,8]{1,0:T(1,128)} %param.23) | copy-start | bytes 100
  104.4 21.2 %collective-permute-start.1 = (bf16[1,8,64,1024]{3,2,1,0:T(8,128)(2,1)}, bf16[1,8,64,1024]{3,2,1,0:T(8,128)(2,1)}, u32[]{:S(2)}, u32[]{:S(2)}) collective-permute-start(bf16[1,8,64,1024]{3,2,1,0:T(8,128)(2,1)} %reshape.388), channel_id=1, source_target_pairs={{0,32},{32,64},{64,96},{1,33},{33,65},{65,97},{2,34},{34,66},{66,9... | collective-permute-start | bytes 3145736 | tf_op jit(solution)/shard_map/ppermute | solution.py:26
  215.3 24.2 %collective-permute-start.2 = (bf16[1,8,64,1024]{3,2,1,0:T(8,128)(2,1)}, bf16[1,8,64,1024]{3,2,1,0:T(8,128)(2,1)}, u32[]{:S(2)}, u32[]{:S(2)}) collective-permute-start(bf16[1,8,64,1024]{3,2,1,0:T(8,128)(2,1)} %reshape.389), channel_id=1, source_target_pairs={{0,32},{32,64},{64,96},{1,33},{33,65},{65,97},{2,34},{34,66},{66,9... | collective-permute-start | bytes 3145736 | tf_op jit(solution)/shard_map/ppermute | solution.py:26
  319.9 8.2 copy-start.8
  326.7 572.4 %collective-permute-start.3 = (bf16[1,8,64,1024]{3,2,1,0:T(8,128)(2,1)}, bf16[1,8,64,1024]{3,2,1,0:T(8,128)(2,1)}, u32[]{:S(2)}, u32[]{:S(2)}) collective-permute-start(bf16[1,8,64,1024]{3,2,1,0:T(8,128)(2,1)} %reshape.390), channel_id=1, source_target_pairs={{0,32},{32,64},{64,96},{1,33},{33,65},{65,97},{2,34},{34,66},{66,9... | collective-permute-start | bytes 3145736 | tf_op jit(solution)/shard_map/ppermute | solution.py:26
  328.0 843.7 %collective-permute-start.4 = (bf16[1,8,64,64]{3,2,1,0:T(8,128)(2,1)S(1)}, bf16[1,8,64,64]{3,2,1,0:T(8,128)(2,1)S(1)}, u32[]{:S(2)}, u32[]{:S(2)}) collective-permute-start(bf16[1,8,64,64]{3,2,1,0:T(8,128)(2,1)S(1)} %bitcast.193), channel_id=1, source_target_pairs={{1,0},{2,1},{3,2},{4,3},{5,4},{6,5},{7,6},{8,7},{9,8},{10,9},{11,1... | collective-permute-start | bytes 196616 | tf_op jit(solution)/shard_map/ppermute | solution.py:20
  1090.7 2.9 copy-start.3
  1090.7 68.4 %copy-start.7 = (f32[8]{0:T(128)S(1)}, f32[8]{0:T(128)}, u32[]{:S(2)}) copy-start(f32[8]{0:T(128)} %copy-done.6) | copy-start | bytes 100
  1090.7 68.9 %copy-start.5 = (f32[8]{0:T(128)S(1)}, f32[8]{0:T(128)}, u32[]{:S(2)}) copy-start(f32[8]{0:T(128)} %copy-done.4) | copy-start | bytes 100
where the time goes:
time: 1190 us; the launch traced here: 1180 us
  waiting for transfers between devices  625 us (53%)
  blocking collectives  264 us (22%)
  matrix products  182 us (15%)
  local copies, waits for them, and re-layouts  50.8 us (4%)
  other arithmetic  28 us (2%)
  loops' own time  26.5 us (2%)
    ppermute x3, waiting for transfers between devices, shifted(): return lax.ppermute(block, axis, route)  613 us
    psum x4, blocking collectives, on_device(): sums = lax.psum(jnp.sum(absorbed * absorbed, axis=(0, 2, 3, 4)), 'col')  264 us
    dot_general x1, matrix products, absorb_site(): jnp.einsum('clbe,dbe->cld', second, right_proj.reshape(PAD, PAD, DB), pre...  80.2 us
    dot_general x1, matrix products, absorb_site(): jnp.einsum('cwkb,wkle->clbe', first, transfer.reshape(DB, KM, KM, DB), pr...  74.9 us
    another operation x4, loops' own time, on_device(): lax.cond(row_index == turn, absorb_turn, lambda: jnp.zeros(full_shape, jn...  26.5 us
  transfers between devices with their start and end apart: 5, of which 4 were waited for; matrix products, arithmetic and copies ran while one was open for 17% of the time, Pallas kernels for 0%

commit v1 on v0

v1 whole, which is shorter than its diff:
```python
import math

import jax
import jax.numpy as jnp
from jax import lax
from jax.experimental import pallas as pl
from jax.experimental.pallas import tpu as pltpu
from jax.sharding import PartitionSpec as P

SEC = 8
PAD = 64
KM = 16
DB = 16
ROWS = 4
WIDE = 256
GROUPS = WIDE // PAD
SITE = KM * PAD

BF16 = jnp.bfloat16
F32 = jnp.float32

epsilon = 1e-06


def mm(a, b):
    return jnp.dot(a, b, preferred_element_type=F32)


def mmt(a, b):
    return lax.dot_general(a, b, (((1,), (1,)), ((), ())), preferred_element_type=F32)


def iota2(shape, dim):
    return lax.broadcasted_iota(jnp.int32, shape, dim)


def digit_swap():
    i, j = iota2((WIDE, WIDE), 0), iota2((WIDE, WIDE), 1)
    return jnp.where((i // 16 == j % 16) & (i % 16 == j // 16), 1.0, 0.0).astype(BF16)


def bond_swap():
    i, j = iota2((SITE, SITE), 0), iota2((SITE, SITE), 1)
    return ((i // DB == j % PAD) & (i % DB == j // PAD)).astype(BF16)


def total(x):
    return jnp.sum(jnp.sum(x, axis=1, keepdims=True), axis=0, keepdims=True)


def chain_kernel(
    pt_ref, q_ref, m_ref, perm_ref, u_ref, st_ref, bdm, bdq, xs, ys, pw, qw, stack
):
    swap = digit_swap()
    bdm[...] = jnp.zeros_like(bdm)
    bdq[...] = jnp.zeros_like(bdq)
    for src, dst in ((pt_ref.at[:, 0], pw), (q_ref.at[:, 0], qw)):
        acc = None
        for part in range(4):
            rows = src[:, part * PAD : (part + 1) * PAD, :].reshape(ROWS * PAD, WIDE)
            term = mm(rows, perm_ref[part * WIDE : (part + 1) * WIDE, :])
            acc = term if acc is None else acc + term
        dst[...] = acc.astype(BF16)
    for r in range(ROWS):
        site = m_ref if r == 0 else u_ref.at[r - 1]
        base = r * PAD
        for k in range(KM):
            lanes = slice(k * PAD, (k + 1) * PAD)
            block = site[:, lanes]
            right = qw[base : base + PAD, lanes]
            for g in range(GROUPS):
                at = slice(g * PAD, (g + 1) * PAD)
                bdm[k, at, at] = block
                bdq[at, k * WIDE + g * PAD : k * WIDE + (g + 1) * PAD] = right
                stack[k * 16 : (k + 1) * 16, at] = pw[base + g * 16 : base + (g + 1) * 16, lanes]
        left = mm(swap, stack[...]).astype(BF16)
        middle = mm(mmt(swap, pt_ref[r, 1]).astype(BF16), swap).astype(BF16)
        for k in range(KM):
            first = mm(left, bdm[k]).astype(BF16)
            xs[:, k * 16 : (k + 1) * 16, :] = first.reshape(16, 16, WIDE)
        for c in range(16):
            second = mm(middle, xs[c]).astype(BF16)
            for e in range(DB):
                ys[c * 16 : (c + 1) * 16, e * WIDE : (e + 1) * WIDE] = second[e * 16 : (e + 1) * 16]
        z = mmt(ys[...], bdq[...])
        top = jnp.max(jnp.max(jnp.abs(z), axis=1, keepdims=True), axis=0, keepdims=True)
        top = jnp.where(top > 0, top, 1.0)
        u = z / top
        st_ref[2 * r : 2 * r + 1, :] = jnp.broadcast_to(top, (1, 128))
        st_ref[2 * r + 1 : 2 * r + 2, :] = jnp.broadcast_to(total(u * u), (1, 128))
        placed = mm(swap, u.astype(BF16)).astype(BF16)
        for l in range(KM):
            for g in range(GROUPS):
                u_ref[r, g * 16 : (g + 1) * 16, l * PAD : (l + 1) * PAD] = placed[
                    l * 16 : (l + 1) * 16, g * PAD : (g + 1) * PAD
                ]


def vmem(count):
    return [pl.BlockSpec(memory_space=pltpu.VMEM)] * count


def chain(pt, q, m, perm, name):
    return pl.pallas_call(
        chain_kernel,
        out_shape=(
            jax.ShapeDtypeStruct((ROWS, PAD, SITE), BF16),
            jax.ShapeDtypeStruct((2 * ROWS, 128), F32),
        ),
        in_specs=vmem(4),
        out_specs=tuple(vmem(2)),
        scratch_shapes=[
            pltpu.VMEM((KM, WIDE, WIDE), BF16),
            pltpu.VMEM((WIDE, DB * WIDE), BF16),
            pltpu.VMEM((16, WIDE, WIDE), BF16),
            pltpu.VMEM((WIDE, DB * WIDE), BF16),
            pltpu.VMEM((ROWS * PAD, SITE), BF16),
            pltpu.VMEM((ROWS * PAD, SITE), BF16),
            pltpu.VMEM((WIDE, WIDE), BF16),
        ],
        compiler_params=pltpu.CompilerParams(vmem_limit_bytes=24 << 20),
        cost_estimate=pl.CostEstimate(
            flops=8_000_000_000, bytes_accessed=4 << 20, transcendentals=0
        ),
        name=name,
    )(pt, q, m, perm)


def weight_kernel(b_ref, el_ref, er_ref, op_ref, w_ref, bde, stack):
    bde[...] = jnp.zeros_like(bde)
    spread = jnp.where(iota2((WIDE, KM), 0) // 16 == iota2((WIDE, KM), 1), 1.0, 0.0).astype(BF16)
    same = iota2((WIDE, WIDE), 0) % 16 == iota2((WIDE, WIDE), 1) % 16

    def sector(s, carry):
        upper = mm(el_ref[s], b_ref[s]).astype(BF16)
        for g in range(GROUPS):
            at = slice(g * PAD, (g + 1) * PAD)
            bde[at, at] = er_ref[s]
        for g in range(4):
            both = mmt(upper[:, g * WIDE : (g + 1) * WIDE], bde[...]).astype(BF16)
            for i in range(4):
                l = g * 4 + i
                for h in range(GROUPS):
                    stack[l * 16 : (l + 1) * 16, h * PAD : (h + 1) * PAD] = both[
                        h * 16 : (h + 1) * 16, i * PAD : (i + 1) * PAD
                    ]
        for q in range(2):
            grown = mmt(mm(spread, op_ref[q, s]).astype(BF16), spread)
            grown = jnp.where(same, grown, 0.0).astype(BF16)
            out = mm(grown, stack[...]).astype(BF16)
            for k in range(KM):
                for h in range(GROUPS):
                    w_ref[q, s, h * 16 : (h + 1) * 16, k * PAD : (k + 1) * PAD] = out[
                        k * 16 : (k + 1) * 16, h * PAD : (h + 1) * PAD
                    ]
        return carry

    lax.fori_loop(0, SEC, sector, 0)


def observable_weights(lower, left_env, right_env, operators):
    return pl.pallas_call(
        weight_kernel,
        out_shape=jax.ShapeDtypeStruct((2, SEC, PAD, SITE), BF16),
        in_specs=vmem(4),
        out_specs=vmem(1)[0],
        scratch_shapes=[pltpu.VMEM((WIDE, WIDE), BF16), pltpu.VMEM((WIDE, WIDE), BF16)],
        compiler_params=pltpu.CompilerParams(vmem_limit_bytes=16 << 20),
        cost_estimate=pl.CostEstimate(
            flops=4_000_000_000, bytes_accessed=4 << 20, transcendentals=0
        ),
        name="observable_weights",
    )(lower, left_env, right_env, operators)


def observe_kernel(u1_ref, u2_ref, w_ref, o_ref):
    values = jnp.zeros((2, SEC), F32)
    at_q, at_s = iota2((2, SEC), 0), iota2((2, SEC), 1)
    for s in range(SEC):
        u = (u1_ref, u2_ref)[s % 2][s // 2].astype(F32)
        for q in range(2):
            here = total(u * w_ref[q, s].astype(F32))
            values = jnp.where((at_q == q) & (at_s == s), here, values)
    o_ref[...] = values


def observe(u1, u2, weights):
    return pl.pallas_call(
        observe_kernel,
        out_shape=jax.ShapeDtypeStruct((2, SEC), F32),
        in_specs=vmem(3),
        out_specs=vmem(1)[0],
        compiler_params=pltpu.CompilerParams(vmem_limit_bytes=16 << 20),
        cost_estimate=pl.CostEstimate(flops=2_000_000, bytes_accessed=3 << 20, transcendentals=0),
        name="observe",
    )(u1, u2, weights)


def finish_kernel(entries, where_ref, g_ref, raw_ref, u1_ref, u2_ref, out_ref, log_ref, obs_ref):
    row, col = where_ref[0], where_ref[1]
    columns = g_ref.shape[0]
    scale = jnp.ones((columns, SEC), F32)
    factor = jnp.zeros((columns, SEC), F32)
    logs = jnp.zeros((1, SEC), F32)
    for r in range(ROWS):
        size = scale * g_ref[:, r * SEC : (r + 1) * SEC]
        squares = size * size * g_ref[:, (ROWS + r) * SEC : (ROWS + r + 1) * SEC]
        norm = jnp.sqrt(jnp.sum(squares, axis=0, keepdims=True) / entries + epsilon)
        scale = size / norm
        factor = jnp.where(row == r, scale, factor)
        logs = jnp.where(row == r, jnp.log(norm), logs)
    factor = jnp.sum(
        jnp.where(iota2((columns, SEC), 0) == col, factor, 0.0), axis=0, keepdims=True
    )
    log_ref[...] = logs
    obs_ref[...] = raw_ref[...] * (factor / math.sqrt(KM))
    for s in range(SEC):
        u = (u1_ref, u2_ref)[s % 2][s // 2].astype(F32)
        out_ref[s] = (u * factor[:, s : s + 1]).astype(BF16)


def finish(entries, where, gathered, raw, u1, u2):
    return pl.pallas_call(
        lambda *refs: finish_kernel(entries, *refs),
        out_shape=(
            jax.ShapeDtypeStruct((SEC, PAD, SITE), BF16),
            jax.ShapeDtypeStruct((1, SEC), F32),
            jax.ShapeDtypeStruct((2, SEC), F32),
        ),
        in_specs=[pl.BlockSpec(memory_space=pltpu.SMEM)] + vmem(4),
        out_specs=tuple(vmem(3)),
        compiler_params=pltpu.CompilerParams(vmem_limit_bytes=16 << 20),
        cost_estimate=pl.CostEstimate(flops=2_000_000, bytes_accessed=2 << 20, transcendentals=0),
        name="finish",
    )(where, gathered, raw, u1, u2)


def passed_along(block, axis, distance):
    devices = range(lax.axis_size(axis))
    route = [((i - distance) % len(devices), i) for i in devices]
    return lax.ppermute(block, axis, route)


def across_rows(block):
    return lax.all_to_all(block, "row", 0, 0)


def parts(x, k):
    x = x.reshape(ROWS, 2, PAD, GROUPS, WIDE)[:, k]
    return x.transpose(0, 2, 1, 3).reshape(ROWS, 1, WIDE, WIDE)


def on_device(
    top_boundary, row_transfer, proj_in, proj_out, bottom_boundary, environments, operators, ranks
):
    row, col = lax.axis_index("row"), lax.axis_index("col")
    columns = lax.axis_size("col")
    inside = jnp.arange(PAD, dtype=jnp.int32)[None, :, None] < ranks[0][:, None, None]
    zero = jnp.zeros((), BF16)
    lefts = jnp.where(inside, proj_in[0, 0], zero)
    rights = jnp.where(inside, proj_out[0, 0], zero)
    transfers = row_transfer[0, 0].reshape(ROWS, 2, WIDE, WIDE)
    envs = environments[0, 0]
    perm = bond_swap()

    def lefts_and_transfers(k):
        return jnp.concatenate([parts(lefts, k), transfers[:, k : k + 1]], axis=1)

    pt1 = across_rows(lefts_and_transfers(0))
    next1 = passed_along(parts(rights, 0), "col", -1)
    next2 = passed_along(parts(rights, 1), "col", -1)
    next_envs = passed_along(envs, "col", -1)
    q1 = across_rows(next1)
    pt2 = across_rows(lefts_and_transfers(1))
    q2 = across_rows(next2)
    weights = observable_weights(bottom_boundary[0, 0], envs, next_envs, operators)
    mine = lax.dynamic_slice_in_dim(top_boundary[0], 2 * row, 2, axis=0)
    u1, st1 = chain(pt1, q1, mine[0], perm, "chain_first")
    got1 = across_rows(u1)
    u2, st2 = chain(pt2, q2, mine[1], perm, "chain_second")
    got2 = across_rows(u2)
    stats = jnp.stack([st1[:, 0], st2[:, 0]])
    stats = across_rows(jnp.broadcast_to(stats[None], (ROWS, 2, 2 * ROWS)))
    stats = stats.reshape(SEC, ROWS, 2).transpose(2, 1, 0).reshape(1, 2 * ROWS * SEC)
    gathered = lax.all_to_all(
        jnp.broadcast_to(stats[None], (columns, 1, 2 * ROWS * SEC)), "col", 0, 0
    ).reshape(columns, 2 * ROWS * SEC)
    raw = observe(got1, got2, weights)
    entries = float(columns * PAD * KM * PAD)
    place = jnp.stack([row, col]).astype(jnp.int32)
    sites, logs, values = finish(entries, place, gathered, raw, got1, got2)
    return sites[None, None], logs, values[:, None, None]


def solution(mesh):
    in_specs = (
        P("col", None, None, None),
        P("row", "col", None, None, None),
        P("row", "col", None, None, None),
        P("row", "col", None, None, None),
        P("row", "col", None, None, None),
        P("row", "col", None, None, None),
        P(),
        P("row", None),
    )
    out_specs = (P("row", "col", None, None, None), P("row", None), P(None, "row", "col", None))
    return jax.shard_map(
        on_device, mesh=mesh, in_specs=in_specs, out_specs=out_specs, check_vma=False
    )
```

time: 1190 us -> 152 us (0.13)
  the two profiles are of different devices: /device:TPU:25 before, /device:TPU:1 now
where the time goes in v1:
time: 152 us; the launch traced here: 151 us
  starting transfers between devices  49.2 us (32%)
  Pallas kernels  44.3 us (29%)
  waiting for transfers between devices  24.4 us (16%)
  blocking collectives  17.4 us (11%)
  local copies, waits for them, and re-layouts  9.8 us (6%)
  other arithmetic  4.75 us (3%)
    pallas_call x2, Pallas kernels, chain(): pl.pallas_call(chain_kernel, out_shape=(jax.ShapeDtypeStruct((ROWS, PAD,...  34.4 us
    all_to_all x5, waiting for transfers between devices, across_rows(): return lax.all_to_all(block, 'row', 0, 0)  24.4 us
    all_to_all x5, starting transfers between devices, across_rows(): return lax.all_to_all(block, 'row', 0, 0)  20.5 us
    all_to_all x2, blocking collectives, across_rows(): return lax.all_to_all(block, 'row', 0, 0)  17.4 us
    all_to_all x1, starting transfers between devices, on_device(): lax.all_to_all(jnp.broadcast_to(stats[None], (columns, 1, 2 * ROWS * SEC)...  15.5 us
    ppermute x3, starting transfers between devices, passed_along(): return lax.ppermute(block, axis, route)  13.2 us
    pallas_call x1, Pallas kernels, observable_weights(): pl.pallas_call(weight_kernel, out_shape=jax.ShapeDtypeStruct((2, SEC, PAD...  7.37 us
  transfers between devices with their start and end apart: 9, of which 3 were waited for; matrix products, arithmetic and copies ran while one was open for 3% of the time, Pallas kernels for 17%

profile of v1, /device:TPU:1, one launch (start us, length us, event | category | flops | bytes accessed | tf_op | source)
XLA Modules:
  0.0 150.8 jit_solution(16895996685854169596)
XLA Ops:
  0.7 2.2 %fusion.15 = (bf16[4,1,256,256]{3,2,1,0:T(8,128)(2,1)}, bf16[4,1,256,256]{3,2,1,0:T(8,128)(2,1)S(1)}) fusion(bf16[4,2,256,256]{3,2,1,0:T(8,128)(2,1)} %bitcast.47), kind=kLoop, calls=%fused_computation.35 | loop fusion | bytes 2097152 | tf_op jit(solution)/shard_map/slice | solution.py:267
  5.1 1.9 %squeeze.31 = bf16[4,2,64,4,256]{4,3,2,1,0:T(4,128)(2,1)S(1)} reshape(bf16[1,1,8,64,1024]{4,3,2,1,0:T(8,128)(2,1)} %param.10) | data formatting | bytes 2097152 | tf_op jit(solution)/shard_map/squeeze | solution.py:260
  8.2 1.1 pad_maximum_fusion.1
  9.2 5.0 %all-to-all-start.2 = ((bf16[4,2,256,256]{3,2,1,0:T(8,128)(2,1)}), bf16[4,2,256,256]{3,2,1,0:T(8,128)(2,1)S(1)}, u32[]{:S(2)}, u32[]{:S(2)}) async-start(bf16[4,2,256,256]{3,2,1,0:T(8,128)(2,1)} %pad_maximum_fusion.1), calls=%async_computation.2 | async-start | bytes 2097152 | tf_op jit(solution)/shard_map/all_to_all | solution.py:245
  15.2 5.4 %collective-permute-start = (bf16[4,1,256,256]{3,2,1,0:T(8,128)(2,1)}, bf16[4,1,256,256]{3,2,1,0:T(8,128)(2,1)}, u32[]{:S(2)}, u32[]{:S(2)}) collective-permute-start(bf16[4,1,256,256]{3,2,1,0:T(8,128)(2,1)} %bitcast.8), channel_id=1, source_target_pairs={{1,0},{2,1},{3,2},{4,3},{5,4},{6,5},{7,6},{8,7},{9,8},{10,9},{11,1... | collective-permute-start | bytes 1572872 | tf_op jit(solution)/shard_map/ppermute | solution.py:241
  20.6 1.1 pad_maximum_fusion
  21.7 6.7 %all-to-all-done.2.pt_ref = bf16[4,2,256,256]{3,2,1,0:T(8,128)(2,1)S(1)} async-done(((bf16[4,2,256,256]{3,2,1,0:T(8,128)(2,1)}), bf16[4,2,256,256]{3,2,1,0:T(8,128)(2,1)S(1)}, u32[]{:S(2)}, u32[]{:S(2)}) %all-to-all-start.2) | async-done | bytes 1048608 | tf_op jit(solution)/shard_map/all_to_all | solution.py:245
  28.4 3.5 %all-to-all-start = ((bf16[4,2,256,256]{3,2,1,0:T(8,128)(2,1)}), bf16[4,2,256,256]{3,2,1,0:T(8,128)(2,1)S(1)}, u32[]{:S(2)}, u32[]{:S(2)}) async-start(bf16[4,2,256,256]{3,2,1,0:T(8,128)(2,1)} %pad_maximum_fusion), calls=%async_computation | async-start | bytes 2097152 | tf_op jit(solution)/shard_map/all_to_all | solution.py:245
  32.0 1.0 dynamic-slice_bitcast_fusion.1
  33.0 12.1 %all-to-all-done.pt_ref = bf16[4,2,256,256]{3,2,1,0:T(8,128)(2,1)S(1)} async-done(((bf16[4,2,256,256]{3,2,1,0:T(8,128)(2,1)}), bf16[4,2,256,256]{3,2,1,0:T(8,128)(2,1)S(1)}, u32[]{:S(2)}, u32[]{:S(2)}) %all-to-all-start) | async-done | bytes 1048608 | tf_op jit(solution)/shard_map/all_to_all | solution.py:245
  45.2 4.1 %all-to-all-start.3 = ((bf16[4,1,256,256]{3,2,1,0:T(8,128)(2,1)}), bf16[4,1,256,256]{3,2,1,0:T(8,128)(2,1)}, u32[]{:S(2)}, u32[]{:S(2)}) async-start(bf16[4,1,256,256]{3,2,1,0:T(8,128)(2,1)} %collective-permute-done.1), calls=%async_computation.3 | async-start | bytes 1048576 | tf_op jit(solution)/shard_map/all_to_all | solution.py:245
  49.3 1.4 fusion.1.perm_ref
  50.8 5.5 %all-to-all-done.3.q_ref = bf16[4,1,256,256]{3,2,1,0:T(8,128)(2,1)} async-done(((bf16[4,1,256,256]{3,2,1,0:T(8,128)(2,1)}), bf16[4,1,256,256]{3,2,1,0:T(8,128)(2,1)}, u32[]{:S(2)}, u32[]{:S(2)}) %all-to-all-start.3) | async-done | bytes 524320 | tf_op jit(solution)/shard_map/all_to_all | solution.py:245
  56.3 4.3 %all-to-all-start.1 = ((bf16[4,1,256,256]{3,2,1,0:T(8,128)(2,1)}), bf16[4,1,256,256]{3,2,1,0:T(8,128)(2,1)}, u32[]{:S(2)}, u32[]{:S(2)}) async-start(bf16[4,1,256,256]{3,2,1,0:T(8,128)(2,1)} %collective-permute-done), calls=%async_computation.1 | async-start | bytes 1048576 | tf_op jit(solution)/shard_map/all_to_all | solution.py:245
  60.7 17.6 %chain_second.1 = (bf16[4,64,1024]{2,1,0:T(8,128)(2,1)}, f32[8,128]{1,0:T(8,128)S(1)}) custom-call(bf16[4,2,256,256]{3,2,1,0:T(8,128)(2,1)S(1)} %all-to-all-done.2.pt_ref, bf16[4,1,256,256]{3,2,1,0:T(8,128)(2,1)} %all-to-all-done.3.q_ref, bf16[64,1024]{1,0:T(8,128)(2,1)S(1)} %get-tuple-element.27.m_ref, bf16[1024,1024]{1,0:T(8,128)(2,1)S(1)} %fusion.1.perm_ref), custom_call_target="tpu_custom_call" | custom-call | flops 8000000000 | bytes 4194304 | tf_op jit(solution)/shard_map/chain_second/pallas_call | solution.py:104
  78.3 1.2 copy-done.1
  79.6 16.8 %chain_first.1 = (bf16[4,64,1024]{2,1,0:T(8,128)(2,1)S(1)}, f32[8,128]{1,0:T(8,128)S(1)}) custom-call(bf16[4,2,256,256]{3,2,1,0:T(8,128)(2,1)S(1)} %copy-done.1, bf16[4,1,256,256]{3,2,1,0:T(8,128)(2,1)} %all-to-all-done.1.q_ref, bf16[64,1024]{1,0:T(8,128)(2,1)S(1)} %get-tuple-element.26.m_ref, bf16[1024,1024]{1,0:T(8,128)(2,1)S(1)} %fusion.1.perm_ref), custom_call_target="tpu_custom_call" | custom-call | flops 8000000000 | bytes 4194304 | tf_op jit(solution)/shard_map/chain_first/pallas_call | solution.py:104
  96.5 8.1 %all_to_all.40 = f32[4,2,8]{2,1,0:T(2,128)S(1)} all-to-all(f32[4,2,8]{2,1,0:T(2,128)S(1)} %broadcast_in_dim.38), channel_id=1, replica_groups=mesh['row'=4,'col'=32] {'row'}, dimensions={0} | all-to-all | bytes 512 | tf_op jit(solution)/shard_map/all_to_all | solution.py:245
  104.6 9.3 %all_to_all.41.u1_ref.refs_3_ = bf16[4,64,1024]{2,1,0:T(8,128)(2,1)S(1)} all-to-all(bf16[4,64,1024]{2,1,0:T(8,128)(2,1)S(1)} %get-tuple-element.12), channel_id=1, replica_groups=mesh['row'=4,'col'=32] {'row'}, dimensions={0} | all-to-all | bytes 1048576 | tf_op jit(solution)/shard_map/all_to_all | solution.py:245
  113.9 3.5 %all-to-all-start.7 = ((bf16[4,64,1024]{2,1,0:T(8,128)(2,1)}), bf16[4,64,1024]{2,1,0:T(8,128)(2,1)S(1)}, u32[]{:S(2)}, u32[]{:S(2)}) async-start(bf16[4,64,1024]{2,1,0:T(8,128)(2,1)} %get-tuple-element.13), calls=%async_computation.7 | async-start | bytes 1048576 | tf_op jit(solution)/shard_map/all_to_all | solution.py:245
  117.4 6.9 %collective-permute-start.2 = (bf16[8,64,64]{2,1,0:T(8,128)(2,1)S(1)}, bf16[8,64,64]{2,1,0:T(8,128)(2,1)S(1)}, u32[]{:S(2)}, u32[]{:S(2)}) collective-permute-start(bf16[8,64,64]{2,1,0:T(8,128)(2,1)S(1)} %bitcast.43), channel_id=1, source_target_pairs={{1,0},{2,1},{3,2},{4,3},{5,4},{6,5},{7,6},{8,7},{9,8},{10,9},{11,1... | collective-permute-start | bytes 196616 | tf_op jit(solution)/shard_map/ppermute | solution.py:241
  125.3 15.5 %all-to-all-start.5 = ((f32[32,1,64]{2,1,0:T(1,128)}), f32[32,1,64]{2,1,0:T(1,128)S(1)}, u32[]{:S(2)}, u32[]{:S(2)}) async-start(f32[32,1,64]{2,1,0:T(1,128)} %broadcast_in_dim.40), calls=%async_computation.5 | async-start | bytes 32768 | tf_op jit(solution)/shard_map/all_to_all | solution.py:285
  140.8 7.4 %observable_weights.1.w_ref = bf16[2,8,64,1024]{3,2,1,0:T(8,128)(2,1)S(1)} custom-call(bf16[8,64,1024]{2,1,0:T(8,128)(2,1)S(1)} %bitcast.42, bf16[8,64,64]{2,1,0:T(8,128)(2,1)S(1)} %bitcast.44, bf16[8,64,64]{2,1,0:T(8,128)(2,1)S(1)} %collective-permute-done.2.er_ref, bf16[2,8,16,16]{3,2,1,0:T(8,128)(2,1)S(1)} %copy-done.4), custom_call_target="tpu_custom_call" | custom-call | flops 4000000000 | bytes 4194304 | tf_op jit(solution)/shard_map/observable_weights/pallas_call | solution.py:162
  148.8 2.0 %finish.1 = (bf16[8,64,1024]{2,1,0:T(8,128)(2,1)}, f32[1,8]{1,0:T(1,128)}, f32[2,8]{1,0:T(2,128)}) custom-call(s32[2]{0:T(128)S(1)} %pad_add_fusion.refs_0_, f32[32,64]{1,0:T(8,128)S(1)} %bitcast.41, f32[2,8]{1,0:T(2,128)S(1)} %observe.1.refs_2_, bf16[4,64,1024]{2,1,0:T(8,128)(2,1)S(1)} %all_to_all.41.u1_ref.refs_3_, ...), custom_call_target="tpu_custom_call" | custom-call | flops 2000000 | bytes 2097152 | tf_op jit(solution)/shard_map/finish/pallas_call | solution.py:223
  (46 shorter events, 6.4 us)
Async XLA Ops:
  0.6 2.2 %copy-start.6 = (bf16[1,1,8,64,1024]{4,3,2,1,0:T(8,128)(2,1)S(1)}, bf16[1,1,8,64,1024]{4,3,2,1,0:T(8,128)(2,1)}, u32[]{:S(2)}) copy-start(bf16[1,1,8,64,1024]{4,3,2,1,0:T(8,128)(2,1)} %param.11) | copy-start | bytes 3145732
  0.6 3.5 %copy-start.7 = (s32[1,8]{1,0:T(1,128)S(1)}, s32[1,8]{1,0:T(1,128)}, u32[]{:S(2)}) copy-start(s32[1,8]{1,0:T(1,128)} %param.15) | copy-start | bytes 100
  8.2 12.4 %copy-start.5 = (bf16[4,1,256,256]{3,2,1,0:T(8,128)(2,1)S(1)}, bf16[4,1,256,256]{3,2,1,0:T(8,128)(2,1)}, u32[]{:S(2)}) copy-start(bf16[4,1,256,256]{3,2,1,0:T(8,128)(2,1)} %get-tuple-element.32) | copy-start | bytes 1572868
  9.2 19.2 %all-to-all-start.2 = ((bf16[4,2,256,256]{3,2,1,0:T(8,128)(2,1)}), bf16[4,2,256,256]{3,2,1,0:T(8,128)(2,1)S(1)}, u32[]{:S(2)}, u32[]{:S(2)}) async-start(bf16[4,2,256,256]{3,2,1,0:T(8,128)(2,1)} %pad_maximum_fusion.1), calls=%async_computation.2 | async-start | bytes 2097152 | tf_op jit(solution)/shard_map/all_to_all | solution.py:245
  14.2 18.8 %collective-permute-start.1 = (bf16[4,1,256,256]{3,2,1,0:T(8,128)(2,1)S(1)}, bf16[4,1,256,256]{3,2,1,0:T(8,128)(2,1)}, u32[]{:S(2)}, u32[]{:S(2)}) collective-permute-start(bf16[4,1,256,256]{3,2,1,0:T(8,128)(2,1)S(1)} %bitcast.48), channel_id=1, source_target_pairs={{1,0},{2,1},{3,2},{4,3},{5,4},{6,5},{7,6},{8,7},{9,8},{10,9},{11,1... | collective-permute-start | bytes 1572872 | tf_op jit(solution)/shard_map/ppermute | solution.py:241
  15.2 35.6 %collective-permute-start = (bf16[4,1,256,256]{3,2,1,0:T(8,128)(2,1)}, bf16[4,1,256,256]{3,2,1,0:T(8,128)(2,1)}, u32[]{:S(2)}, u32[]{:S(2)}) collective-permute-start(bf16[4,1,256,256]{3,2,1,0:T(8,128)(2,1)} %bitcast.8), channel_id=1, source_target_pairs={{1,0},{2,1},{3,2},{4,3},{5,4},{6,5},{7,6},{8,7},{9,8},{10,9},{11,1... | collective-permute-start | bytes 1572872 | tf_op jit(solution)/shard_map/ppermute | solution.py:241
  28.4 16.8 %all-to-all-start = ((bf16[4,2,256,256]{3,2,1,0:T(8,128)(2,1)}), bf16[4,2,256,256]{3,2,1,0:T(8,128)(2,1)S(1)}, u32[]{:S(2)}, u32[]{:S(2)}) async-start(bf16[4,2,256,256]{3,2,1,0:T(8,128)(2,1)} %pad_maximum_fusion), calls=%async_computation | async-start | bytes 2097152 | tf_op jit(solution)/shard_map/all_to_all | solution.py:245
  45.2 4.1 %copy-start = (bf16[4,2,256,256]{3,2,1,0:T(8,128)(2,1)}, bf16[4,2,256,256]{3,2,1,0:T(8,128)(2,1)S(1)}, u32[]{:S(2)}) copy-start(bf16[4,2,256,256]{3,2,1,0:T(8,128)(2,1)S(1)} %all-to-all-done.pt_ref) | copy-start | bytes 3145732
  45.2 11.1 %all-to-all-start.3 = ((bf16[4,1,256,256]{3,2,1,0:T(8,128)(2,1)}), bf16[4,1,256,256]{3,2,1,0:T(8,128)(2,1)}, u32[]{:S(2)}, u32[]{:S(2)}) async-start(bf16[4,1,256,256]{3,2,1,0:T(8,128)(2,1)} %collective-permute-done.1), calls=%async_computation.3 | async-start | bytes 1048576 | tf_op jit(solution)/shard_map/all_to_all | solution.py:245
  56.3 22.0 %all-to-all-start.1 = ((bf16[4,1,256,256]{3,2,1,0:T(8,128)(2,1)}), bf16[4,1,256,256]{3,2,1,0:T(8,128)(2,1)}, u32[]{:S(2)}, u32[]{:S(2)}) async-start(bf16[4,1,256,256]{3,2,1,0:T(8,128)(2,1)} %collective-permute-done), calls=%async_computation.1 | async-start | bytes 1048576 | tf_op jit(solution)/shard_map/all_to_all | solution.py:245
  78.3 1.2 copy-start.1
  96.4 21.1 %copy-start.3 = (bf16[1,1,8,64,64]{4,3,2,1,0:T(8,128)(2,1)S(1)}, bf16[1,1,8,64,64]{4,3,2,1,0:T(8,128)(2,1)}, u32[]{:S(2)}) copy-start(bf16[1,1,8,64,64]{4,3,2,1,0:T(8,128)(2,1)} %param.13) | copy-start | bytes 196612
  96.4 44.4 %copy-start.2 = (bf16[1,1,8,64,1024]{4,3,2,1,0:T(8,128)(2,1)S(1)}, bf16[1,1,8,64,1024]{4,3,2,1,0:T(8,128)(2,1)}, u32[]{:S(2)}) copy-start(bf16[1,1,8,64,1024]{4,3,2,1,0:T(8,128)(2,1)} %param.12) | copy-start | bytes 3145732
  96.4 44.4 %copy-start.4 = (bf16[2,8,16,16]{3,2,1,0:T(8,128)(2,1)S(1)}, bf16[2,8,16,16]{3,2,1,0:T(8,128)(2,1)}, u32[]{:S(2)}) copy-start(bf16[2,8,16,16]{3,2,1,0:T(8,128)(2,1)} %op_ref.1) | copy-start | bytes 24580
  113.9 10.7 %all-to-all-start.7 = ((bf16[4,64,1024]{2,1,0:T(8,128)(2,1)}), bf16[4,64,1024]{2,1,0:T(8,128)(2,1)S(1)}, u32[]{:S(2)}, u32[]{:S(2)}) async-start(bf16[4,64,1024]{2,1,0:T(8,128)(2,1)} %get-tuple-element.13), calls=%async_computation.7 | async-start | bytes 1048576 | tf_op jit(solution)/shard_map/all_to_all | solution.py:245
  117.4 23.4 %collective-permute-start.2 = (bf16[8,64,64]{2,1,0:T(8,128)(2,1)S(1)}, bf16[8,64,64]{2,1,0:T(8,128)(2,1)S(1)}, u32[]{:S(2)}, u32[]{:S(2)}) collective-permute-start(bf16[8,64,64]{2,1,0:T(8,128)(2,1)S(1)} %bitcast.43), channel_id=1, source_target_pairs={{1,0},{2,1},{3,2},{4,3},{5,4},{6,5},{7,6},{8,7},{9,8},{10,9},{11,1... | collective-permute-start | bytes 196616 | tf_op jit(solution)/shard_map/ppermute | solution.py:241
  125.3 23.6 %all-to-all-start.5 = ((f32[32,1,64]{2,1,0:T(1,128)}), f32[32,1,64]{2,1,0:T(1,128)S(1)}, u32[]{:S(2)}, u32[]{:S(2)}) async-start(f32[32,1,64]{2,1,0:T(1,128)} %broadcast_in_dim.40), calls=%async_computation.5 | async-start | bytes 32768 | tf_op jit(solution)/shard_map/all_to_all | solution.py:285

commit v2 on v1

v2 whole, which is shorter than its diff:
```python
import math

import jax
import jax.numpy as jnp
from jax import lax
from jax.experimental import pallas as pl
from jax.experimental.pallas import tpu as pltpu
from jax.sharding import PartitionSpec as P

SEC = 8
PAD = 64
KM = 16
DB = 16
ROWS = 4
WIDE = 256
GROUPS = WIDE // PAD
SITE = KM * PAD
LANES = 128

BF16 = jnp.bfloat16
F32 = jnp.float32

epsilon = 1e-06


def mm(a, b):
    return jnp.dot(a, b, preferred_element_type=F32)


def mmt(a, b):
    return lax.dot_general(a, b, (((1,), (1,)), ((), ())), preferred_element_type=F32)


def iota2(shape, dim):
    return lax.broadcasted_iota(jnp.int32, shape, dim)


def digit_swap():
    i, j = iota2((WIDE, WIDE), 0), iota2((WIDE, WIDE), 1)
    return jnp.where((i // 16 == j % 16) & (i % 16 == j // 16), 1.0, 0.0).astype(BF16)


def bond_swap():
    i, j = iota2((SITE, SITE), 0), iota2((SITE, SITE), 1)
    return jnp.where(j == (i % DB) * PAD + i // DB, 1.0, 0.0).astype(BF16)


def total(x):
    return jnp.sum(jnp.sum(x, axis=1, keepdims=True), axis=0, keepdims=True)


def vmem(count):
    return [pl.BlockSpec(memory_space=pltpu.VMEM)] * count


def smem():
    return pl.BlockSpec(memory_space=pltpu.SMEM)


def masked(block, inside):
    return jnp.where(inside, block.astype(F32), 0.0).astype(BF16)


def pack_first_kernel(me_ref, rank_ref, p_ref, t_ref, q_ref, *refs):
    outs, rights, (held, sems) = refs[:ROWS], refs[ROWS : ROWS + 2], refs[ROWS + 2 :]
    me = me_ref[0]
    at = iota2((PAD, WIDE), 0)
    copies = []
    for x in range(ROWS):
        s = 2 * (me ^ x)
        copies.append(
            (
                pltpu.make_async_copy(p_ref.at[s], held.at[x], sems.at[0, x]),
                pltpu.make_async_copy(t_ref.at[s], outs[x].at[1], sems.at[1, x]),
                pltpu.make_async_copy(q_ref.at[s], rights[0].at[x], sems.at[2, x]),
                pltpu.make_async_copy(q_ref.at[s + 1], rights[1].at[x], sems.at[3, x]),
            )
        )
    for group in copies:
        for copy in group:
            copy.start()
    for x in range(ROWS):
        inside = at < rank_ref[0, 2 * (me ^ x)]
        copies[x][0].wait()
        for g in range(GROUPS):
            outs[x][0, g * PAD : (g + 1) * PAD, :] = masked(
                held[x, :, g * WIDE : (g + 1) * WIDE], inside
            )
    for group in copies:
        for copy in group[1:]:
            copy.wait()


def pack_first(me, ranks, p, t, q):
    piece = jax.ShapeDtypeStruct((2, WIDE, WIDE), BF16)
    right = jax.ShapeDtypeStruct((ROWS, PAD, SITE), BF16)
    return pl.pallas_call(
        pack_first_kernel,
        out_shape=(piece,) * ROWS + (right,) * 2,
        in_specs=[smem(), smem()] + [pl.BlockSpec(memory_space=pl.ANY)] * 3,
        out_specs=tuple(vmem(ROWS + 2)),
        scratch_shapes=[pltpu.VMEM((ROWS, PAD, SITE), BF16), pltpu.SemaphoreType.DMA((4, ROWS))],
        compiler_params=pltpu.CompilerParams(vmem_limit_bytes=56 << 20),
        cost_estimate=pl.CostEstimate(flops=1_000_000, bytes_accessed=2 << 20, transcendentals=0),
        name="pack_first",
    )(me, ranks, p, t, q)


def pack_second_kernel(me_ref, rank_ref, p_ref, t_ref, q1_ref, q2_ref, ready_ref, *refs):
    firsts, seconds = refs[:ROWS], refs[ROWS : 2 * ROWS]
    held, sems = refs[2 * ROWS :]
    me = me_ref[0]
    at = iota2((PAD, WIDE), 0)
    copies = []
    for x in range(ROWS):
        s = 2 * (me ^ x) + 1
        copies.append(
            (
                pltpu.make_async_copy(p_ref.at[s], held.at[x], sems.at[0, x]),
                pltpu.make_async_copy(t_ref.at[s], seconds[x].at[1], sems.at[1, x]),
            )
        )
    for pair in copies:
        for copy in pair:
            copy.start()
    for x in range(ROWS):
        s = 2 * (me ^ x)
        inside = [at < rank_ref[0, s + k] for k in range(2)]
        copies[x][0].wait()
        for g in range(GROUPS):
            rows, lanes = slice(g * PAD, (g + 1) * PAD), slice(g * WIDE, (g + 1) * WIDE)
            seconds[x][0, rows, :] = masked(held[x, :, lanes], inside[1])
            firsts[x][rows, :] = masked(q1_ref[x, :, lanes], inside[0])
            seconds[x][2, rows, :] = masked(q2_ref[x, :, lanes], inside[1])
    for x in range(ROWS):
        copies[x][1].wait()


def pack_second(me, ranks, p, t, q1, q2, ready):
    one = jax.ShapeDtypeStruct((WIDE, WIDE), BF16)
    three = jax.ShapeDtypeStruct((3, WIDE, WIDE), BF16)
    return pl.pallas_call(
        pack_second_kernel,
        out_shape=(one,) * ROWS + (three,) * ROWS,
        in_specs=[smem(), smem()] + [pl.BlockSpec(memory_space=pl.ANY)] * 2 + vmem(3),
        out_specs=tuple(vmem(2 * ROWS)),
        scratch_shapes=[pltpu.VMEM((ROWS, PAD, SITE), BF16), pltpu.SemaphoreType.DMA((2, ROWS))],
        compiler_params=pltpu.CompilerParams(vmem_limit_bytes=8 << 20),
        cost_estimate=pl.CostEstimate(flops=1_000_000, bytes_accessed=4 << 20, transcendentals=0),
        name="pack_second",
    )(me, ranks, p, t, q1, q2, ready)


def chain_kernel(
    me_ref, pts, qs, m_ref, perm_ref, before_ref, befores, us, st_ref,
    bdm, bdq, xs, ys, qw, pw, lefts, middles, stack, site, sem,
):
    me = me_ref[0]
    start = pltpu.make_async_copy(m_ref.at[2 * me + len(befores) // ROWS], site, sem)
    start.start()
    swap = digit_swap()
    bdm[...] = jnp.zeros_like(bdm)
    bdq[...] = jnp.zeros_like(bdq)
    for pieces, dst in (([ref.at[0] for ref in pts], pw), (qs, qw)):
        acc = None
        for part in range(GROUPS):
            rows = jnp.concatenate([ref[part * PAD : (part + 1) * PAD, :] for ref in pieces], axis=0)
            term = mm(rows, perm_ref[part * WIDE : (part + 1) * WIDE, :])
            acc = term if acc is None else acc + term
        dst[...] = acc.astype(BF16)
    for x in range(ROWS):
        for w in range(DB):
            for g in range(GROUPS):
                stack[w * 16 : (w + 1) * 16, g * PAD : (g + 1) * PAD] = pw[
                    x * PAD + g * 16 : x * PAD + (g + 1) * 16, w * PAD : (w + 1) * PAD
                ]
        lefts[me ^ x] = mm(swap, stack[...]).astype(BF16)
        middles[me ^ x] = mm(mmt(swap, pts[x][1]).astype(BF16), swap).astype(BF16)
    start.wait()
    for x in range(len(befores)):
        us[x][0] = befores[x][0]

    def row(r, carry):
        base = pl.multiple_of((me ^ r) * PAD, PAD)
        for k in range(KM):
            lanes = slice(k * PAD, (k + 1) * PAD)
            block = site[:, lanes]
            right = qw[pl.ds(base, PAD), lanes]
            for g in range(GROUPS):
                at = slice(g * PAD, (g + 1) * PAD)
                bdm[k, at, at] = block
                bdq[at, k * WIDE + g * PAD : k * WIDE + (g + 1) * PAD] = right
        left = lefts[r]
        middle = middles[r]
        for k in range(KM):
            first = mm(left, bdm[k]).astype(BF16)
            xs[:, k * 16 : (k + 1) * 16, :] = first.reshape(16, 16, WIDE)
        for c in range(16):
            second = mm(middle, xs[c]).astype(BF16)
            for e in range(DB):
                ys[c * 16 : (c + 1) * 16, e * WIDE : (e + 1) * WIDE] = second[e * 16 : (e + 1) * 16]
        z = mmt(ys[...], bdq[...])
        top = jnp.max(jnp.max(jnp.abs(z), axis=1, keepdims=True), axis=0, keepdims=True)
        top = jnp.where(top > 0, top, 1.0)
        u = z / top
        placed = mm(swap, u.astype(BF16)).astype(BF16)
        for l in range(KM):
            for g in range(GROUPS):
                site[g * 16 : (g + 1) * 16, l * PAD : (l + 1) * PAD] = placed[
                    l * 16 : (l + 1) * 16, g * PAD : (g + 1) * PAD
                ]
        for x in range(ROWS):

            @pl.when(r == me ^ x)
            def _(x=x):
                us[x][len(befores) // ROWS] = site[...]

        lane = iota2((1, LANES), 1)
        carry = jnp.where(lane == 2 * r, top, carry)
        return jnp.where(lane == 2 * r + 1, total(u * u), carry)

    stats = lax.fori_loop(0, ROWS, row, jnp.zeros((1, LANES), F32))
    if befores:
        lane = iota2((1, LANES), 1)
        stats = jnp.where(lane < 2 * ROWS, before_ref[0:1, :], pltpu.roll(stats, 2 * ROWS, 1))
    st_ref[...] = jnp.broadcast_to(stats, st_ref.shape)


def chain(me, pts, qs, m, perm, before, befores, copies, name):
    inputs = [me, *pts, *(qs or ()), perm, *([before] if befores else []), *befores, m]
    sites = 2 if befores else 1

    def body(*refs):
        me_ref, *refs = refs
        pt_refs, refs = refs[:ROWS], refs[ROWS:]
        if qs is None:
            q_refs = [ref.at[2] for ref in pt_refs]
        else:
            q_refs, refs = refs[:ROWS], refs[ROWS:]
        perm_ref, *refs = refs
        before_ref = None
        if befores:
            before_ref, *refs = refs
        before_sites, refs = refs[: len(befores)], refs[len(befores) :]
        m_ref, *refs = refs
        us, (st_ref, *scratch) = refs[:ROWS], refs[ROWS:]
        chain_kernel(
            me_ref, pt_refs, q_refs, m_ref, perm_ref, before_ref, before_sites, us, st_ref, *scratch
        )

    site = jax.ShapeDtypeStruct((sites, PAD, SITE), BF16)
    return pl.pallas_call(
        body,
        out_shape=(site,) * ROWS + (jax.ShapeDtypeStruct((copies, LANES), F32),),
        in_specs=[smem()] + vmem(len(inputs) - 2) + [pl.BlockSpec(memory_space=pl.ANY)],
        out_specs=tuple(vmem(ROWS + 1)),
        scratch_shapes=[
            pltpu.VMEM((KM, WIDE, WIDE), BF16),
            pltpu.VMEM((WIDE, DB * WIDE), BF16),
            pltpu.VMEM((16, WIDE, WIDE), BF16),
            pltpu.VMEM((WIDE, DB * WIDE), BF16),
            pltpu.VMEM((ROWS * PAD, SITE), BF16),
            pltpu.VMEM((ROWS * PAD, SITE), BF16),
            pltpu.VMEM((ROWS, WIDE, WIDE), BF16),
            pltpu.VMEM((ROWS, WIDE, WIDE), BF16),
            pltpu.VMEM((WIDE, WIDE), BF16),
            pltpu.VMEM((PAD, SITE), BF16),
            pltpu.SemaphoreType.DMA,
        ],
        compiler_params=pltpu.CompilerParams(vmem_limit_bytes=24 << 20),
        cost_estimate=pl.CostEstimate(
            flops=12_000_000_000, bytes_accessed=4 << 20, transcendentals=0
        ),
        name=name,
    )(*inputs)


def weight_kernel(el_ref, er_ref, op_ref, lower_ref, w_ref, done_ref, perm_ref, bde, stack, b_ref, sem):
    copy = pltpu.make_async_copy(lower_ref, b_ref, sem)
    copy.start()
    done_ref[...] = jnp.zeros_like(done_ref)
    bde[...] = jnp.zeros_like(bde)
    spread = jnp.where(iota2((WIDE, KM), 0) // 16 == iota2((WIDE, KM), 1), 1.0, 0.0).astype(BF16)
    same = iota2((WIDE, WIDE), 0) % 16 == iota2((WIDE, WIDE), 1) % 16
    perm_ref[...] = bond_swap()
    copy.wait()

    def sector(s, carry):
        upper = mm(el_ref[s], b_ref[s]).astype(BF16)
        for g in range(GROUPS):
            at = slice(g * PAD, (g + 1) * PAD)
            bde[at, at] = er_ref[s]
        for g in range(4):
            both = mmt(upper[:, g * WIDE : (g + 1) * WIDE], bde[...]).astype(BF16)
            for i in range(4):
                l = g * 4 + i
                for h in range(GROUPS):
                    stack[l * 16 : (l + 1) * 16, h * PAD : (h + 1) * PAD] = both[
                        h * 16 : (h + 1) * 16, i * PAD : (i + 1) * PAD
                    ]
        for q in range(2):
            grown = mmt(mm(spread, op_ref[q, s]).astype(BF16), spread)
            grown = jnp.where(same, grown, 0.0).astype(BF16)
            out = mm(grown, stack[...]).astype(BF16)
            for k in range(KM):
                for h in range(GROUPS):
                    w_ref[q, s, h * 16 : (h + 1) * 16, k * PAD : (k + 1) * PAD] = out[
                        k * 16 : (k + 1) * 16, h * PAD : (h + 1) * PAD
                    ]
        return carry

    lax.fori_loop(0, SEC, sector, 0)


def observable_weights(lower, left_env, right_env, operators):
    return pl.pallas_call(
        weight_kernel,
        out_shape=(
            jax.ShapeDtypeStruct((2, SEC, PAD, SITE), BF16),
            jax.ShapeDtypeStruct((8, LANES), F32),
            jax.ShapeDtypeStruct((SITE, SITE), BF16),
        ),
        in_specs=vmem(3) + [pl.BlockSpec(memory_space=pl.ANY)],
        out_specs=tuple(vmem(3)),
        scratch_shapes=[
            pltpu.VMEM((WIDE, WIDE), BF16),
            pltpu.VMEM((WIDE, WIDE), BF16),
            pltpu.VMEM((SEC, PAD, SITE), BF16),
            pltpu.SemaphoreType.DMA,
        ],
        compiler_params=pltpu.CompilerParams(vmem_limit_bytes=16 << 20),
        cost_estimate=pl.CostEstimate(
            flops=6_000_000_000, bytes_accessed=4 << 20, transcendentals=0
        ),
        name="observable_weights",
    )(left_env, right_env, operators, lower)


def finish_kernel(entries, me_ref, g_ref, w_ref, *refs):
    us, (out_ref, log_ref, obs_ref) = refs[:ROWS], refs[ROWS:]
    row, col = me_ref[0], me_ref[1]
    columns = g_ref.shape[0] // ROWS
    at_s = iota2((1, SEC), 1)
    at_qs, at_q = iota2((2, SEC), 1), iota2((2, SEC), 0)
    logs = jnp.zeros((1, SEC), F32)
    factors = []
    for i in range(ROWS):
        for k in range(2):
            scale = jnp.ones((columns, 1), F32)
            factor = jnp.zeros((columns, 1), F32)
            log = jnp.zeros((1, 1), F32)
            here = pl.ds(i * columns, columns)
            for r in range(ROWS):
                lane = 2 * ROWS * k + 2 * r
                size = scale * g_ref[here, lane : lane + 1]
                squares = size * size * g_ref[here, lane + 1 : lane + 2]
                norm = jnp.sqrt(jnp.sum(squares, axis=0, keepdims=True) / entries + epsilon)
                scale = size / norm
                factor = jnp.where(row == r, scale, factor)
                log = jnp.where(row == r, jnp.log(norm), log)
            at_col = iota2((columns, 1), 0) == col
            factors.append(jnp.sum(jnp.where(at_col, factor, 0.0), axis=0, keepdims=True))
            logs = jnp.where(at_s == 2 * i + k, log, logs)
    log_ref[...] = logs
    values = jnp.zeros((2, SEC), F32)
    for k in range(2):
        for x in range(ROWS):
            i = row ^ x
            s = 2 * i + k
            factor = factors[k]
            for other in range(1, ROWS):
                factor = jnp.where(i == other, factors[2 * other + k], factor)
            u = us[x][k].astype(F32) * factor
            out_ref[s] = u.astype(BF16)
            for q in range(2):
                value = total(u * w_ref[q, s].astype(F32))
                values = jnp.where((at_q == q) & (at_qs == s), value, values)
    obs_ref[...] = values / math.sqrt(KM)


def finish(entries, me, gathered, weights, us):
    return pl.pallas_call(
        lambda *refs: finish_kernel(entries, *refs),
        out_shape=(
            jax.ShapeDtypeStruct((SEC, PAD, SITE), BF16),
            jax.ShapeDtypeStruct((1, SEC), F32),
            jax.ShapeDtypeStruct((2, SEC), F32),
        ),
        in_specs=[smem()] + vmem(2 + len(us)),
        out_specs=tuple(vmem(3)),
        compiler_params=pltpu.CompilerParams(vmem_limit_bytes=16 << 20),
        cost_estimate=pl.CostEstimate(flops=2_000_000, bytes_accessed=2 << 20, transcendentals=0),
        name="finish",
    )(me, gathered, weights, *us)


def passed_along(block, axis, distance):
    devices = range(lax.axis_size(axis))
    route = [((i - distance) % len(devices), i) for i in devices]
    return lax.ppermute(block, axis, route)


def exchanged(block, x):
    return lax.ppermute(block, "row", [(i, i ^ x) for i in range(ROWS)])


NEAR_FIRST = (1, 3, 2)


def exchanged_all(blocks):
    got = {x: exchanged(blocks[x], x) for x in NEAR_FIRST}
    return [blocks[0]] + [got[x] for x in range(1, ROWS)]


def on_device(
    top_boundary, row_transfer, proj_in, proj_out, bottom_boundary, environments, operators, ranks
):
    row, col = lax.axis_index("row"), lax.axis_index("col")
    columns = lax.axis_size("col")
    me = jnp.stack([row, col]).astype(jnp.int32)
    envs = environments[0, 0]
    lefts, transfers = proj_in[0, 0], row_transfer[0, 0]
    *pts1, q1, q2 = pack_first(me, ranks, lefts, transfers, proj_out[0, 0])
    q1 = passed_along(q1, "col", -1)
    q2 = passed_along(q2, "col", -1)
    next_envs = passed_along(envs, "col", -1)
    pts1 = exchanged_all(pts1)
    weights, ready, perm = observable_weights(bottom_boundary[0, 0], envs, next_envs, operators)
    packed = pack_second(me, ranks, lefts, transfers, q1, q2, ready)
    qs1 = exchanged_all(packed[:ROWS])
    ptqs2 = exchanged_all(packed[ROWS:])
    top = top_boundary[0]
    *us1, stats = chain(me, pts1, qs1, top, perm, None, (), 8, "chain_first")
    everyone = ROWS * columns
    *us, stats = chain(me, ptqs2, None, top, perm, stats, us1, everyone, "chain_second")
    us = exchanged_all(us)
    gathered = lax.all_to_all(stats, ("row", "col"), 0, 0, tiled=True)
    entries = float(columns * PAD * KM * PAD)
    sites, logs, values = finish(entries, me, gathered, weights, us)
    return sites[None, None], logs, values[:, None, None]


def solution(mesh):
    in_specs = (
        P("col", None, None, None),
        P("row", "col", None, None, None),
        P("row", "col", None, None, None),
        P("row", "col", None, None, None),
        P("row", "col", None, None, None),
        P("row", "col", None, None, None),
        P(),
        P("row", None),
    )
    out_specs = (P("row", "col", None, None, None), P("row", None), P(None, "row", "col", None))
    return jax.shard_map(
        on_device, mesh=mesh, in_specs=in_specs, out_specs=out_specs, check_vma=False
    )
```

time: 152 us -> 100 us (0.66)
  starting transfers between devices: 49.2 us -> 23.7 us
  waiting for transfers between devices: 24.4 us -> 2.11 us
  local copies, waits for them, and re-layouts: 9.8 us -> 0.05 us
  Pallas kernels: 44.3 us -> 51.6 us
  other arithmetic: 4.75 us -> 0.66 us
  blocking collectives: 17.4 us -> 21.1 us
    all_to_all x6 -> x0, starting transfers between devices: 36 us -> none  [the longest x5 20.5 us: across_rows(): return lax.all_to_all(block, 'row', 0, 0)]
    all_to_all x6 -> x0, waiting for transfers between devices: 24.4 us -> none  [the longest x5 24.4 us: across_rows(): return lax.all_to_all(block, 'row', 0, 0)]
    ppermute x0 -> x12, starting transfers between devices: none -> 15.8 us  [exchanged(): return lax.ppermute(block, 'row', [(i, i ^ x) for i in range(ROWS)])]
    pallas_call x4 -> x5, Pallas kernels: 42.4 us -> 49 us  [the longest x2 35 us: chain(): pl.pallas_call(body, out_shape=(site,) * ROWS + (jax.ShapeDtypeStruct((co...]
    ppermute x3, starting transfers between devices: 13.2 us -> 7.94 us  [passed_along(): return lax.ppermute(block, axis, route)]
    all_to_all x2 -> x1, blocking collectives: 17.4 us -> 21.1 us  [on_device(): gathered = lax.all_to_all(stats, ('row', 'col'), 0, 0, tiled=True)]
    squeeze x3 -> x0, local copies, waits for them, and re-layouts: 3.63 us -> none  [the longest x1 1.86 us: on_device(): lefts = jnp.where(inside, proj_in[0, 0], zero)]
    slice x4 -> x0, local copies, waits for them, and re-layouts: 3.33 us -> none  [the longest x1 2.17 us: lefts_and_transfers(): return jnp.concatenate([parts(lefts, k), transfers[:, k:k + 1]], axis=1)]
  transfers between devices with their start and end apart: 9 -> 15, of which waited for: 3 -> 2; matrix products, arithmetic and copies ran while one was open for 3% -> 1% of each run, Pallas kernels for 17% -> 31%
where the time goes in v2:
time: 100 us
  Pallas kernels  51.6 us (52%)
  starting transfers between devices  23.7 us (24%)
  blocking collectives  21.1 us (21%)
  waiting for transfers between devices  2.11 us (2%)
    pallas_call x2, Pallas kernels, chain(): pl.pallas_call(body, out_shape=(site,) * ROWS + (jax.ShapeDtypeStruct((co...  35 us
    all_to_all x1, blocking collectives, on_device(): gathered = lax.all_to_all(stats, ('row', 'col'), 0, 0, tiled=True)  21.1 us
    ppermute x12, starting transfers between devices, exchanged(): return lax.ppermute(block, 'row', [(i, i ^ x) for i in range(ROWS)])  15.8 us
    pallas_call x1, Pallas kernels, observable_weights(): pl.pallas_call(weight_kernel, out_shape=(jax.ShapeDtypeStruct((2, SEC, PA...  7.97 us
    ppermute x3, starting transfers between devices, passed_along(): return lax.ppermute(block, axis, route)  7.94 us
    pallas_call x1, Pallas kernels, pack_first(): pl.pallas_call(pack_first_kernel, out_shape=(piece,) * ROWS + (right,) *...  3.74 us
    pallas_call x1, Pallas kernels, finish(): pl.pallas_call(lambda *refs: finish_kernel(entries, *refs), out_shape=(ja...  2.59 us
    pallas_call x1, Pallas kernels, pack_second(): pl.pallas_call(pack_second_kernel, out_shape=(one,) * ROWS + (three,) * R...  2.29 us
  transfers between devices with their start and end apart: 15, of which 2 were waited for; matrix products, arithmetic and copies ran while one was open for 1% of the time, Pallas kernels for 31%

profile of v2, /device:TPU:1, one launch (start us, length us, event | category | flops | bytes accessed | tf_op | source)
XLA Modules:
  0.0 100.1 jit_solution(1547912161202316753)
XLA Ops:
  0.7 1.5 %collective-permute-start.2 = (bf16[8,64,64]{2,1,0:T(8,128)(2,1)}, bf16[8,64,64]{2,1,0:T(8,128)(2,1)S(1)}, u32[]{:S(2)}, u32[]{:S(2)}) collective-permute-start(bf16[8,64,64]{2,1,0:T(8,128)(2,1)} %bitcast.25), channel_id=1, source_target_pairs={{1,0},{2,1},{3,2},{4,3},{5,4},{6,5},{7,6},{8,7},{9,8},{10,9},{11,1... | collective-permute-start | bytes 196616 | tf_op jit(solution)/shard_map/ppermute | solution.py:400
  2.2 0.7 pad_add_fusion.me_ref.refs_0_
  2.8 3.7 %pack_first.1 = (bf16[2,256,256]{2,1,0:T(8,128)(2,1)}, bf16[2,256,256]{2,1,0:T(8,128)(2,1)}, bf16[2,256,256]{2,1,0:T(8,128)(2,1)}, bf16[2,256,256]{2,1,0:T(8,128...) custom-call(s32[2]{0:T(128)} %pad_add_fusion.me_ref.refs_0_, s32[1,8]{1,0:T(1,128)} %rank_ref.3, ...), custom_call_target="tpu_custom_call" | custom-call | flops 1000000 | bytes 2097152 | tf_op jit(solution)/shard_map/pack_first/pallas_call | solution.py:97
  6.6 1.5 %collective-permute-start.6 = (bf16[2,256,256]{2,1,0:T(8,128)(2,1)}, bf16[2,256,256]{2,1,0:T(8,128)(2,1)S(1)}, u32[]{:S(2)}, u32[]{:S(2)}) collective-permute-start(bf16[2,256,256]{2,1,0:T(8,128)(2,1)} %get-tuple-element.42), channel_id=1, source_target_pairs={{0,32},{32,0},{64,96},{96,64},{1,33},{33,1},{65,97},{97,65},{2,34}... | collective-permute-start | bytes 786440 | tf_op jit(solution)/shard_map/ppermute | solution.py:404
  8.0 2.6 %collective-permute-start.7 = (bf16[2,256,256]{2,1,0:T(8,128)(2,1)}, bf16[2,256,256]{2,1,0:T(8,128)(2,1)S(1)}, u32[]{:S(2)}, u32[]{:S(2)}) collective-permute-start(bf16[2,256,256]{2,1,0:T(8,128)(2,1)} %get-tuple-element.43), channel_id=1, source_target_pairs={{0,64},{32,96},{64,0},{96,32},{1,65},{33,97},{65,1},{97,33},{2,66}... | collective-permute-start | bytes 786440 | tf_op jit(solution)/shard_map/ppermute | solution.py:404
  10.6 6.5 %collective-permute-start = (bf16[4,64,1024]{2,1,0:T(8,128)(2,1)}, bf16[4,64,1024]{2,1,0:T(8,128)(2,1)S(1)}, u32[]{:S(2)}, u32[]{:S(2)}) collective-permute-start(bf16[4,64,1024]{2,1,0:T(8,128)(2,1)} %get-tuple-element.33), channel_id=1, source_target_pairs={{1,0},{2,1},{3,2},{4,3},{5,4},{6,5},{7,6},{8,7},{9,8},{10,9},{11,1... | collective-permute-start | bytes 1572872 | tf_op jit(solution)/shard_map/ppermute | solution.py:400
  17.1 0.0 copy-start
  17.1 0.0 copy-start.1
  17.2 8.0 %observable_weights.1 = (bf16[2,8,64,1024]{3,2,1,0:T(8,128)(2,1)S(1)}, f32[8,128]{1,0:T(8,128)S(1)}, bf16[1024,1024]{1,0:T(8,128)(2,1)S(1)}) custom-call(bf16[8,64,64]{2,1,0:T(8,128)(2,1)S(1)} %bitcast.26, bf16[8,64,64]{2,1,0:T(8,128)(2,1)S(1)} %collective-permute-done.2.er_ref, bf16[2,8,16,16]{3,2,1,0:T(8,128)(2,1)S(1)} %copy-done.8, ...), custom_call_target="tpu_custom_call" | custom-call | flops 6000000000 | bytes 4194304 | tf_op jit(solution)/shard_map/observable_weights/pallas_call | solution.py:316
  25.2 1.0 %collective-permute-done.1.q2_ref = bf16[4,64,1024]{2,1,0:T(8,128)(2,1)S(1)} collective-permute-done((bf16[4,64,1024]{2,1,0:T(8,128)(2,1)}, bf16[4,64,1024]{2,1,0:T(8,128)(2,1)S(1)}, u32[]{:S(2)}, u32[]{:S(2)}) %collective-permute-start.1) | collective-permute-done | bytes 524320 | tf_op jit(solution)/shard_map/ppermute | solution.py:400
  26.2 2.3 %pack_second.1 = (bf16[256,256]{1,0:T(8,128)(2,1)S(1)}, bf16[256,256]{1,0:T(8,128)(2,1)S(1)}, bf16[256,256]{1,0:T(8,128)(2,1)S(1)}, bf16[256,256]{1,0:T(8,128)(2...) custom-call(s32[2]{0:T(128)S(1)} %copy-done.2, ...), custom_call_target="tpu_custom_call" | custom-call | flops 1000000 | bytes 4194304 | tf_op jit(solution)/shard_map/pack_second/pallas_call | solution.py:142
  28.5 0.1 collective-permute-start.9
  28.6 3.6 %collective-permute-start.10 = (bf16[256,256]{1,0:T(8,128)(2,1)S(1)}, bf16[256,256]{1,0:T(8,128)(2,1)S(1)}, u32[]{:S(2)}, u32[]{:S(2)}) collective-permute-start(bf16[256,256]{1,0:T(8,128)(2,1)S(1)} %get-tuple-element.47), channel_id=1, source_target_pairs={{0,64},{32,96},{64,0},{96,32},{1,65},{33,97},{65,1},{97,33},{2,66}... | collective-permute-start | bytes 393224 | tf_op jit(solution)/shard_map/ppermute | solution.py:404
  32.2 0.2 collective-permute-start.11
  32.5 3.6 %collective-permute-start.4 = (bf16[3,256,256]{2,1,0:T(8,128)(2,1)S(1)}, bf16[3,256,256]{2,1,0:T(8,128)(2,1)S(1)}, u32[]{:S(2)}, u32[]{:S(2)}) collective-permute-start(bf16[3,256,256]{2,1,0:T(8,128)(2,1)S(1)} %get-tuple-element.38), channel_id=1, source_target_pairs={{0,64},{32,96},{64,0},{96,32},{1,65},{33,97},{65,1},{97,33},{2,66}... | collective-permute-start | bytes 1179656 | tf_op jit(solution)/shard_map/ppermute | solution.py:404
  36.1 0.2 collective-permute-start.5
  36.3 1.0 %collective-permute-done.11.refs_8_ = bf16[256,256]{1,0:T(8,128)(2,1)S(1)} collective-permute-done((bf16[256,256]{1,0:T(8,128)(2,1)S(1)}, bf16[256,256]{1,0:T(8,128)(2,1)S(1)}, u32[]{:S(2)}, u32[]{:S(2)}) %collective-permute-start.11) | collective-permute-done | bytes 131104 | tf_op jit(solution)/shard_map/ppermute | solution.py:404
  37.4 17.5 %chain_first.1 = (bf16[1,64,1024]{2,1,0:T(8,128)(2,1)S(1)}, bf16[1,64,1024]{2,1,0:T(8,128)(2,1)S(1)}, bf16[1,64,1024]{2,1,0:T(8,128)(2,1)S(1)}, bf16[1,64,1024]{2,1,0:T(8,128)(2,1)S(1)}, f32[8,128]{1,0:T(8,128)S(1)}) custom-call(s32[2]{0:T(128)S(1)} %copy-done.2, bf16[2,256,256]{2,1,0:T(8,128)(2,1)S(1)} %copy-done.6, ...), custom_call_target="tpu_custom_call" | custom-call | flops 12000000000 | bytes 4194304 | tf_op jit(solution)/shard_map/chain_first/pallas_call | solution.py:252
  54.9 17.5 %chain_second.1 = (bf16[2,64,1024]{2,1,0:T(8,128)(2,1)S(1)}, bf16[2,64,1024]{2,1,0:T(8,128)(2,1)S(1)}, bf16[2,64,1024]{2,1,0:T(8,128)(2,1)S(1)}, bf16[2,64,1024]{2,1,0:T(8,128)(2,1)S(1)}, f32[128,128]{1,0:T(8,128)S(1)}) custom-call(s32[2]{0:T(128)S(1)} %copy-done.2, bf16[3,256,256]{2,1,0:T(8,128)(2,1)S(1)} %get-tuple-element.36.refs_1_, ...), custom_call_target="tpu_custom_call" | custom-call | flops 12000000000 | bytes 4194304 | tf_op jit(solution)/shard_map/chain_second/pallas_call | solution.py:252
  72.4 0.1 collective-permute-start.12
  72.5 2.6 %collective-permute-start.13 = (bf16[2,64,1024]{2,1,0:T(8,128)(2,1)S(1)}, bf16[2,64,1024]{2,1,0:T(8,128)(2,1)S(1)}, u32[]{:S(2)}, u32[]{:S(2)}) collective-permute-start(bf16[2,64,1024]{2,1,0:T(8,128)(2,1)S(1)} %get-tuple-element.58), channel_id=1, source_target_pairs={{0,64},{32,96},{64,0},{96,32},{1,65},{33,97},{65,1},{97,33},{2,66}... | collective-permute-start | bytes 786440 | tf_op jit(solution)/shard_map/ppermute | solution.py:404
  75.1 1.3 %collective-permute-start.14 = (bf16[2,64,1024]{2,1,0:T(8,128)(2,1)S(1)}, bf16[2,64,1024]{2,1,0:T(8,128)(2,1)S(1)}, u32[]{:S(2)}, u32[]{:S(2)}) collective-permute-start(bf16[2,64,1024]{2,1,0:T(8,128)(2,1)S(1)} %get-tuple-element.59), channel_id=1, source_target_pairs={{0,96},{32,64},{64,32},{96,0},{1,97},{33,65},{65,33},{97,1},{2,98}... | collective-permute-start | bytes 786440 | tf_op jit(solution)/shard_map/ppermute | solution.py:404
  76.4 21.1 %all_to_all.11 = f32[128,1,128]{2,1,0:T(1,128)S(1)} all-to-all(f32[128,1,128]{2,1,0:T(1,128)S(1)} %bitcast.21), channel_id=1, replica_groups=mesh['row'=4,'col'=32] {'row','col'}, dimensions={0} | all-to-all | bytes 131072 | tf_op jit(solution)/shard_map/all_to_all | solution.py:437
  97.5 2.6 %finish.1 = (bf16[8,64,1024]{2,1,0:T(8,128)(2,1)}, f32[1,8]{1,0:T(1,128)}, f32[2,8]{1,0:T(2,128)}) custom-call(s32[2]{0:T(128)S(1)} %copy-done.2, f32[128,128]{1,0:T(8,128)S(1)} %bitcast.20, bf16[2,8,64,1024]{3,2,1,0:T(8,128)(2,1)S(1)} %get-tuple-element.55.refs_2_, bf16[2,64,1024]{2,1,0:T(8,128)(2,1)S(1)} %get-tuple-element.56.refs_3_, ...), custom_call_target="tpu_custom_call" | custom-call | flops 2000000 | bytes 2097152 | tf_op jit(solution)/shard_map/finish/pallas_call | solution.py:382
  (32 shorter events, 0.1 us)
Async XLA Ops:
  0.6 16.5 %copy-start.7 = (bf16[1,1,8,64,64]{4,3,2,1,0:T(8,128)(2,1)S(1)}, bf16[1,1,8,64,64]{4,3,2,1,0:T(8,128)(2,1)}, u32[]{:S(2)}) copy-start(bf16[1,1,8,64,64]{4,3,2,1,0:T(8,128)(2,1)} %param.13) | copy-start | bytes 196612
  0.6 16.5 %copy-start.8 = (bf16[2,8,16,16]{3,2,1,0:T(8,128)(2,1)S(1)}, bf16[2,8,16,16]{3,2,1,0:T(8,128)(2,1)}, u32[]{:S(2)}) copy-start(bf16[2,8,16,16]{3,2,1,0:T(8,128)(2,1)} %op_ref.1) | copy-start | bytes 24580
  0.7 16.5 %copy-start.4 = (bf16[1,1,8,64,1024]{4,3,2,1,0:T(8,128)(2,1)S(1)}, bf16[1,1,8,64,1024]{4,3,2,1,0:T(8,128)(2,1)}, u32[]{:S(2)}) copy-start(bf16[1,1,8,64,1024]{4,3,2,1,0:T(8,128)(2,1)} %param.12) | copy-start | bytes 3145732
  0.7 16.4 %collective-permute-start.2 = (bf16[8,64,64]{2,1,0:T(8,128)(2,1)}, bf16[8,64,64]{2,1,0:T(8,128)(2,1)S(1)}, u32[]{:S(2)}, u32[]{:S(2)}) collective-permute-start(bf16[8,64,64]{2,1,0:T(8,128)(2,1)} %bitcast.25), channel_id=1, source_target_pairs={{1,0},{2,1},{3,2},{4,3},{5,4},{6,5},{7,6},{8,7},{9,8},{10,9},{11,1... | collective-permute-start | bytes 196616 | tf_op jit(solution)/shard_map/ppermute | solution.py:400
  6.6 25.7 %collective-permute-start.6 = (bf16[2,256,256]{2,1,0:T(8,128)(2,1)}, bf16[2,256,256]{2,1,0:T(8,128)(2,1)S(1)}, u32[]{:S(2)}, u32[]{:S(2)}) collective-permute-start(bf16[2,256,256]{2,1,0:T(8,128)(2,1)} %get-tuple-element.42), channel_id=1, source_target_pairs={{0,32},{32,0},{64,96},{96,64},{1,33},{33,1},{65,97},{97,65},{2,34}... | collective-permute-start | bytes 786440 | tf_op jit(solution)/shard_map/ppermute | solution.py:404
  8.0 24.5 %collective-permute-start.7 = (bf16[2,256,256]{2,1,0:T(8,128)(2,1)}, bf16[2,256,256]{2,1,0:T(8,128)(2,1)S(1)}, u32[]{:S(2)}, u32[]{:S(2)}) collective-permute-start(bf16[2,256,256]{2,1,0:T(8,128)(2,1)} %get-tuple-element.43), channel_id=1, source_target_pairs={{0,64},{32,96},{64,0},{96,32},{1,65},{33,97},{65,1},{97,33},{2,66}... | collective-permute-start | bytes 786440 | tf_op jit(solution)/shard_map/ppermute | solution.py:404
  10.6 21.8 %collective-permute-start.8 = (bf16[2,256,256]{2,1,0:T(8,128)(2,1)}, bf16[2,256,256]{2,1,0:T(8,128)(2,1)S(1)}, u32[]{:S(2)}, u32[]{:S(2)}) collective-permute-start(bf16[2,256,256]{2,1,0:T(8,128)(2,1)} %get-tuple-element.44), channel_id=1, source_target_pairs={{0,96},{32,64},{64,32},{96,0},{1,97},{33,65},{65,33},{97,1},{2,98}... | collective-permute-start | bytes 786440 | tf_op jit(solution)/shard_map/ppermute | solution.py:404
  10.6 14.5 %collective-permute-start = (bf16[4,64,1024]{2,1,0:T(8,128)(2,1)}, bf16[4,64,1024]{2,1,0:T(8,128)(2,1)S(1)}, u32[]{:S(2)}, u32[]{:S(2)}) collective-permute-start(bf16[4,64,1024]{2,1,0:T(8,128)(2,1)} %get-tuple-element.33), channel_id=1, source_target_pairs={{1,0},{2,1},{3,2},{4,3},{5,4},{6,5},{7,6},{8,7},{9,8},{10,9},{11,1... | collective-permute-start | bytes 1572872 | tf_op jit(solution)/shard_map/ppermute | solution.py:400
  17.1 9.1 %collective-permute-start.1 = (bf16[4,64,1024]{2,1,0:T(8,128)(2,1)}, bf16[4,64,1024]{2,1,0:T(8,128)(2,1)S(1)}, u32[]{:S(2)}, u32[]{:S(2)}) collective-permute-start(bf16[4,64,1024]{2,1,0:T(8,128)(2,1)} %get-tuple-element.34), channel_id=1, source_target_pairs={{1,0},{2,1},{3,2},{4,3},{5,4},{6,5},{7,6},{8,7},{9,8},{10,9},{11,1... | collective-permute-start | bytes 1572872 | tf_op jit(solution)/shard_map/ppermute | solution.py:400
  17.1 9.1 %copy-start = (bf16[1,1,8,64,1024]{4,3,2,1,0:T(8,128)(2,1)S(1)}, bf16[1,1,8,64,1024]{4,3,2,1,0:T(8,128)(2,1)}, u32[]{:S(2)}) copy-start(bf16[1,1,8,64,1024]{4,3,2,1,0:T(8,128)(2,1)} %param.10) | copy-start | bytes 3145732
  17.1 9.1 %copy-start.1 = (bf16[1,1,8,256,256]{4,3,2,1,0:T(8,128)(2,1)S(1)}, bf16[1,1,8,256,256]{4,3,2,1,0:T(8,128)(2,1)}, u32[]{:S(2)}) copy-start(bf16[1,1,8,256,256]{4,3,2,1,0:T(8,128)(2,1)} %param.9) | copy-start | bytes 3145732
  17.1 9.1 %copy-start.2 = (s32[2]{0:T(128)S(1)}, s32[2]{0:T(128)}, u32[]{:S(2)}) copy-start(s32[2]{0:T(128)} %pad_add_fusion.me_ref.refs_0_) | copy-start | bytes 28
  17.2 9.1 %copy-start.3 = (s32[1,8]{1,0:T(1,128)S(1)}, s32[1,8]{1,0:T(1,128)}, u32[]{:S(2)}) copy-start(s32[1,8]{1,0:T(1,128)} %rank_ref.3) | copy-start | bytes 100
  25.1 12.2 %copy-start.5 = (bf16[1,8,64,1024]{3,2,1,0:T(8,128)(2,1)S(1)}, bf16[1,8,64,1024]{3,2,1,0:T(8,128)(2,1)}, u32[]{:S(2)}) copy-start(bf16[1,8,64,1024]{3,2,1,0:T(8,128)(2,1)} %param.8) | copy-start | bytes 3145732
  25.2 12.2 %copy-start.6 = (bf16[2,256,256]{2,1,0:T(8,128)(2,1)S(1)}, bf16[2,256,256]{2,1,0:T(8,128)(2,1)}, u32[]{:S(2)}) copy-start(bf16[2,256,256]{2,1,0:T(8,128)(2,1)} %get-tuple-element.41.refs_1_) | copy-start | bytes 786436
  28.5 7.6 %collective-permute-start.9 = (bf16[256,256]{1,0:T(8,128)(2,1)S(1)}, bf16[256,256]{1,0:T(8,128)(2,1)S(1)}, u32[]{:S(2)}, u32[]{:S(2)}) collective-permute-start(bf16[256,256]{1,0:T(8,128)(2,1)S(1)} %get-tuple-element.46), channel_id=1, source_target_pairs={{0,32},{32,0},{64,96},{96,64},{1,33},{33,1},{65,97},{97,65},{2,34}... | collective-permute-start | bytes 393224 | tf_op jit(solution)/shard_map/ppermute | solution.py:404
  28.6 7.7 %collective-permute-start.10 = (bf16[256,256]{1,0:T(8,128)(2,1)S(1)}, bf16[256,256]{1,0:T(8,128)(2,1)S(1)}, u32[]{:S(2)}, u32[]{:S(2)}) collective-permute-start(bf16[256,256]{1,0:T(8,128)(2,1)S(1)} %get-tuple-element.47), channel_id=1, source_target_pairs={{0,64},{32,96},{64,0},{96,32},{1,65},{33,97},{65,1},{97,33},{2,66}... | collective-permute-start | bytes 393224 | tf_op jit(solution)/shard_map/ppermute | solution.py:404
  32.2 5.2 %collective-permute-start.11 = (bf16[256,256]{1,0:T(8,128)(2,1)S(1)}, bf16[256,256]{1,0:T(8,128)(2,1)S(1)}, u32[]{:S(2)}, u32[]{:S(2)}) collective-permute-start(bf16[256,256]{1,0:T(8,128)(2,1)S(1)} %get-tuple-element.48), channel_id=1, source_target_pairs={{0,96},{32,64},{64,32},{96,0},{1,97},{33,65},{65,33},{97,1},{2,98}... | collective-permute-start | bytes 393224 | tf_op jit(solution)/shard_map/ppermute | solution.py:404
  32.5 22.4 %collective-permute-start.3 = (bf16[3,256,256]{2,1,0:T(8,128)(2,1)S(1)}, bf16[3,256,256]{2,1,0:T(8,128)(2,1)S(1)}, u32[]{:S(2)}, u32[]{:S(2)}) collective-permute-start(bf16[3,256,256]{2,1,0:T(8,128)(2,1)S(1)} %get-tuple-element.37), channel_id=1, source_target_pairs={{0,32},{32,0},{64,96},{96,64},{1,33},{33,1},{65,97},{97,65},{2,34}... | collective-permute-start | bytes 1179656 | tf_op jit(solution)/shard_map/ppermute | solution.py:404
  32.5 22.4 %collective-permute-start.4 = (bf16[3,256,256]{2,1,0:T(8,128)(2,1)S(1)}, bf16[3,256,256]{2,1,0:T(8,128)(2,1)S(1)}, u32[]{:S(2)}, u32[]{:S(2)}) collective-permute-start(bf16[3,256,256]{2,1,0:T(8,128)(2,1)S(1)} %get-tuple-element.38), channel_id=1, source_target_pairs={{0,64},{32,96},{64,0},{96,32},{1,65},{33,97},{65,1},{97,33},{2,66}... | collective-permute-start | bytes 1179656 | tf_op jit(solution)/shard_map/ppermute | solution.py:404
  36.1 18.8 %collective-permute-start.5 = (bf16[3,256,256]{2,1,0:T(8,128)(2,1)S(1)}, bf16[3,256,256]{2,1,0:T(8,128)(2,1)S(1)}, u32[]{:S(2)}, u32[]{:S(2)}) collective-permute-start(bf16[3,256,256]{2,1,0:T(8,128)(2,1)S(1)} %get-tuple-element.39), channel_id=1, source_target_pairs={{0,96},{32,64},{64,32},{96,0},{1,97},{33,65},{65,33},{97,1},{2,98}... | collective-permute-start | bytes 1179656 | tf_op jit(solution)/shard_map/ppermute | solution.py:404
  72.4 25.1 %collective-permute-start.12 = (bf16[2,64,1024]{2,1,0:T(8,128)(2,1)S(1)}, bf16[2,64,1024]{2,1,0:T(8,128)(2,1)S(1)}, u32[]{:S(2)}, u32[]{:S(2)}) collective-permute-start(bf16[2,64,1024]{2,1,0:T(8,128)(2,1)S(1)} %get-tuple-element.57), channel_id=1, source_target_pairs={{0,32},{32,0},{64,96},{96,64},{1,33},{33,1},{65,97},{97,65},{2,34}... | collective-permute-start | bytes 786440 | tf_op jit(solution)/shard_map/ppermute | solution.py:404
  72.5 25.0 %collective-permute-start.13 = (bf16[2,64,1024]{2,1,0:T(8,128)(2,1)S(1)}, bf16[2,64,1024]{2,1,0:T(8,128)(2,1)S(1)}, u32[]{:S(2)}, u32[]{:S(2)}) collective-permute-start(bf16[2,64,1024]{2,1,0:T(8,128)(2,1)S(1)} %get-tuple-element.58), channel_id=1, source_target_pairs={{0,64},{32,96},{64,0},{96,32},{1,65},{33,97},{65,1},{97,33},{2,66}... | collective-permute-start | bytes 786440 | tf_op jit(solution)/shard_map/ppermute | solution.py:404
  75.1 22.4 %collective-permute-start.14 = (bf16[2,64,1024]{2,1,0:T(8,128)(2,1)S(1)}, bf16[2,64,1024]{2,1,0:T(8,128)(2,1)S(1)}, u32[]{:S(2)}, u32[]{:S(2)}) collective-permute-start(bf16[2,64,1024]{2,1,0:T(8,128)(2,1)S(1)} %get-tuple-element.59), channel_id=1, source_target_pairs={{0,96},{32,64},{64,32},{96,0},{1,97},{33,65},{65,33},{97,1},{2,98}... | collective-permute-start | bytes 786440 | tf_op jit(solution)/shard_map/ppermute | solution.py:404

commit v3 on v2

v3 whole, which is shorter than its diff:
```python
import math

import jax
import jax.numpy as jnp
import numpy as np
from jax import lax
from jax.experimental import pallas as pl
from jax.experimental.pallas import tpu as pltpu
from jax.sharding import PartitionSpec as P

SEC = 8
PAD = 64
KM = 16
DB = 16
ROWS = 4
WIDE = 256
GROUPS = WIDE // PAD
SITE = KM * PAD
LANES = 128

BF16 = jnp.bfloat16
F32 = jnp.float32

epsilon = 1e-06


def mm(a, b):
    return jnp.dot(a, b, preferred_element_type=F32)


def mmt(a, b):
    return lax.dot_general(a, b, (((1,), (1,)), ((), ())), preferred_element_type=F32)


def iota2(shape, dim):
    return lax.broadcasted_iota(jnp.int32, shape, dim)


def digit_swap():
    i, j = iota2((WIDE, WIDE), 0), iota2((WIDE, WIDE), 1)
    return jnp.where((i // 16 == j % 16) & (i % 16 == j // 16), 1.0, 0.0).astype(BF16)


def bond_swap():
    i = np.arange(SITE)
    matrix = np.zeros((SITE, SITE), np.float32)
    matrix[i, (i % DB) * PAD + i // DB] = 1.0
    return jnp.asarray(matrix, BF16)


def total(x):
    return jnp.sum(jnp.sum(x, axis=1, keepdims=True), axis=0, keepdims=True)


def vmem(count):
    return [pl.BlockSpec(memory_space=pltpu.VMEM)] * count


def smem():
    return pl.BlockSpec(memory_space=pltpu.SMEM)


def masked(block, inside):
    return jnp.where(inside, block.astype(F32), 0.0).astype(BF16)


def anywhere(count):
    return [pl.BlockSpec(memory_space=pl.ANY)] * count


def params(mib):
    return pltpu.CompilerParams(vmem_limit_bytes=mib << 20)


def light(mib):
    return pl.CostEstimate(flops=1_000_000, bytes_accessed=mib << 20, transcendentals=0)


def pack_kernel(k, rank_ref, p_ref, t_ref, after_ref, *refs):
    rights, raws = (), ()
    if k == 0:
        q_ref, *refs = refs
        outs, raws, (held, sems) = refs[:ROWS], refs[ROWS : ROWS + 2], refs[ROWS + 2 :]
    else:
        *rights, outs, held, sems = refs[0], refs[1 : ROWS + 1], refs[ROWS + 1], refs[ROWS + 2]
    me = lax.axis_index("row")
    at = iota2((PAD, WIDE), 0)
    copies = []
    for x in range(ROWS):
        s = 2 * (me ^ x) + k
        copies.append(
            (
                pltpu.make_async_copy(p_ref.at[s], held.at[x], sems.at[0, x]),
                pltpu.make_async_copy(t_ref.at[s], outs[x].at[1], sems.at[1, x]),
            )
        )
    picks = [
        pltpu.make_async_copy(q_ref.at[2 * (me ^ x) + j], raws[j].at[x], sems.at[2 + j, x])
        for j in range(len(raws))
        for x in range(ROWS)
    ]
    for pair in copies:
        for copy in pair:
            copy.start()
    for copy in picks:
        copy.start()
    for x in range(ROWS):
        inside = at < rank_ref[0, 2 * (me ^ x) + k]
        copies[x][0].wait()
        for g in range(GROUPS):
            rows, lanes = slice(g * PAD, (g + 1) * PAD), slice(g * WIDE, (g + 1) * WIDE)
            outs[x][0, rows, :] = masked(held[x, :, lanes], inside)
            if k == 1:
                outs[x][2, rows, :] = masked(rights[0][x, :, lanes], inside)
    for x in range(ROWS):
        copies[x][1].wait()
    for copy in picks:
        copy.wait()


def pack(k, ranks, p, t, after, *rights):
    raws = () if k else (jax.ShapeDtypeStruct((ROWS, PAD, SITE), BF16),) * 2
    return pl.pallas_call(
        lambda *refs: pack_kernel(k, *refs),
        out_shape=(jax.ShapeDtypeStruct((2 + k, WIDE, WIDE), BF16),) * ROWS + raws,
        in_specs=[smem()] + anywhere(3) + (vmem(1) if k else anywhere(1)),
        out_specs=tuple(vmem(ROWS + len(raws))),
        scratch_shapes=[pltpu.VMEM((ROWS, PAD, SITE), BF16), pltpu.SemaphoreType.DMA((4, ROWS))],
        compiler_params=params(8 if k else 56),
        cost_estimate=light(2),
        name="pack_second" if k else "pack_first",
    )(ranks, p, t, after, *rights)


def mask_rights_kernel(rank_ref, after_ref, q_ref, *outs):
    me = lax.axis_index("row")
    at = iota2((PAD, WIDE), 0)
    for x in range(ROWS):
        inside = at < rank_ref[0, 2 * (me ^ x)]
        for g in range(GROUPS):
            rows, lanes = slice(g * PAD, (g + 1) * PAD), slice(g * WIDE, (g + 1) * WIDE)
            outs[x][rows, :] = masked(q_ref[x, :, lanes], inside)


def mask_rights(ranks, after, q):
    return pl.pallas_call(
        mask_rights_kernel,
        out_shape=(jax.ShapeDtypeStruct((WIDE, WIDE), BF16),) * ROWS,
        in_specs=[smem()] + anywhere(1) + vmem(1),
        out_specs=tuple(vmem(ROWS)),
        compiler_params=params(8),
        cost_estimate=light(1),
        name="mask_rights",
    )(ranks, after, q)


def chain_kernel(
    pts, qs, m_ref, perm_ref, before_ref, befores, us, st_ref,
    bdm, bdq, xs, ys, qw, pw, lefts, middles, stack, site, place, zs, held, sem,
):
    me = lax.axis_index("row")
    k0 = len(befores) // ROWS
    start = pltpu.make_async_copy(m_ref.at[2 * me + k0], site, sem)
    start.start()
    swap = digit_swap()
    bdm[...] = jnp.zeros_like(bdm)
    bdq[...] = jnp.zeros_like(bdq)
    for pieces, dst in (([ref.at[0] for ref in pts], pw), (qs, qw)):
        acc = None
        for part in range(GROUPS):
            rows = jnp.concatenate([ref[part * PAD : (part + 1) * PAD, :] for ref in pieces], axis=0)
            term = mm(rows, perm_ref[part * WIDE : (part + 1) * WIDE, :])
            acc = term if acc is None else acc + term
        dst[...] = acc.astype(BF16)
    for x in range(ROWS):
        for w in range(DB):
            for g in range(GROUPS):
                stack[x, w * 16 : (w + 1) * 16, g * PAD : (g + 1) * PAD] = pw[
                    x * PAD + g * 16 : x * PAD + (g + 1) * 16, w * PAD : (w + 1) * PAD
                ]
    for x in range(ROWS):
        lefts[me ^ x] = mm(swap, stack[x]).astype(BF16)
        middles[me ^ x] = mm(mmt(swap, pts[x][1]).astype(BF16), swap).astype(BF16)
    start.wait()
    for x in range(len(befores)):
        us[x][0] = befores[x][0]
    lane = iota2((1, LANES), 1)
    stats = jnp.zeros((1, LANES), F32)
    inverse = None
    for r in range(ROWS):
        base = pl.multiple_of((me ^ r) * PAD, PAD)
        left, middle = lefts[r], middles[r]
        for k in range(KM):
            lanes = slice(k * PAD, (k + 1) * PAD)
            right = qw[pl.ds(base, PAD), lanes]
            for g in range(GROUPS):
                at = slice(g * PAD, (g + 1) * PAD)
                if r == 0:
                    bdm[k, at, at] = site[:, lanes]
                else:
                    for h in range(GROUPS):
                        bdm[k, g * PAD + h * 16 : g * PAD + (h + 1) * 16, at] = place[
                            k * 16 : (k + 1) * 16, h * PAD : (h + 1) * PAD
                        ]
                bdq[r % 2, at, k * WIDE + g * PAD : k * WIDE + (g + 1) * PAD] = right
            first = mm(left, bdm[k]).astype(BF16)
            xs[:, k * 16 : (k + 1) * 16, :] = first.reshape(16, 16, WIDE)
        for c in range(16):
            second = mm(middle, xs[c]).astype(BF16)
            for e in range(DB):
                ys[c * 16 : (c + 1) * 16, e * WIDE : (e + 1) * WIDE] = second[e * 16 : (e + 1) * 16]
            if r > 0:
                for g in range(GROUPS):
                    held[r - 1, g * 16 : (g + 1) * 16, c * PAD : (c + 1) * PAD] = place[
                        c * 16 : (c + 1) * 16, g * PAD : (g + 1) * PAD
                    ]

        @pl.when(me >= 0)
        def _(r=r):
            zs[...] = mmt(ys[...], bdq[r % 2])

        z = zs[...]
        if inverse is not None:
            z = z * inverse
        place[...] = mm(swap, z.astype(BF16)).astype(BF16)
        top = jnp.max(jnp.max(jnp.abs(z), axis=1, keepdims=True), axis=0, keepdims=True)
        top = jnp.where(top > 0, top, 1.0)
        inverse = 1.0 / top
        stats = jnp.where(lane == 2 * r, top, stats)
        stats = jnp.where(lane == 2 * r + 1, total(z * z), stats)
    for c in range(KM):
        for g in range(GROUPS):
            held[ROWS - 1, g * 16 : (g + 1) * 16, c * PAD : (c + 1) * PAD] = place[
                c * 16 : (c + 1) * 16, g * PAD : (g + 1) * PAD
            ]
    for x in range(ROWS):
        us[x][k0] = held[me ^ x]
    if befores:
        stats = jnp.where(lane < 2 * ROWS, before_ref[0:1, :], pltpu.roll(stats, 2 * ROWS, 1))
    st_ref[...] = jnp.broadcast_to(stats, st_ref.shape)


def chain(pts, qs, m, perm, before, befores, after, copies, name):
    inputs = [*pts, *(qs or ()), perm, *([before] if befores else []), *befores, after, m]
    sites = 2 if befores else 1

    def body(*refs):
        pt_refs, refs = refs[:ROWS], refs[ROWS:]
        if qs is None:
            q_refs = [ref.at[2] for ref in pt_refs]
        else:
            q_refs, refs = refs[:ROWS], refs[ROWS:]
        perm_ref, *refs = refs
        before_ref = None
        if befores:
            before_ref, *refs = refs
        before_sites, refs = refs[: len(befores)], refs[len(befores) :]
        _, m_ref, *refs = refs
        us, (st_ref, *scratch) = refs[:ROWS], refs[ROWS:]
        chain_kernel(
            pt_refs, q_refs, m_ref, perm_ref, before_ref, before_sites, us, st_ref, *scratch
        )

    site = jax.ShapeDtypeStruct((sites, PAD, SITE), BF16)
    return pl.pallas_call(
        body,
        out_shape=(site,) * ROWS + (jax.ShapeDtypeStruct((copies, LANES), F32),),
        in_specs=vmem(len(inputs) - 2) + anywhere(2),
        out_specs=tuple(vmem(ROWS + 1)),
        scratch_shapes=[
            pltpu.VMEM((KM, WIDE, WIDE), BF16),
            pltpu.VMEM((2, WIDE, DB * WIDE), BF16),
            pltpu.VMEM((16, WIDE, WIDE), BF16),
            pltpu.VMEM((WIDE, DB * WIDE), BF16),
            pltpu.VMEM((ROWS * PAD, SITE), BF16),
            pltpu.VMEM((ROWS * PAD, SITE), BF16),
            pltpu.VMEM((ROWS, WIDE, WIDE), BF16),
            pltpu.VMEM((ROWS, WIDE, WIDE), BF16),
            pltpu.VMEM((ROWS, WIDE, WIDE), BF16),
            pltpu.VMEM((PAD, SITE), BF16),
            pltpu.VMEM((WIDE, WIDE), BF16),
            pltpu.VMEM((WIDE, WIDE), F32),
            pltpu.VMEM((ROWS, PAD, SITE), BF16),
            pltpu.SemaphoreType.DMA,
        ],
        compiler_params=pltpu.CompilerParams(vmem_limit_bytes=24 << 20),
        cost_estimate=pl.CostEstimate(
            flops=12_000_000_000, bytes_accessed=4 << 20, transcendentals=0
        ),
        name=name,
    )(*inputs)


HALF = SEC // 2


def weight_kernel(first, el_ref, er_ref, op_ref, after_ref, lower_ref, w_ref, bde, stack, b_ref, sems):
    copies = [
        pltpu.make_async_copy(lower_ref.at[first + s], b_ref.at[s], sems.at[s]) for s in range(HALF)
    ]
    for copy in copies:
        copy.start()
    bde[...] = jnp.zeros_like(bde)
    spread = jnp.where(iota2((WIDE, KM), 0) // 16 == iota2((WIDE, KM), 1), 1.0, 0.0).astype(BF16)
    same = iota2((WIDE, WIDE), 0) % 16 == iota2((WIDE, WIDE), 1) % 16
    for copy in copies:
        copy.wait()

    both = {}
    for s in range(HALF):
        for g in range(GROUPS):
            at = slice(g * PAD, (g + 1) * PAD)
            bde[s, at, at] = er_ref[first + s]
    uppers = [mm(el_ref[first + s], b_ref[s]).astype(BF16) for s in range(HALF)]
    for s in range(HALF):
        for g in range(4):
            both[s, g] = mmt(uppers[s][:, g * WIDE : (g + 1) * WIDE], bde[s]).astype(BF16)
    for s in range(HALF):
        for l in range(KM):
            i = l % 4
            for h in range(GROUPS):
                stack[s, l * 16 : (l + 1) * 16, h * PAD : (h + 1) * PAD] = both[s, l // 4][
                    h * 16 : (h + 1) * 16, i * PAD : (i + 1) * PAD
                ]
    pairs = [(q, s) for s in range(HALF) for q in range(2)]
    spreads = [mm(spread, op_ref[q, first + s]).astype(BF16) for q, s in pairs]
    grown = [jnp.where(same, mmt(rows, spread), 0.0).astype(BF16) for rows in spreads]
    for (q, s), matrix in zip(pairs, grown):
        out = mm(matrix, stack[s]).astype(BF16)
        for k in range(KM):
            for h in range(GROUPS):
                w_ref[q, s, h * 16 : (h + 1) * 16, k * PAD : (k + 1) * PAD] = out[
                    k * 16 : (k + 1) * 16, h * PAD : (h + 1) * PAD
                ]


def observable_weights(first, lower, left_env, right_env, operators, after):
    return pl.pallas_call(
        lambda *refs: weight_kernel(first, *refs),
        out_shape=jax.ShapeDtypeStruct((2, HALF, PAD, SITE), BF16),
        in_specs=vmem(3) + anywhere(2),
        out_specs=vmem(1)[0],
        scratch_shapes=[
            pltpu.VMEM((HALF, WIDE, WIDE), BF16),
            pltpu.VMEM((HALF, WIDE, WIDE), BF16),
            pltpu.VMEM((HALF, PAD, SITE), BF16),
            pltpu.SemaphoreType.DMA((HALF,)),
        ],
        compiler_params=pltpu.CompilerParams(vmem_limit_bytes=16 << 20),
        cost_estimate=pl.CostEstimate(
            flops=3_000_000_000, bytes_accessed=2 << 20, transcendentals=0
        ),
        name="observable_weights",
    )(left_env, right_env, operators, after, lower)


def finish_kernel(entries, g_ref, *refs):
    *refs, low_ref, high_ref, out_ref, log_ref, obs_ref = refs
    us = refs
    row, col = lax.axis_index("row"), lax.axis_index("col")
    columns = g_ref.shape[0] // ROWS
    at_s = iota2((1, SEC), 1)
    at_qs, at_q = iota2((2, SEC), 1), iota2((2, SEC), 0)
    logs = jnp.zeros((1, SEC), F32)
    factors = []
    for i in range(ROWS):
        for k in range(2):
            scale = jnp.ones((columns, 1), F32)
            factor = jnp.zeros((columns, 1), F32)
            log = jnp.zeros((1, 1), F32)
            here = pl.ds(i * columns, columns)
            for r in range(ROWS):
                lane = 2 * ROWS * k + 2 * r
                squares = scale * scale * g_ref[here, lane + 1 : lane + 2]
                norm = jnp.sqrt(jnp.sum(squares, axis=0, keepdims=True) / entries + epsilon)
                scale = scale / norm
                factor = jnp.where(row == r, scale, factor)
                log = jnp.where(row == r, jnp.log(norm), log)
                scale = scale * g_ref[here, lane : lane + 1]
            at_col = iota2((columns, 1), 0) == col
            factors.append(jnp.sum(jnp.where(at_col, factor, 0.0), axis=0, keepdims=True))
            logs = jnp.where(at_s == 2 * i + k, log, logs)
    log_ref[...] = logs
    values = jnp.zeros((2, SEC), F32)
    for k in range(2):
        for x in range(ROWS):
            i = row ^ x
            s = 2 * i + k
            upper_half = i >= ROWS // 2
            at = s - jnp.where(upper_half, HALF, 0)
            factor = factors[k]
            for other in range(1, ROWS):
                factor = jnp.where(i == other, factors[2 * other + k], factor)
            u = us[x][k].astype(F32) * factor
            out_ref[s] = u.astype(BF16)
            for q in range(2):
                w = jnp.where(upper_half, high_ref[q, at].astype(F32), low_ref[q, at].astype(F32))
                value = total(u * w)
                values = jnp.where((at_q == q) & (at_qs == s), value, values)
    obs_ref[...] = values / math.sqrt(KM)


def finish(entries, gathered, weights, us):
    return pl.pallas_call(
        lambda *refs: finish_kernel(entries, *refs),
        out_shape=(
            jax.ShapeDtypeStruct((SEC, PAD, SITE), BF16),
            jax.ShapeDtypeStruct((1, SEC), F32),
            jax.ShapeDtypeStruct((2, SEC), F32),
        ),
        in_specs=vmem(3 + len(us)),
        out_specs=tuple(vmem(3)),
        compiler_params=pltpu.CompilerParams(vmem_limit_bytes=16 << 20),
        cost_estimate=pl.CostEstimate(flops=2_000_000, bytes_accessed=2 << 20, transcendentals=0),
        name="finish",
    )(gathered, *us, *weights)


def following(block):
    return passed_along(block, "col", -1)


def passed_along(block, axis, distance):
    devices = range(lax.axis_size(axis))
    route = [((i - distance) % len(devices), i) for i in devices]
    return lax.ppermute(block, axis, route)


def exchanged(block, x):
    return lax.ppermute(block, "row", [(i, i ^ x) for i in range(ROWS)])


NEAR_FIRST = (1, 3, 2)


def exchanged_all(blocks):
    got = {x: exchanged(blocks[x], x) for x in NEAR_FIRST}
    return [blocks[0]] + [got[x] for x in range(1, ROWS)]


def on_device(
    top_boundary, row_transfer, proj_in, proj_out, bottom_boundary, environments, operators, ranks
):
    columns = lax.axis_size("col")
    envs = environments[0, 0]
    lefts, transfers = proj_in[0, 0], row_transfer[0, 0]
    perm = bond_swap()
    lower = bottom_boundary[0, 0]
    *packed, q1, q2 = pack(0, ranks, lefts, transfers, ranks, proj_out[0, 0])
    pts1 = exchanged_all(packed)
    next1, next2, next_envs = following(q1), following(q2), following(envs)
    rights = mask_rights(ranks, ranks, next1)
    qs1 = exchanged_all(rights)
    packed = pack(1, ranks, lefts, transfers, rights[0], next2)
    ptqs2 = exchanged_all(packed)
    low = observable_weights(0, lower, envs, next_envs, operators, packed[0])
    top = top_boundary[0]
    *us1, stats = chain(pts1, qs1, top, perm, None, (), low, 8, "chain_first")
    high = observable_weights(HALF, lower, envs, next_envs, operators, stats)
    everyone = ROWS * columns
    *us, stats = chain(ptqs2, None, top, perm, stats, us1, high, everyone, "chain_second")
    us = exchanged_all(us)
    gathered = lax.all_to_all(stats, ("row", "col"), 0, 0, tiled=True)
    entries = float(columns * PAD * KM * PAD)
    sites, logs, values = finish(entries, gathered, (low, high), us)
    return sites[None, None], logs, values[:, None, None]


def solution(mesh):
    in_specs = (
        P("col", None, None, None),
        P("row", "col", None, None, None),
        P("row", "col", None, None, None),
        P("row", "col", None, None, None),
        P("row", "col", None, None, None),
        P("row", "col", None, None, None),
        P(),
        P("row", None),
    )
    out_specs = (P("row", "col", None, None, None), P("row", None), P(None, "row", "col", None))
    return jax.shard_map(
        on_device, mesh=mesh, in_specs=in_specs, out_specs=out_specs, check_vma=False
    )
```

time: 100 us -> 91.3 us (0.913)
  Pallas kernels: 51.6 us -> 40.9 us
  waiting for transfers between devices: 2.11 us -> 6.46 us
  blocking collectives: 21.1 us -> 20 us
    pallas_call x2, Pallas kernels: 35 us -> 26.2 us  [chain(): pl.pallas_call(body, out_shape=(site,) * ROWS + (jax.ShapeDtypeStruct((co...]
    ppermute x12, waiting for transfers between devices: 1.07 us -> 3.94 us  [exchanged(): return lax.ppermute(block, 'row', [(i, i ^ x) for i in range(ROWS)])]
    pallas_call x3 -> x5, Pallas kernels: 14 us -> 12.5 us  [the longest x2 6.12 us: pack(): pl.pallas_call(lambda *refs: pack_kernel(k, *refs), out_shape=(jax.ShapeD...]
    ppermute x3, waiting for transfers between devices: 1.04 us -> 2.53 us  [passed_along(): return lax.ppermute(block, axis, route)]
    all_to_all x1, blocking collectives: 21.1 us -> 20 us  [on_device(): gathered = lax.all_to_all(stats, ('row', 'col'), 0, 0, tiled=True)]
    ppermute x12, starting transfers between devices: 15.8 us -> 14.7 us  [exchanged(): return lax.ppermute(block, 'row', [(i, i ^ x) for i in range(ROWS)])]
  transfers between devices with their start and end apart: 15 -> 15, of which waited for: 2 -> 3; matrix products, arithmetic and copies ran while one was open for 1% -> 0% of each run, Pallas kernels for 31% -> 24%
where the time goes in v3:
time: 91.3 us; the launch traced here: 91.1 us
  Pallas kernels  40.9 us (45%)
  starting transfers between devices  22.9 us (25%)
  blocking collectives  20 us (22%)
  waiting for transfers between devices  6.46 us (7%)
    pallas_call x2, Pallas kernels, chain(): pl.pallas_call(body, out_shape=(site,) * ROWS + (jax.ShapeDtypeStruct((co...  26.2 us
    all_to_all x1, blocking collectives, on_device(): gathered = lax.all_to_all(stats, ('row', 'col'), 0, 0, tiled=True)  20 us
    ppermute x12, starting transfers between devices, exchanged(): return lax.ppermute(block, 'row', [(i, i ^ x) for i in range(ROWS)])  14.7 us
    ppermute x3, starting transfers between devices, passed_along(): return lax.ppermute(block, axis, route)  8.2 us
    pallas_call x2, Pallas kernels, pack(): pl.pallas_call(lambda *refs: pack_kernel(k, *refs), out_shape=(jax.ShapeD...  6.12 us
    pallas_call x2, Pallas kernels, observable_weights(): pl.pallas_call(lambda *refs: weight_kernel(first, *refs), out_shape=jax.S...  5.72 us
    ppermute x12, waiting for transfers between devices, exchanged(): return lax.ppermute(block, 'row', [(i, i ^ x) for i in range(ROWS)])  3.94 us
    ppermute x3, waiting for transfers between devices, passed_along(): return lax.ppermute(block, axis, route)  2.53 us
  transfers between devices with their start and end apart: 15, of which 3 were waited for; matrix products, arithmetic and copies ran while one was open for 0% of the time, Pallas kernels for 24%

profile of v3, /device:TPU:1, one launch (start us, length us, event | category | flops | bytes accessed | tf_op | source)
XLA Modules:
  0.0 91.1 jit_solution(18329757569419060438)
XLA Ops:
  0.7 3.9 %pack_first.1 = (bf16[2,256,256]{2,1,0:T(8,128)(2,1)}, bf16[2,256,256]{2,1,0:T(8,128)(2,1)}, bf16[2,256,256]{2,1,0:T(8,128)(2,1)}, bf16[2,256,256]{2,1,0:T(8,128...) custom-call(s32[1,8]{1,0:T(1,128)} %refs_0_.3, bf16[8,64,1024]{2,1,0:T(8,128)(2,1)} %bitcast.14, ...), custom_call_target="tpu_custom_call" | custom-call | flops 1000000 | bytes 2097152 | tf_op jit(solution)/shard_map/pack_first/pallas_call | solution.py:123
  4.6 1.5 %collective-permute-start = (bf16[4,64,1024]{2,1,0:T(8,128)(2,1)}, bf16[4,64,1024]{2,1,0:T(8,128)(2,1)S(1)}, u32[]{:S(2)}, u32[]{:S(2)}) collective-permute-start(bf16[4,64,1024]{2,1,0:T(8,128)(2,1)} %get-tuple-element.30), channel_id=1, source_target_pairs={{1,0},{2,1},{3,2},{4,3},{5,4},{6,5},{7,6},{8,7},{9,8},{10,9},{11,1... | collective-permute-start | bytes 1572872 | tf_op jit(solution)/shard_map/ppermute | solution.py:426
  6.1 5.8 %collective-permute-start.1 = (bf16[4,64,1024]{2,1,0:T(8,128)(2,1)}, bf16[4,64,1024]{2,1,0:T(8,128)(2,1)S(1)}, u32[]{:S(2)}, u32[]{:S(2)}) collective-permute-start(bf16[4,64,1024]{2,1,0:T(8,128)(2,1)} %get-tuple-element.32), channel_id=1, source_target_pairs={{1,0},{2,1},{3,2},{4,3},{5,4},{6,5},{7,6},{8,7},{9,8},{10,9},{11,1... | collective-permute-start | bytes 1572872 | tf_op jit(solution)/shard_map/ppermute | solution.py:426
  11.8 1.3 %collective-permute-start.5 = (bf16[2,256,256]{2,1,0:T(8,128)(2,1)}, bf16[2,256,256]{2,1,0:T(8,128)(2,1)S(1)}, u32[]{:S(2)}, u32[]{:S(2)}) collective-permute-start(bf16[2,256,256]{2,1,0:T(8,128)(2,1)} %get-tuple-element.38), channel_id=1, source_target_pairs={{0,32},{32,0},{64,96},{96,64},{1,33},{33,1},{65,97},{97,65},{2,34}... | collective-permute-start | bytes 786440 | tf_op jit(solution)/shard_map/ppermute | solution.py:430
  13.1 1.0 %collective-permute-start.11 = (bf16[8,64,64]{2,1,0:T(8,128)(2,1)S(1)}, bf16[8,64,64]{2,1,0:T(8,128)(2,1)S(1)}, u32[]{:S(2)}, u32[]{:S(2)}) collective-permute-start(bf16[8,64,64]{2,1,0:T(8,128)(2,1)S(1)} %bitcast.24), channel_id=1, source_target_pairs={{1,0},{2,1},{3,2},{4,3},{5,4},{6,5},{7,6},{8,7},{9,8},{10,9},{11,1... | collective-permute-start | bytes 196616 | tf_op jit(solution)/shard_map/ppermute | solution.py:426
  14.1 2.6 %collective-permute-start.6 = (bf16[2,256,256]{2,1,0:T(8,128)(2,1)}, bf16[2,256,256]{2,1,0:T(8,128)(2,1)S(1)}, u32[]{:S(2)}, u32[]{:S(2)}) collective-permute-start(bf16[2,256,256]{2,1,0:T(8,128)(2,1)} %get-tuple-element.39), channel_id=1, source_target_pairs={{0,64},{32,96},{64,0},{96,32},{1,65},{33,97},{65,1},{97,33},{2,66}... | collective-permute-start | bytes 786440 | tf_op jit(solution)/shard_map/ppermute | solution.py:430
  16.7 0.4 collective-permute-start.7
  17.1 0.6 mask_rights.1
  17.7 2.5 %collective-permute-done.1.refs_4_ = bf16[4,64,1024]{2,1,0:T(8,128)(2,1)S(1)} collective-permute-done((bf16[4,64,1024]{2,1,0:T(8,128)(2,1)}, bf16[4,64,1024]{2,1,0:T(8,128)(2,1)S(1)}, u32[]{:S(2)}, u32[]{:S(2)}) %collective-permute-start.1) | collective-permute-done | bytes 524320 | tf_op jit(solution)/shard_map/ppermute | solution.py:426
  20.2 1.3 %collective-permute-start.8 = (bf16[256,256]{1,0:T(8,128)(2,1)S(1)}, bf16[256,256]{1,0:T(8,128)(2,1)S(1)}, u32[]{:S(2)}, u32[]{:S(2)}) collective-permute-start(bf16[256,256]{1,0:T(8,128)(2,1)S(1)} %get-tuple-element.41), channel_id=1, source_target_pairs={{0,32},{32,0},{64,96},{96,64},{1,33},{33,1},{65,97},{97,65},{2,34}... | collective-permute-start | bytes 393224 | tf_op jit(solution)/shard_map/ppermute | solution.py:430
  21.5 2.3 %pack_second.1 = (bf16[3,256,256]{2,1,0:T(8,128)(2,1)S(1)}, bf16[3,256,256]{2,1,0:T(8,128)(2,1)S(1)}, bf16[3,256,256]{2,1,0:T(8,128)(2,1)S(1)}, bf16[3,256,256]{2,1,0:T(8,128)(2,1)S(1)}) custom-call(s32[1,8]{1,0:T(1,128)S(1)} %copy-done.2, bf16[8,64,1024]{2,1,0:T(8,128)(2,1)S(1)} %bitcast.15, bf16[8,256,256]{2,1,0:T(8,128)(2,1)S(1)} %bitcast.17, ...), custom_call_target="tpu_custom_call" | custom-call | flops 1000000 | bytes 2097152 | tf_op jit(solution)/shard_map/pack_second/pallas_call | solution.py:123
  23.8 2.7 %collective-permute-start.9 = (bf16[256,256]{1,0:T(8,128)(2,1)S(1)}, bf16[256,256]{1,0:T(8,128)(2,1)S(1)}, u32[]{:S(2)}, u32[]{:S(2)}) collective-permute-start(bf16[256,256]{1,0:T(8,128)(2,1)S(1)} %get-tuple-element.42), channel_id=1, source_target_pairs={{0,64},{32,96},{64,0},{96,32},{1,65},{33,97},{65,1},{97,33},{2,66}... | collective-permute-start | bytes 393224 | tf_op jit(solution)/shard_map/ppermute | solution.py:430
  26.6 2.9 %observable_weights.2.refs_9_.refs_5_ = bf16[2,4,64,1024]{3,2,1,0:T(8,128)(2,1)S(1)} custom-call(bf16[8,64,64]{2,1,0:T(8,128)(2,1)S(1)} %bitcast.25, bf16[8,64,64]{2,1,0:T(8,128)(2,1)S(1)} %collective-permute-done.11.refs_1_, bf16[2,8,16,16]{3,2,1,0:T(8,128)(2,1)S(1)} %copy-done.7, bf16[3,256,256]{2,1,0:T(8,128)(2,1)S(1)} %get-tuple-element.33.refs_3_.refs_0_, ...), custom_call_target="tpu_custom_call" | custom-call | flops 3000000000 | bytes 2097152 | tf_op jit(solution)/shard_map/observable_weights/pallas_call | solution.py:338
  29.4 0.1 collective-permute-start.2
  29.5 1.4 %collective-permute-done.7.refs_3_ = bf16[2,256,256]{2,1,0:T(8,128)(2,1)S(1)} collective-permute-done((bf16[2,256,256]{2,1,0:T(8,128)(2,1)}, bf16[2,256,256]{2,1,0:T(8,128)(2,1)S(1)}, u32[]{:S(2)}, u32[]{:S(2)}) %collective-permute-start.7) | collective-permute-done | bytes 262176 | tf_op jit(solution)/shard_map/ppermute | solution.py:430
  30.9 2.4 %collective-permute-start.3 = (bf16[3,256,256]{2,1,0:T(8,128)(2,1)S(1)}, bf16[3,256,256]{2,1,0:T(8,128)(2,1)S(1)}, u32[]{:S(2)}, u32[]{:S(2)}) collective-permute-start(bf16[3,256,256]{2,1,0:T(8,128)(2,1)S(1)} %get-tuple-element.35), channel_id=1, source_target_pairs={{0,64},{32,96},{64,0},{96,32},{1,65},{33,97},{65,1},{97,33},{2,66}... | collective-permute-start | bytes 1179656 | tf_op jit(solution)/shard_map/ppermute | solution.py:430
  33.4 2.5 %collective-permute-done.10.refs_7_ = bf16[256,256]{1,0:T(8,128)(2,1)S(1)} collective-permute-done((bf16[256,256]{1,0:T(8,128)(2,1)S(1)}, bf16[256,256]{1,0:T(8,128)(2,1)S(1)}, u32[]{:S(2)}, u32[]{:S(2)}) %collective-permute-start.10) | collective-permute-done | bytes 131104 | tf_op jit(solution)/shard_map/ppermute | solution.py:430
  35.9 13.2 %chain_first.1 = (bf16[1,64,1024]{2,1,0:T(8,128)(2,1)S(1)}, bf16[1,64,1024]{2,1,0:T(8,128)(2,1)S(1)}, bf16[1,64,1024]{2,1,0:T(8,128)(2,1)S(1)}, bf16[1,64,1024]{2,1,0:T(8,128)(2,1)S(1)}, f32[8,128]{1,0:T(8,128)S(1)}) custom-call(bf16[2,256,256]{2,1,0:T(8,128)(2,1)S(1)} %copy-done.5, bf16[2,256,256]{2,1,0:T(8,128)(2,1)S(1)} %collective-permute-done.5.refs_1_, ...), custom_call_target="tpu_custom_call" | custom-call | flops 12000000000 | bytes 4194304 | tf_op jit(solution)/shard_map/chain_first/pallas_call | solution.py:265
  49.1 2.9 %observable_weights.3.refs_10_.refs_6_ = bf16[2,4,64,1024]{3,2,1,0:T(8,128)(2,1)S(1)} custom-call(bf16[8,64,64]{2,1,0:T(8,128)(2,1)S(1)} %bitcast.26, bf16[8,64,64]{2,1,0:T(8,128)(2,1)S(1)} %collective-permute-done.11.refs_1_, bf16[2,8,16,16]{3,2,1,0:T(8,128)(2,1)S(1)} %copy-done.7, f32[8,128]{1,0:T(8,128)S(1)} %get-tuple-element.44.refs_3_.refs_5_, ...), custom_call_target="tpu_custom_call" | custom-call | flops 3000000000 | bytes 2097152 | tf_op jit(solution)/shard_map/observable_weights/pallas_call | solution.py:338
  52.0 13.0 %chain_second.1 = (bf16[2,64,1024]{2,1,0:T(8,128)(2,1)S(1)}, bf16[2,64,1024]{2,1,0:T(8,128)(2,1)S(1)}, bf16[2,64,1024]{2,1,0:T(8,128)(2,1)S(1)}, bf16[2,64,1024]{2,1,0:T(8,128)(2,1)S(1)}, f32[128,128]{1,0:T(8,128)S(1)}) custom-call(bf16[3,256,256]{2,1,0:T(8,128)(2,1)S(1)} %get-tuple-element.33.refs_3_.refs_0_, ...), custom_call_target="tpu_custom_call" | custom-call | flops 12000000000 | bytes 4194304 | tf_op jit(solution)/shard_map/chain_second/pallas_call | solution.py:265
  65.1 1.3 %collective-permute-start.13 = (bf16[2,64,1024]{2,1,0:T(8,128)(2,1)S(1)}, bf16[2,64,1024]{2,1,0:T(8,128)(2,1)S(1)}, u32[]{:S(2)}, u32[]{:S(2)}) collective-permute-start(bf16[2,64,1024]{2,1,0:T(8,128)(2,1)S(1)} %get-tuple-element.52), channel_id=1, source_target_pairs={{0,64},{32,96},{64,0},{96,32},{1,65},{33,97},{65,1},{97,33},{2,66}... | collective-permute-start | bytes 786440 | tf_op jit(solution)/shard_map/ppermute | solution.py:430
  66.5 2.5 %collective-permute-start.14 = (bf16[2,64,1024]{2,1,0:T(8,128)(2,1)S(1)}, bf16[2,64,1024]{2,1,0:T(8,128)(2,1)S(1)}, u32[]{:S(2)}, u32[]{:S(2)}) collective-permute-start(bf16[2,64,1024]{2,1,0:T(8,128)(2,1)S(1)} %get-tuple-element.53), channel_id=1, source_target_pairs={{0,96},{32,64},{64,32},{96,0},{1,97},{33,65},{65,33},{97,1},{2,98}... | collective-permute-start | bytes 786440 | tf_op jit(solution)/shard_map/ppermute | solution.py:430
  69.0 20.0 %all_to_all.11 = f32[128,1,128]{2,1,0:T(1,128)S(1)} all-to-all(f32[128,1,128]{2,1,0:T(1,128)S(1)} %bitcast.19), channel_id=1, replica_groups=mesh['row'=4,'col'=32] {'row','col'}, dimensions={0} | all-to-all | bytes 131072 | tf_op jit(solution)/shard_map/all_to_all | solution.py:463
  88.9 2.2 %finish.1 = (bf16[8,64,1024]{2,1,0:T(8,128)(2,1)}, f32[1,8]{1,0:T(1,128)}, f32[2,8]{1,0:T(2,128)}) custom-call(f32[128,128]{1,0:T(8,128)S(1)} %bitcast.18, bf16[2,64,1024]{2,1,0:T(8,128)(2,1)S(1)} %get-tuple-element.50.refs_1_, bf16[2,64,1024]{2,1,0:T(8,128)(2,1)S(1)} %collective-permute-done.12.refs_2_, ...), custom_call_target="tpu_custom_call" | custom-call | flops 2000000 | bytes 2097152 | tf_op jit(solution)/shard_map/finish/pallas_call | solution.py:404
  (33 shorter events, 0.2 us)
Async XLA Ops:
  0.6 16.4 %copy-start.2 = (s32[1,8]{1,0:T(1,128)S(1)}, s32[1,8]{1,0:T(1,128)}, u32[]{:S(2)}) copy-start(s32[1,8]{1,0:T(1,128)} %refs_0_.3) | copy-start | bytes 100
  0.6 20.9 %copy-start = (bf16[1,1,8,64,1024]{4,3,2,1,0:T(8,128)(2,1)S(1)}, bf16[1,1,8,64,1024]{4,3,2,1,0:T(8,128)(2,1)}, u32[]{:S(2)}) copy-start(bf16[1,1,8,64,1024]{4,3,2,1,0:T(8,128)(2,1)} %param.11) | copy-start | bytes 3145732
  0.7 20.9 %copy-start.1 = (bf16[1,1,8,256,256]{4,3,2,1,0:T(8,128)(2,1)S(1)}, bf16[1,1,8,256,256]{4,3,2,1,0:T(8,128)(2,1)}, u32[]{:S(2)}) copy-start(bf16[1,1,8,256,256]{4,3,2,1,0:T(8,128)(2,1)} %param.10) | copy-start | bytes 3145732
  0.7 12.5 %copy-start.6 = (bf16[1,1,8,64,64]{4,3,2,1,0:T(8,128)(2,1)S(1)}, bf16[1,1,8,64,64]{4,3,2,1,0:T(8,128)(2,1)}, u32[]{:S(2)}) copy-start(bf16[1,1,8,64,64]{4,3,2,1,0:T(8,128)(2,1)} %param.14) | copy-start | bytes 196612
  4.5 22.0 %copy-start.3 = (bf16[1,1,8,64,1024]{4,3,2,1,0:T(8,128)(2,1)S(1)}, bf16[1,1,8,64,1024]{4,3,2,1,0:T(8,128)(2,1)}, u32[]{:S(2)}) copy-start(bf16[1,1,8,64,1024]{4,3,2,1,0:T(8,128)(2,1)} %param.13) | copy-start | bytes 3145732
  4.6 22.0 %copy-start.7 = (bf16[2,8,16,16]{3,2,1,0:T(8,128)(2,1)S(1)}, bf16[2,8,16,16]{3,2,1,0:T(8,128)(2,1)}, u32[]{:S(2)}) copy-start(bf16[2,8,16,16]{3,2,1,0:T(8,128)(2,1)} %refs_2_.3) | copy-start | bytes 24580
  4.6 12.1 %collective-permute-start = (bf16[4,64,1024]{2,1,0:T(8,128)(2,1)}, bf16[4,64,1024]{2,1,0:T(8,128)(2,1)S(1)}, u32[]{:S(2)}, u32[]{:S(2)}) collective-permute-start(bf16[4,64,1024]{2,1,0:T(8,128)(2,1)} %get-tuple-element.30), channel_id=1, source_target_pairs={{1,0},{2,1},{3,2},{4,3},{5,4},{6,5},{7,6},{8,7},{9,8},{10,9},{11,1... | collective-permute-start | bytes 1572872 | tf_op jit(solution)/shard_map/ppermute | solution.py:426
  6.1 14.2 %collective-permute-start.1 = (bf16[4,64,1024]{2,1,0:T(8,128)(2,1)}, bf16[4,64,1024]{2,1,0:T(8,128)(2,1)S(1)}, u32[]{:S(2)}, u32[]{:S(2)}) collective-permute-start(bf16[4,64,1024]{2,1,0:T(8,128)(2,1)} %get-tuple-element.32), channel_id=1, source_target_pairs={{1,0},{2,1},{3,2},{4,3},{5,4},{6,5},{7,6},{8,7},{9,8},{10,9},{11,1... | collective-permute-start | bytes 1572872 | tf_op jit(solution)/shard_map/ppermute | solution.py:426
  11.8 14.7 %collective-permute-start.5 = (bf16[2,256,256]{2,1,0:T(8,128)(2,1)}, bf16[2,256,256]{2,1,0:T(8,128)(2,1)S(1)}, u32[]{:S(2)}, u32[]{:S(2)}) collective-permute-start(bf16[2,256,256]{2,1,0:T(8,128)(2,1)} %get-tuple-element.38), channel_id=1, source_target_pairs={{0,32},{32,0},{64,96},{96,64},{1,33},{33,1},{65,97},{97,65},{2,34}... | collective-permute-start | bytes 786440 | tf_op jit(solution)/shard_map/ppermute | solution.py:430
  13.1 10.7 %collective-permute-start.11 = (bf16[8,64,64]{2,1,0:T(8,128)(2,1)S(1)}, bf16[8,64,64]{2,1,0:T(8,128)(2,1)S(1)}, u32[]{:S(2)}, u32[]{:S(2)}) collective-permute-start(bf16[8,64,64]{2,1,0:T(8,128)(2,1)S(1)} %bitcast.24), channel_id=1, source_target_pairs={{1,0},{2,1},{3,2},{4,3},{5,4},{6,5},{7,6},{8,7},{9,8},{10,9},{11,1... | collective-permute-start | bytes 196616 | tf_op jit(solution)/shard_map/ppermute | solution.py:426
  14.1 15.4 %collective-permute-start.6 = (bf16[2,256,256]{2,1,0:T(8,128)(2,1)}, bf16[2,256,256]{2,1,0:T(8,128)(2,1)S(1)}, u32[]{:S(2)}, u32[]{:S(2)}) collective-permute-start(bf16[2,256,256]{2,1,0:T(8,128)(2,1)} %get-tuple-element.39), channel_id=1, source_target_pairs={{0,64},{32,96},{64,0},{96,32},{1,65},{33,97},{65,1},{97,33},{2,66}... | collective-permute-start | bytes 786440 | tf_op jit(solution)/shard_map/ppermute | solution.py:430
  16.7 14.2 %collective-permute-start.7 = (bf16[2,256,256]{2,1,0:T(8,128)(2,1)}, bf16[2,256,256]{2,1,0:T(8,128)(2,1)S(1)}, u32[]{:S(2)}, u32[]{:S(2)}) collective-permute-start(bf16[2,256,256]{2,1,0:T(8,128)(2,1)} %get-tuple-element.40), channel_id=1, source_target_pairs={{0,96},{32,64},{64,32},{96,0},{1,97},{33,65},{65,33},{97,1},{2,98}... | collective-permute-start | bytes 786440 | tf_op jit(solution)/shard_map/ppermute | solution.py:430
  20.2 13.1 %collective-permute-start.8 = (bf16[256,256]{1,0:T(8,128)(2,1)S(1)}, bf16[256,256]{1,0:T(8,128)(2,1)S(1)}, u32[]{:S(2)}, u32[]{:S(2)}) collective-permute-start(bf16[256,256]{1,0:T(8,128)(2,1)S(1)} %get-tuple-element.41), channel_id=1, source_target_pairs={{0,32},{32,0},{64,96},{96,64},{1,33},{33,1},{65,97},{97,65},{2,34}... | collective-permute-start | bytes 393224 | tf_op jit(solution)/shard_map/ppermute | solution.py:430
  23.8 9.6 %collective-permute-start.9 = (bf16[256,256]{1,0:T(8,128)(2,1)S(1)}, bf16[256,256]{1,0:T(8,128)(2,1)S(1)}, u32[]{:S(2)}, u32[]{:S(2)}) collective-permute-start(bf16[256,256]{1,0:T(8,128)(2,1)S(1)} %get-tuple-element.42), channel_id=1, source_target_pairs={{0,64},{32,96},{64,0},{96,32},{1,65},{33,97},{65,1},{97,33},{2,66}... | collective-permute-start | bytes 393224 | tf_op jit(solution)/shard_map/ppermute | solution.py:430
  26.5 9.4 %collective-permute-start.10 = (bf16[256,256]{1,0:T(8,128)(2,1)S(1)}, bf16[256,256]{1,0:T(8,128)(2,1)S(1)}, u32[]{:S(2)}, u32[]{:S(2)}) collective-permute-start(bf16[256,256]{1,0:T(8,128)(2,1)S(1)} %get-tuple-element.43), channel_id=1, source_target_pairs={{0,96},{32,64},{64,32},{96,0},{1,97},{33,65},{65,33},{97,1},{2,98}... | collective-permute-start | bytes 393224 | tf_op jit(solution)/shard_map/ppermute | solution.py:430
  26.5 9.4 %copy-start.4 = (bf16[1,8,64,1024]{3,2,1,0:T(8,128)(2,1)S(1)}, bf16[1,8,64,1024]{3,2,1,0:T(8,128)(2,1)}, u32[]{:S(2)}) copy-start(bf16[1,8,64,1024]{3,2,1,0:T(8,128)(2,1)} %param.9) | copy-start | bytes 3145732
  26.5 9.4 %copy-start.5 = (bf16[2,256,256]{2,1,0:T(8,128)(2,1)S(1)}, bf16[2,256,256]{2,1,0:T(8,128)(2,1)}, u32[]{:S(2)}) copy-start(bf16[2,256,256]{2,1,0:T(8,128)(2,1)} %get-tuple-element.37.refs_0_) | copy-start | bytes 786436
  26.6 9.4 %copy-start.8 = (bf16[1024,1024]{1,0:T(8,128)(2,1)S(1)}, bf16[1024,1024]{1,0:T(8,128)(2,1)}, u32[]{:S(2)}) copy-start(bf16[1024,1024]{1,0:T(8,128)(2,1)} %constant.2.clone.refs_8_.refs_4_) | copy-start | bytes 6291460
  29.4 22.5 %collective-permute-start.2 = (bf16[3,256,256]{2,1,0:T(8,128)(2,1)S(1)}, bf16[3,256,256]{2,1,0:T(8,128)(2,1)S(1)}, u32[]{:S(2)}, u32[]{:S(2)}) collective-permute-start(bf16[3,256,256]{2,1,0:T(8,128)(2,1)S(1)} %get-tuple-element.34), channel_id=1, source_target_pairs={{0,32},{32,0},{64,96},{96,64},{1,33},{33,1},{65,97},{97,65},{2,34}... | collective-permute-start | bytes 1179656 | tf_op jit(solution)/shard_map/ppermute | solution.py:430
  30.9 21.0 %collective-permute-start.3 = (bf16[3,256,256]{2,1,0:T(8,128)(2,1)S(1)}, bf16[3,256,256]{2,1,0:T(8,128)(2,1)S(1)}, u32[]{:S(2)}, u32[]{:S(2)}) collective-permute-start(bf16[3,256,256]{2,1,0:T(8,128)(2,1)S(1)} %get-tuple-element.35), channel_id=1, source_target_pairs={{0,64},{32,96},{64,0},{96,32},{1,65},{33,97},{65,1},{97,33},{2,66}... | collective-permute-start | bytes 1179656 | tf_op jit(solution)/shard_map/ppermute | solution.py:430
  33.4 18.6 %collective-permute-start.4 = (bf16[3,256,256]{2,1,0:T(8,128)(2,1)S(1)}, bf16[3,256,256]{2,1,0:T(8,128)(2,1)S(1)}, u32[]{:S(2)}, u32[]{:S(2)}) collective-permute-start(bf16[3,256,256]{2,1,0:T(8,128)(2,1)S(1)} %get-tuple-element.36), channel_id=1, source_target_pairs={{0,96},{32,64},{64,32},{96,0},{1,97},{33,65},{65,33},{97,1},{2,98}... | collective-permute-start | bytes 1179656 | tf_op jit(solution)/shard_map/ppermute | solution.py:430
  65.0 23.9 %collective-permute-start.12 = (bf16[2,64,1024]{2,1,0:T(8,128)(2,1)S(1)}, bf16[2,64,1024]{2,1,0:T(8,128)(2,1)S(1)}, u32[]{:S(2)}, u32[]{:S(2)}) collective-permute-start(bf16[2,64,1024]{2,1,0:T(8,128)(2,1)S(1)} %get-tuple-element.51), channel_id=1, source_target_pairs={{0,32},{32,0},{64,96},{96,64},{1,33},{33,1},{65,97},{97,65},{2,34}... | collective-permute-start | bytes 786440 | tf_op jit(solution)/shard_map/ppermute | solution.py:430
  65.1 23.8 %collective-permute-start.13 = (bf16[2,64,1024]{2,1,0:T(8,128)(2,1)S(1)}, bf16[2,64,1024]{2,1,0:T(8,128)(2,1)S(1)}, u32[]{:S(2)}, u32[]{:S(2)}) collective-permute-start(bf16[2,64,1024]{2,1,0:T(8,128)(2,1)S(1)} %get-tuple-element.52), channel_id=1, source_target_pairs={{0,64},{32,96},{64,0},{96,32},{1,65},{33,97},{65,1},{97,33},{2,66}... | collective-permute-start | bytes 786440 | tf_op jit(solution)/shard_map/ppermute | solution.py:430
  66.5 22.5 %collective-permute-start.14 = (bf16[2,64,1024]{2,1,0:T(8,128)(2,1)S(1)}, bf16[2,64,1024]{2,1,0:T(8,128)(2,1)S(1)}, u32[]{:S(2)}, u32[]{:S(2)}) collective-permute-start(bf16[2,64,1024]{2,1,0:T(8,128)(2,1)S(1)} %get-tuple-element.53), channel_id=1, source_target_pairs={{0,96},{32,64},{64,32},{96,0},{1,97},{33,65},{65,33},{97,1},{2,98}... | collective-permute-start | bytes 786440 | tf_op jit(solution)/shard_map/ppermute | solution.py:430

commit v4 on v3

--- a/solution.py
+++ b/solution.py
@@ -76,11 +76,21 @@
     return pl.CostEstimate(flops=1_000_000, bytes_accessed=mib << 20, transcendentals=0)
 
 
+ENV = PAD // 2
+
+
+def env_lanes(s, h):
+    return slice((h * SEC + s) * PAD, (h * SEC + s + 1) * PAD)
+
+
 def pack_kernel(k, rank_ref, p_ref, t_ref, after_ref, *refs):
     rights, raws = (), ()
     if k == 0:
-        q_ref, *refs = refs
-        outs, raws, (held, sems) = refs[:ROWS], refs[ROWS : ROWS + 2], refs[ROWS + 2 :]
+        q_ref, env_ref, *refs = refs
+        outs, raws = refs[:ROWS], refs[ROWS : ROWS + 2]
+        held, env, sems = refs[ROWS + 2 :]
+        bring = pltpu.make_async_copy(env_ref, env, sems.at[4, 0])
+        bring.start()
     else:
         *rights, outs, held, sems = refs[0], refs[1 : ROWS + 1], refs[ROWS + 1], refs[ROWS + 2]
     me = lax.axis_index("row")
@@ -95,7 +105,9 @@
             )
         )
     picks = [
-        pltpu.make_async_copy(q_ref.at[2 * (me ^ x) + j], raws[j].at[x], sems.at[2 + j, x])
+        pltpu.make_async_copy(
+            q_ref.at[2 * (me ^ x) + j], raws[j].at[pl.ds(x * PAD, PAD)], sems.at[2 + j, x]
+        )
         for j in range(len(raws))
         for x in range(ROWS)
     ]
@@ -111,21 +123,37 @@
             rows, lanes = slice(g * PAD, (g + 1) * PAD), slice(g * WIDE, (g + 1) * WIDE)
             outs[x][0, rows, :] = masked(held[x, :, lanes], inside)
             if k == 1:
-                outs[x][2, rows, :] = masked(rights[0][x, :, lanes], inside)
+                outs[x][2, rows, :] = masked(
+                    rights[0][x * PAD : (x + 1) * PAD, lanes], inside
+                )
     for x in range(ROWS):
         copies[x][1].wait()
+    if k == 0:
+        bring.wait()
+        for s in range(SEC):
+            for h in range(2):
+                raws[0][ROWS * PAD :, env_lanes(s, h)] = env[s, h * ENV : (h + 1) * ENV, :]
     for copy in picks:
         copy.wait()
 
 
 def pack(k, ranks, p, t, after, *rights):
-    raws = () if k else (jax.ShapeDtypeStruct((ROWS, PAD, SITE), BF16),) * 2
+    raws, env = (), []
+    if k == 0:
+        raws = tuple(
+            jax.ShapeDtypeStruct((ROWS * PAD + extra, SITE), BF16) for extra in (ENV, 0)
+        )
+        env = [pltpu.VMEM((SEC, PAD, PAD), BF16)]
     return pl.pallas_call(
         lambda *refs: pack_kernel(k, *refs),
         out_shape=(jax.ShapeDtypeStruct((2 + k, WIDE, WIDE), BF16),) * ROWS + raws,
-        in_specs=[smem()] + anywhere(3) + (vmem(1) if k else anywhere(1)),
+        in_specs=[smem()] + anywhere(3) + (vmem(1) if k else anywhere(2)),
         out_specs=tuple(vmem(ROWS + len(raws))),
-        scratch_shapes=[pltpu.VMEM((ROWS, PAD, SITE), BF16), pltpu.SemaphoreType.DMA((4, ROWS))],
+        scratch_shapes=[
+            pltpu.VMEM((ROWS, PAD, SITE), BF16),
+            *env,
+            pltpu.SemaphoreType.DMA((5, ROWS)),
+        ],
         compiler_params=params(8 if k else 56),
         cost_estimate=light(2),
         name="pack_second" if k else "pack_first",
@@ -139,7 +167,7 @@
         inside = at < rank_ref[0, 2 * (me ^ x)]
         for g in range(GROUPS):
             rows, lanes = slice(g * PAD, (g + 1) * PAD), slice(g * WIDE, (g + 1) * WIDE)
-            outs[x][rows, :] = masked(q_ref[x, :, lanes], inside)
+            outs[x][rows, :] = masked(q_ref[x * PAD : (x + 1) * PAD, lanes], inside)
 
 
 def mask_rights(ranks, after, q):
@@ -310,7 +338,9 @@
     for s in range(HALF):
         for g in range(GROUPS):
             at = slice(g * PAD, (g + 1) * PAD)
-            bde[s, at, at] = er_ref[first + s]
+            for h in range(2):
+                half = slice(g * PAD + h * ENV, g * PAD + (h + 1) * ENV)
+                bde[s, half, at] = er_ref[ROWS * PAD :, env_lanes(first + s, h)]
     uppers = [mm(el_ref[first + s], b_ref[s]).astype(BF16) for s in range(HALF)]
     for s in range(HALF):
         for g in range(4):
@@ -446,17 +476,17 @@
     lefts, transfers = proj_in[0, 0], row_transfer[0, 0]
     perm = bond_swap()
     lower = bottom_boundary[0, 0]
-    *packed, q1, q2 = pack(0, ranks, lefts, transfers, ranks, proj_out[0, 0])
+    *packed, q1, q2 = pack(0, ranks, lefts, transfers, ranks, proj_out[0, 0], envs)
     pts1 = exchanged_all(packed)
-    next1, next2, next_envs = following(q1), following(q2), following(envs)
+    next1, next2 = following(q1), following(q2)
     rights = mask_rights(ranks, ranks, next1)
     qs1 = exchanged_all(rights)
-    packed = pack(1, ranks, lefts, transfers, rights[0], next2)
+    low = observable_weights(0, lower, envs, next1, operators, rights[0])
+    packed = pack(1, ranks, lefts, transfers, low, next2)
     ptqs2 = exchanged_all(packed)
-    low = observable_weights(0, lower, envs, next_envs, operators, packed[0])
     top = top_boundary[0]
-    *us1, stats = chain(pts1, qs1, top, perm, None, (), low, 8, "chain_first")
-    high = observable_weights(HALF, lower, envs, next_envs, operators, stats)
+    *us1, stats = chain(pts1, qs1, top, perm, None, (), packed[0], 8, "chain_first")
+    high = observable_weights(HALF, lower, envs, next1, operators, stats)
     everyone = ROWS * columns
     *us, stats = chain(ptqs2, None, top, perm, stats, us1, high, everyone, "chain_second")
     us = exchanged_all(us)

time: 91.3 us -> 90.3 us (0.989)
  waiting for transfers between devices: 6.46 us -> 4 us
  starting transfers between devices: 22.9 us -> 24.1 us
    ppermute x3 -> x2, waiting for transfers between devices: 2.53 us -> 0.01 us  [passed_along(): return lax.ppermute(block, axis, route)]
    ppermute x12, starting transfers between devices: 14.7 us -> 16.9 us  [exchanged(): return lax.ppermute(block, 'row', [(i, i ^ x) for i in range(ROWS)])]
    ppermute x3 -> x2, starting transfers between devices: 8.2 us -> 7.25 us  [passed_along(): return lax.ppermute(block, axis, route)]
  transfers between devices with their start and end apart: 15 -> 14, of which waited for: 3 -> 3; matrix products, arithmetic and copies ran while one was open for 0% -> 0% of each run, Pallas kernels for 24% -> 24%
where the time goes in v4:
time: 90.3 us; the launch traced here: 90.2 us
  Pallas kernels  40.7 us (45%)
  starting transfers between devices  24.1 us (27%)
  blocking collectives  20.4 us (23%)
  waiting for transfers between devices  4 us (4%)
    pallas_call x2, Pallas kernels, chain(): pl.pallas_call(body, out_shape=(site,) * ROWS + (jax.ShapeDtypeStruct((co...  25.9 us
    all_to_all x1, blocking collectives, on_device(): gathered = lax.all_to_all(stats, ('row', 'col'), 0, 0, tiled=True)  20.4 us
    ppermute x12, starting transfers between devices, exchanged(): return lax.ppermute(block, 'row', [(i, i ^ x) for i in range(ROWS)])  16.9 us
    ppermute x2, starting transfers between devices, passed_along(): return lax.ppermute(block, axis, route)  7.25 us
    pallas_call x2, Pallas kernels, pack(): pl.pallas_call(lambda *refs: pack_kernel(k, *refs), out_shape=(jax.ShapeD...  6.25 us
    pallas_call x2, Pallas kernels, observable_weights(): pl.pallas_call(lambda *refs: weight_kernel(first, *refs), out_shape=jax.S...  5.73 us
    ppermute x12, waiting for transfers between devices, exchanged(): return lax.ppermute(block, 'row', [(i, i ^ x) for i in range(ROWS)])  4 us
    pallas_call x1, Pallas kernels, finish(): pl.pallas_call(lambda *refs: finish_kernel(entries, *refs), out_shape=(ja...  2.21 us
  transfers between devices with their start and end apart: 14, of which 3 were waited for; matrix products, arithmetic and copies ran while one was open for 0% of the time, Pallas kernels for 24%

profile of v4, /device:TPU:1, one launch (start us, length us, event | category | flops | bytes accessed | tf_op | source)
XLA Modules:
  0.0 90.2 jit_solution(17490221251237277875)
XLA Ops:
  0.7 4.0 %pack_first.1 = (bf16[2,256,256]{2,1,0:T(8,128)(2,1)}, bf16[2,256,256]{2,1,0:T(8,128)(2,1)}, bf16[2,256,256]{2,1,0:T(8,128)(2,1)}, bf16[2,256,256]{2,1,0:T(8,128...) custom-call(s32[1,8]{1,0:T(1,128)} %refs_0_.3, bf16[8,64,1024]{2,1,0:T(8,128)(2,1)} %bitcast.14, ...), custom_call_target="tpu_custom_call" | custom-call | flops 1000000 | bytes 2097152 | tf_op jit(solution)/shard_map/pack_first/pallas_call | solution.py:147
  4.6 1.5 %collective-permute-start = (bf16[288,1024]{1,0:T(8,128)(2,1)}, bf16[288,1024]{1,0:T(8,128)(2,1)S(1)}, u32[]{:S(2)}, u32[]{:S(2)}) collective-permute-start(bf16[288,1024]{1,0:T(8,128)(2,1)} %get-tuple-element.30), channel_id=1, source_target_pairs={{1,0},{2,1},{3,2},{4,3},{5,4},{6,5},{7,6},{8,7},{9,8},{10,9},{11,1... | collective-permute-start | bytes 1769480 | tf_op jit(solution)/shard_map/ppermute | solution.py:456
  6.1 5.8 %collective-permute-start.1 = (bf16[256,1024]{1,0:T(8,128)(2,1)}, bf16[256,1024]{1,0:T(8,128)(2,1)S(1)}, u32[]{:S(2)}, u32[]{:S(2)}) collective-permute-start(bf16[256,1024]{1,0:T(8,128)(2,1)} %get-tuple-element.32), channel_id=1, source_target_pairs={{1,0},{2,1},{3,2},{4,3},{5,4},{6,5},{7,6},{8,7},{9,8},{10,9},{11,1... | collective-permute-start | bytes 1572872 | tf_op jit(solution)/shard_map/ppermute | solution.py:456
  11.9 1.3 %collective-permute-start.5 = (bf16[2,256,256]{2,1,0:T(8,128)(2,1)}, bf16[2,256,256]{2,1,0:T(8,128)(2,1)S(1)}, u32[]{:S(2)}, u32[]{:S(2)}) collective-permute-start(bf16[2,256,256]{2,1,0:T(8,128)(2,1)} %get-tuple-element.38), channel_id=1, source_target_pairs={{0,32},{32,0},{64,96},{96,64},{1,33},{33,1},{65,97},{97,65},{2,34}... | collective-permute-start | bytes 786440 | tf_op jit(solution)/shard_map/ppermute | solution.py:460
  13.2 2.6 %collective-permute-start.6 = (bf16[2,256,256]{2,1,0:T(8,128)(2,1)}, bf16[2,256,256]{2,1,0:T(8,128)(2,1)S(1)}, u32[]{:S(2)}, u32[]{:S(2)}) collective-permute-start(bf16[2,256,256]{2,1,0:T(8,128)(2,1)} %get-tuple-element.39), channel_id=1, source_target_pairs={{0,64},{32,96},{64,0},{96,32},{1,65},{33,97},{65,1},{97,33},{2,66}... | collective-permute-start | bytes 786440 | tf_op jit(solution)/shard_map/ppermute | solution.py:460
  15.8 0.6 mask_rights.1
  16.5 0.7 collective-permute-start.8
  17.1 2.1 %collective-permute-done.5.refs_1_ = bf16[2,256,256]{2,1,0:T(8,128)(2,1)S(1)} collective-permute-done((bf16[2,256,256]{2,1,0:T(8,128)(2,1)}, bf16[2,256,256]{2,1,0:T(8,128)(2,1)S(1)}, u32[]{:S(2)}, u32[]{:S(2)}) %collective-permute-start.5) | collective-permute-done | bytes 262176 | tf_op jit(solution)/shard_map/ppermute | solution.py:460
  19.3 2.9 %collective-permute-start.9 = (bf16[256,256]{1,0:T(8,128)(2,1)S(1)}, bf16[256,256]{1,0:T(8,128)(2,1)S(1)}, u32[]{:S(2)}, u32[]{:S(2)}) collective-permute-start(bf16[256,256]{1,0:T(8,128)(2,1)S(1)} %get-tuple-element.42), channel_id=1, source_target_pairs={{0,64},{32,96},{64,0},{96,32},{1,65},{33,97},{65,1},{97,33},{2,66}... | collective-permute-start | bytes 393224 | tf_op jit(solution)/shard_map/ppermute | solution.py:460
  22.2 1.5 %collective-permute-start.10 = (bf16[256,256]{1,0:T(8,128)(2,1)S(1)}, bf16[256,256]{1,0:T(8,128)(2,1)S(1)}, u32[]{:S(2)}, u32[]{:S(2)}) collective-permute-start(bf16[256,256]{1,0:T(8,128)(2,1)S(1)} %get-tuple-element.43), channel_id=1, source_target_pairs={{0,96},{32,64},{64,32},{96,0},{1,97},{33,65},{65,33},{97,1},{2,98}... | collective-permute-start | bytes 393224 | tf_op jit(solution)/shard_map/ppermute | solution.py:460
  23.8 2.9 %observable_weights.2.refs_3_.refs_5_ = bf16[2,4,64,1024]{3,2,1,0:T(8,128)(2,1)S(1)} custom-call(bf16[8,64,64]{2,1,0:T(8,128)(2,1)S(1)} %bitcast.20, bf16[288,1024]{1,0:T(8,128)(2,1)S(1)} %collective-permute-done.q_ref.refs_1_, bf16[2,8,16,16]{3,2,1,0:T(8,128)(2,1)S(1)} %copy-done.7, bf16[256,256]{1,0:T(8,128)(2,1)S(1)} %get-tuple-element.31.refs_3_.refs_4_, ...), custom_call_target="tpu_custom_call" | custom-call | flops 3000000000 | bytes 2097152 | tf_op jit(solution)/shard_map/observable_weights/pallas_call | solution.py:368
  26.7 2.3 %pack_second.1 = (bf16[3,256,256]{2,1,0:T(8,128)(2,1)S(1)}, bf16[3,256,256]{2,1,0:T(8,128)(2,1)S(1)}, bf16[3,256,256]{2,1,0:T(8,128)(2,1)S(1)}, bf16[3,256,256]{2,1,0:T(8,128)(2,1)S(1)}) custom-call(s32[1,8]{1,0:T(1,128)S(1)} %copy-done.3, bf16[8,64,1024]{2,1,0:T(8,128)(2,1)S(1)} %bitcast.15, bf16[8,256,256]{2,1,0:T(8,128)(2,1)S(1)} %bitcast.17, ...), custom_call_target="tpu_custom_call" | custom-call | flops 1000000 | bytes 2097152 | tf_op jit(solution)/shard_map/pack_second/pallas_call | solution.py:147
  29.0 0.1 collective-permute-start.2
  29.1 2.3 %collective-permute-start.3 = (bf16[3,256,256]{2,1,0:T(8,128)(2,1)S(1)}, bf16[3,256,256]{2,1,0:T(8,128)(2,1)S(1)}, u32[]{:S(2)}, u32[]{:S(2)}) collective-permute-start(bf16[3,256,256]{2,1,0:T(8,128)(2,1)S(1)} %get-tuple-element.35), channel_id=1, source_target_pairs={{0,64},{32,96},{64,0},{96,32},{1,65},{33,97},{65,1},{97,33},{2,66}... | collective-permute-start | bytes 1179656 | tf_op jit(solution)/shard_map/ppermute | solution.py:460
  31.4 1.5 %collective-permute-start.4 = (bf16[3,256,256]{2,1,0:T(8,128)(2,1)S(1)}, bf16[3,256,256]{2,1,0:T(8,128)(2,1)S(1)}, u32[]{:S(2)}, u32[]{:S(2)}) collective-permute-start(bf16[3,256,256]{2,1,0:T(8,128)(2,1)S(1)} %get-tuple-element.36), channel_id=1, source_target_pairs={{0,96},{32,64},{64,32},{96,0},{1,97},{33,65},{65,33},{97,1},{2,98}... | collective-permute-start | bytes 1179656 | tf_op jit(solution)/shard_map/ppermute | solution.py:460
  33.0 1.7 %collective-permute-done.10.refs_7_ = bf16[256,256]{1,0:T(8,128)(2,1)S(1)} collective-permute-done((bf16[256,256]{1,0:T(8,128)(2,1)S(1)}, bf16[256,256]{1,0:T(8,128)(2,1)S(1)}, u32[]{:S(2)}, u32[]{:S(2)}) %collective-permute-start.10) | collective-permute-done | bytes 131104 | tf_op jit(solution)/shard_map/ppermute | solution.py:460
  34.7 12.9 %chain_first.1 = (bf16[1,64,1024]{2,1,0:T(8,128)(2,1)S(1)}, bf16[1,64,1024]{2,1,0:T(8,128)(2,1)S(1)}, bf16[1,64,1024]{2,1,0:T(8,128)(2,1)S(1)}, bf16[1,64,1024]{2,1,0:T(8,128)(2,1)S(1)}, f32[8,128]{1,0:T(8,128)S(1)}) custom-call(bf16[2,256,256]{2,1,0:T(8,128)(2,1)S(1)} %copy-done.6, bf16[2,256,256]{2,1,0:T(8,128)(2,1)S(1)} %collective-permute-done.5.refs_1_, ...), custom_call_target="tpu_custom_call" | custom-call | flops 12000000000 | bytes 4194304 | tf_op jit(solution)/shard_map/chain_first/pallas_call | solution.py:293
  47.7 2.9 %observable_weights.3.refs_10_.refs_6_ = bf16[2,4,64,1024]{3,2,1,0:T(8,128)(2,1)S(1)} custom-call(bf16[8,64,64]{2,1,0:T(8,128)(2,1)S(1)} %bitcast.21, bf16[288,1024]{1,0:T(8,128)(2,1)S(1)} %collective-permute-done.q_ref.refs_1_, bf16[2,8,16,16]{3,2,1,0:T(8,128)(2,1)S(1)} %copy-done.7, f32[8,128]{1,0:T(8,128)S(1)} %get-tuple-element.44.refs_3_.refs_5_, ...), custom_call_target="tpu_custom_call" | custom-call | flops 3000000000 | bytes 2097152 | tf_op jit(solution)/shard_map/observable_weights/pallas_call | solution.py:368
  50.6 13.0 %chain_second.1 = (bf16[2,64,1024]{2,1,0:T(8,128)(2,1)S(1)}, bf16[2,64,1024]{2,1,0:T(8,128)(2,1)S(1)}, bf16[2,64,1024]{2,1,0:T(8,128)(2,1)S(1)}, bf16[2,64,1024]{2,1,0:T(8,128)(2,1)S(1)}, f32[128,128]{1,0:T(8,128)S(1)}) custom-call(bf16[3,256,256]{2,1,0:T(8,128)(2,1)S(1)} %get-tuple-element.33.refs_9_.refs_0_, ...), custom_call_target="tpu_custom_call" | custom-call | flops 12000000000 | bytes 4194304 | tf_op jit(solution)/shard_map/chain_second/pallas_call | solution.py:293
  63.6 0.1 collective-permute-start.11
  63.7 1.6 %collective-permute-start.12 = (bf16[2,64,1024]{2,1,0:T(8,128)(2,1)S(1)}, bf16[2,64,1024]{2,1,0:T(8,128)(2,1)S(1)}, u32[]{:S(2)}, u32[]{:S(2)}) collective-permute-start(bf16[2,64,1024]{2,1,0:T(8,128)(2,1)S(1)} %get-tuple-element.52), channel_id=1, source_target_pairs={{0,64},{32,96},{64,0},{96,32},{1,65},{33,97},{65,1},{97,33},{2,66}... | collective-permute-start | bytes 786440 | tf_op jit(solution)/shard_map/ppermute | solution.py:460
  65.2 2.3 %collective-permute-start.13 = (bf16[2,64,1024]{2,1,0:T(8,128)(2,1)S(1)}, bf16[2,64,1024]{2,1,0:T(8,128)(2,1)S(1)}, u32[]{:S(2)}, u32[]{:S(2)}) collective-permute-start(bf16[2,64,1024]{2,1,0:T(8,128)(2,1)S(1)} %get-tuple-element.53), channel_id=1, source_target_pairs={{0,96},{32,64},{64,32},{96,0},{1,97},{33,65},{65,33},{97,1},{2,98}... | collective-permute-start | bytes 786440 | tf_op jit(solution)/shard_map/ppermute | solution.py:460
  67.5 20.4 %all_to_all.11 = f32[128,1,128]{2,1,0:T(1,128)S(1)} all-to-all(f32[128,1,128]{2,1,0:T(1,128)S(1)} %bitcast.22), channel_id=1, replica_groups=mesh['row'=4,'col'=32] {'row','col'}, dimensions={0} | all-to-all | bytes 131072 | tf_op jit(solution)/shard_map/all_to_all | solution.py:493
  88.0 2.2 %finish.1 = (bf16[8,64,1024]{2,1,0:T(8,128)(2,1)}, f32[1,8]{1,0:T(1,128)}, f32[2,8]{1,0:T(2,128)}) custom-call(f32[128,128]{1,0:T(8,128)S(1)} %bitcast.18, bf16[2,64,1024]{2,1,0:T(8,128)(2,1)S(1)} %get-tuple-element.50.refs_1_, bf16[2,64,1024]{2,1,0:T(8,128)(2,1)S(1)} %collective-permute-done.11.refs_2_, ...), custom_call_target="tpu_custom_call" | custom-call | flops 2000000 | bytes 2097152 | tf_op jit(solution)/shard_map/finish/pallas_call | solution.py:434
  (31 shorter events, 0.2 us)
Async XLA Ops:
  0.6 15.2 %copy-start.3 = (s32[1,8]{1,0:T(1,128)S(1)}, s32[1,8]{1,0:T(1,128)}, u32[]{:S(2)}) copy-start(s32[1,8]{1,0:T(1,128)} %refs_0_.3) | copy-start | bytes 100
  0.6 23.1 %copy-start.2 = (bf16[1,1,8,64,64]{4,3,2,1,0:T(8,128)(2,1)S(1)}, bf16[1,1,8,64,64]{4,3,2,1,0:T(8,128)(2,1)}, u32[]{:S(2)}) copy-start(bf16[1,1,8,64,64]{4,3,2,1,0:T(8,128)(2,1)} %param.14) | copy-start | bytes 196612
  0.7 23.1 %copy-start.7 = (bf16[2,8,16,16]{3,2,1,0:T(8,128)(2,1)S(1)}, bf16[2,8,16,16]{3,2,1,0:T(8,128)(2,1)}, u32[]{:S(2)}) copy-start(bf16[2,8,16,16]{3,2,1,0:T(8,128)(2,1)} %refs_2_.3) | copy-start | bytes 24580
  0.7 23.1 %copy-start.4 = (bf16[1,1,8,64,1024]{4,3,2,1,0:T(8,128)(2,1)S(1)}, bf16[1,1,8,64,1024]{4,3,2,1,0:T(8,128)(2,1)}, u32[]{:S(2)}) copy-start(bf16[1,1,8,64,1024]{4,3,2,1,0:T(8,128)(2,1)} %param.13) | copy-start | bytes 3145732
  4.6 11.2 %collective-permute-start = (bf16[288,1024]{1,0:T(8,128)(2,1)}, bf16[288,1024]{1,0:T(8,128)(2,1)S(1)}, u32[]{:S(2)}, u32[]{:S(2)}) collective-permute-start(bf16[288,1024]{1,0:T(8,128)(2,1)} %get-tuple-element.30), channel_id=1, source_target_pairs={{1,0},{2,1},{3,2},{4,3},{5,4},{6,5},{7,6},{8,7},{9,8},{10,9},{11,1... | collective-permute-start | bytes 1769480 | tf_op jit(solution)/shard_map/ppermute | solution.py:456
  6.1 16.1 %collective-permute-start.1 = (bf16[256,1024]{1,0:T(8,128)(2,1)}, bf16[256,1024]{1,0:T(8,128)(2,1)S(1)}, u32[]{:S(2)}, u32[]{:S(2)}) collective-permute-start(bf16[256,1024]{1,0:T(8,128)(2,1)} %get-tuple-element.32), channel_id=1, source_target_pairs={{1,0},{2,1},{3,2},{4,3},{5,4},{6,5},{7,6},{8,7},{9,8},{10,9},{11,1... | collective-permute-start | bytes 1572872 | tf_op jit(solution)/shard_map/ppermute | solution.py:456
  11.9 7.4 %collective-permute-start.5 = (bf16[2,256,256]{2,1,0:T(8,128)(2,1)}, bf16[2,256,256]{2,1,0:T(8,128)(2,1)S(1)}, u32[]{:S(2)}, u32[]{:S(2)}) collective-permute-start(bf16[2,256,256]{2,1,0:T(8,128)(2,1)} %get-tuple-element.38), channel_id=1, source_target_pairs={{0,32},{32,0},{64,96},{96,64},{1,33},{33,1},{65,97},{97,65},{2,34}... | collective-permute-start | bytes 786440 | tf_op jit(solution)/shard_map/ppermute | solution.py:460
  13.2 15.8 %collective-permute-start.6 = (bf16[2,256,256]{2,1,0:T(8,128)(2,1)}, bf16[2,256,256]{2,1,0:T(8,128)(2,1)S(1)}, u32[]{:S(2)}, u32[]{:S(2)}) collective-permute-start(bf16[2,256,256]{2,1,0:T(8,128)(2,1)} %get-tuple-element.39), channel_id=1, source_target_pairs={{0,64},{32,96},{64,0},{96,32},{1,65},{33,97},{65,1},{97,33},{2,66}... | collective-permute-start | bytes 786440 | tf_op jit(solution)/shard_map/ppermute | solution.py:460
  15.8 13.3 %collective-permute-start.7 = (bf16[2,256,256]{2,1,0:T(8,128)(2,1)}, bf16[2,256,256]{2,1,0:T(8,128)(2,1)S(1)}, u32[]{:S(2)}, u32[]{:S(2)}) collective-permute-start(bf16[2,256,256]{2,1,0:T(8,128)(2,1)} %get-tuple-element.40), channel_id=1, source_target_pairs={{0,96},{32,64},{64,32},{96,0},{1,97},{33,65},{65,33},{97,1},{2,98}... | collective-permute-start | bytes 786440 | tf_op jit(solution)/shard_map/ppermute | solution.py:460
  16.5 14.9 %collective-permute-start.8 = (bf16[256,256]{1,0:T(8,128)(2,1)S(1)}, bf16[256,256]{1,0:T(8,128)(2,1)S(1)}, u32[]{:S(2)}, u32[]{:S(2)}) collective-permute-start(bf16[256,256]{1,0:T(8,128)(2,1)S(1)} %get-tuple-element.41), channel_id=1, source_target_pairs={{0,32},{32,0},{64,96},{96,64},{1,33},{33,1},{65,97},{97,65},{2,34}... | collective-permute-start | bytes 393224 | tf_op jit(solution)/shard_map/ppermute | solution.py:460
  19.3 13.7 %collective-permute-start.9 = (bf16[256,256]{1,0:T(8,128)(2,1)S(1)}, bf16[256,256]{1,0:T(8,128)(2,1)S(1)}, u32[]{:S(2)}, u32[]{:S(2)}) collective-permute-start(bf16[256,256]{1,0:T(8,128)(2,1)S(1)} %get-tuple-element.42), channel_id=1, source_target_pairs={{0,64},{32,96},{64,0},{96,32},{1,65},{33,97},{65,1},{97,33},{2,66}... | collective-permute-start | bytes 393224 | tf_op jit(solution)/shard_map/ppermute | solution.py:460
  22.2 12.5 %collective-permute-start.10 = (bf16[256,256]{1,0:T(8,128)(2,1)S(1)}, bf16[256,256]{1,0:T(8,128)(2,1)S(1)}, u32[]{:S(2)}, u32[]{:S(2)}) collective-permute-start(bf16[256,256]{1,0:T(8,128)(2,1)S(1)} %get-tuple-element.43), channel_id=1, source_target_pairs={{0,96},{32,64},{64,32},{96,0},{1,97},{33,65},{65,33},{97,1},{2,98}... | collective-permute-start | bytes 393224 | tf_op jit(solution)/shard_map/ppermute | solution.py:460
  23.7 2.9 %copy-start = (bf16[1,1,8,64,1024]{4,3,2,1,0:T(8,128)(2,1)S(1)}, bf16[1,1,8,64,1024]{4,3,2,1,0:T(8,128)(2,1)}, u32[]{:S(2)}) copy-start(bf16[1,1,8,64,1024]{4,3,2,1,0:T(8,128)(2,1)} %param.11) | copy-start | bytes 3145732
  23.8 2.9 %copy-start.1 = (bf16[1,1,8,256,256]{4,3,2,1,0:T(8,128)(2,1)S(1)}, bf16[1,1,8,256,256]{4,3,2,1,0:T(8,128)(2,1)}, u32[]{:S(2)}) copy-start(bf16[1,1,8,256,256]{4,3,2,1,0:T(8,128)(2,1)} %param.10) | copy-start | bytes 3145732
  26.7 8.1 %copy-start.5 = (bf16[1,8,64,1024]{3,2,1,0:T(8,128)(2,1)S(1)}, bf16[1,8,64,1024]{3,2,1,0:T(8,128)(2,1)}, u32[]{:S(2)}) copy-start(bf16[1,8,64,1024]{3,2,1,0:T(8,128)(2,1)} %param.9) | copy-start | bytes 3145732
  26.7 8.1 %copy-start.6 = (bf16[2,256,256]{2,1,0:T(8,128)(2,1)S(1)}, bf16[2,256,256]{2,1,0:T(8,128)(2,1)}, u32[]{:S(2)}) copy-start(bf16[2,256,256]{2,1,0:T(8,128)(2,1)} %get-tuple-element.37.refs_0_) | copy-start | bytes 786436
  26.7 8.1 %copy-start.8 = (bf16[1024,1024]{1,0:T(8,128)(2,1)S(1)}, bf16[1024,1024]{1,0:T(8,128)(2,1)}, u32[]{:S(2)}) copy-start(bf16[1024,1024]{1,0:T(8,128)(2,1)} %constant.2.clone.refs_8_.refs_4_) | copy-start | bytes 6291460
  29.0 21.6 %collective-permute-start.2 = (bf16[3,256,256]{2,1,0:T(8,128)(2,1)S(1)}, bf16[3,256,256]{2,1,0:T(8,128)(2,1)S(1)}, u32[]{:S(2)}, u32[]{:S(2)}) collective-permute-start(bf16[3,256,256]{2,1,0:T(8,128)(2,1)S(1)} %get-tuple-element.34), channel_id=1, source_target_pairs={{0,32},{32,0},{64,96},{96,64},{1,33},{33,1},{65,97},{97,65},{2,34}... | collective-permute-start | bytes 1179656 | tf_op jit(solution)/shard_map/ppermute | solution.py:460
  29.1 21.5 %collective-permute-start.3 = (bf16[3,256,256]{2,1,0:T(8,128)(2,1)S(1)}, bf16[3,256,256]{2,1,0:T(8,128)(2,1)S(1)}, u32[]{:S(2)}, u32[]{:S(2)}) collective-permute-start(bf16[3,256,256]{2,1,0:T(8,128)(2,1)S(1)} %get-tuple-element.35), channel_id=1, source_target_pairs={{0,64},{32,96},{64,0},{96,32},{1,65},{33,97},{65,1},{97,33},{2,66}... | collective-permute-start | bytes 1179656 | tf_op jit(solution)/shard_map/ppermute | solution.py:460
  31.4 19.2 %collective-permute-start.4 = (bf16[3,256,256]{2,1,0:T(8,128)(2,1)S(1)}, bf16[3,256,256]{2,1,0:T(8,128)(2,1)S(1)}, u32[]{:S(2)}, u32[]{:S(2)}) collective-permute-start(bf16[3,256,256]{2,1,0:T(8,128)(2,1)S(1)} %get-tuple-element.36), channel_id=1, source_target_pairs={{0,96},{32,64},{64,32},{96,0},{1,97},{33,65},{65,33},{97,1},{2,98}... | collective-permute-start | bytes 1179656 | tf_op jit(solution)/shard_map/ppermute | solution.py:460
  63.6 24.4 %collective-permute-start.11 = (bf16[2,64,1024]{2,1,0:T(8,128)(2,1)S(1)}, bf16[2,64,1024]{2,1,0:T(8,128)(2,1)S(1)}, u32[]{:S(2)}, u32[]{:S(2)}) collective-permute-start(bf16[2,64,1024]{2,1,0:T(8,128)(2,1)S(1)} %get-tuple-element.51), channel_id=1, source_target_pairs={{0,32},{32,0},{64,96},{96,64},{1,33},{33,1},{65,97},{97,65},{2,34}... | collective-permute-start | bytes 786440 | tf_op jit(solution)/shard_map/ppermute | solution.py:460
  63.7 24.3 %collective-permute-start.12 = (bf16[2,64,1024]{2,1,0:T(8,128)(2,1)S(1)}, bf16[2,64,1024]{2,1,0:T(8,128)(2,1)S(1)}, u32[]{:S(2)}, u32[]{:S(2)}) collective-permute-start(bf16[2,64,1024]{2,1,0:T(8,128)(2,1)S(1)} %get-tuple-element.52), channel_id=1, source_target_pairs={{0,64},{32,96},{64,0},{96,32},{1,65},{33,97},{65,1},{97,33},{2,66}... | collective-permute-start | bytes 786440 | tf_op jit(solution)/shard_map/ppermute | solution.py:460
  65.2 22.7 %collective-permute-start.13 = (bf16[2,64,1024]{2,1,0:T(8,128)(2,1)S(1)}, bf16[2,64,1024]{2,1,0:T(8,128)(2,1)S(1)}, u32[]{:S(2)}, u32[]{:S(2)}) collective-permute-start(bf16[2,64,1024]{2,1,0:T(8,128)(2,1)S(1)} %get-tuple-element.53), channel_id=1, source_target_pairs={{0,96},{32,64},{64,32},{96,0},{1,97},{33,65},{65,33},{97,1},{2,98}... | collective-permute-start | bytes 786440 | tf_op jit(solution)/shard_map/ppermute | solution.py:460

commit v5 on v4

--- a/solution.py
+++ b/solution.py
@@ -230,7 +230,7 @@
                         bdm[k, g * PAD + h * 16 : g * PAD + (h + 1) * 16, at] = place[
                             k * 16 : (k + 1) * 16, h * PAD : (h + 1) * PAD
                         ]
-                bdq[r % 2, at, k * WIDE + g * PAD : k * WIDE + (g + 1) * PAD] = right
+                bdq[at, k * WIDE + g * PAD : k * WIDE + (g + 1) * PAD] = right
             first = mm(left, bdm[k]).astype(BF16)
             xs[:, k * 16 : (k + 1) * 16, :] = first.reshape(16, 16, WIDE)
         for c in range(16):
@@ -244,8 +244,8 @@
                     ]
 
         @pl.when(me >= 0)
-        def _(r=r):
-            zs[...] = mmt(ys[...], bdq[r % 2])
+        def _():
+            zs[...] = mmt(ys[...], bdq[...])
 
         z = zs[...]
         if inverse is not None:
@@ -297,7 +297,7 @@
         out_specs=tuple(vmem(ROWS + 1)),
         scratch_shapes=[
             pltpu.VMEM((KM, WIDE, WIDE), BF16),
-            pltpu.VMEM((2, WIDE, DB * WIDE), BF16),
+            pltpu.VMEM((WIDE, DB * WIDE), BF16),
             pltpu.VMEM((16, WIDE, WIDE), BF16),
             pltpu.VMEM((WIDE, DB * WIDE), BF16),
             pltpu.VMEM((ROWS * PAD, SITE), BF16),

time: 90.3 us -> 90.2 us (level)
  no operation moved by 1% of the time
where the time goes in v5:
time: 90.2 us; the launch traced here: 90 us
  Pallas kernels  40.4 us (45%)
  starting transfers between devices  24.1 us (27%)
  blocking collectives  20.6 us (23%)
  waiting for transfers between devices  4 us (4%)
    pallas_call x2, Pallas kernels, chain(): pl.pallas_call(body, out_shape=(site,) * ROWS + (jax.ShapeDtypeStruct((co...  25.6 us
    all_to_all x1, blocking collectives, on_device(): gathered = lax.all_to_all(stats, ('row', 'col'), 0, 0, tiled=True)  20.6 us
    ppermute x12, starting transfers between devices, exchanged(): return lax.ppermute(block, 'row', [(i, i ^ x) for i in range(ROWS)])  16.9 us
    ppermute x2, starting transfers between devices, passed_along(): return lax.ppermute(block, axis, route)  7.25 us
    pallas_call x2, Pallas kernels, pack(): pl.pallas_call(lambda *refs: pack_kernel(k, *refs), out_shape=(jax.ShapeD...  6.25 us
    pallas_call x2, Pallas kernels, observable_weights(): pl.pallas_call(lambda *refs: weight_kernel(first, *refs), out_shape=jax.S...  5.73 us
    ppermute x12, waiting for transfers between devices, exchanged(): return lax.ppermute(block, 'row', [(i, i ^ x) for i in range(ROWS)])  4 us
    pallas_call x1, Pallas kernels, finish(): pl.pallas_call(lambda *refs: finish_kernel(entries, *refs), out_shape=(ja...  2.21 us
  transfers between devices with their start and end apart: 14, of which 3 were waited for; matrix products, arithmetic and copies ran while one was open for 0% of the time, Pallas kernels for 24%

profile of v5, /device:TPU:1, one launch (start us, length us, event | category | flops | bytes accessed | tf_op | source)
XLA Modules:
  0.0 90.0 jit_solution(18159174744823141258)
XLA Ops:
  0.7 4.0 %pack_first.1 = (bf16[2,256,256]{2,1,0:T(8,128)(2,1)}, bf16[2,256,256]{2,1,0:T(8,128)(2,1)}, bf16[2,256,256]{2,1,0:T(8,128)(2,1)}, bf16[2,256,256]{2,1,0:T(8,128...) custom-call(s32[1,8]{1,0:T(1,128)} %refs_0_.3, bf16[8,64,1024]{2,1,0:T(8,128)(2,1)} %bitcast.14, ...), custom_call_target="tpu_custom_call" | custom-call | flops 1000000 | bytes 2097152 | tf_op jit(solution)/shard_map/pack_first/pallas_call | solution.py:147
  4.6 1.5 %collective-permute-start = (bf16[288,1024]{1,0:T(8,128)(2,1)}, bf16[288,1024]{1,0:T(8,128)(2,1)S(1)}, u32[]{:S(2)}, u32[]{:S(2)}) collective-permute-start(bf16[288,1024]{1,0:T(8,128)(2,1)} %get-tuple-element.30), channel_id=1, source_target_pairs={{1,0},{2,1},{3,2},{4,3},{5,4},{6,5},{7,6},{8,7},{9,8},{10,9},{11,1... | collective-permute-start | bytes 1769480 | tf_op jit(solution)/shard_map/ppermute | solution.py:456
  6.1 5.8 %collective-permute-start.1 = (bf16[256,1024]{1,0:T(8,128)(2,1)}, bf16[256,1024]{1,0:T(8,128)(2,1)S(1)}, u32[]{:S(2)}, u32[]{:S(2)}) collective-permute-start(bf16[256,1024]{1,0:T(8,128)(2,1)} %get-tuple-element.32), channel_id=1, source_target_pairs={{1,0},{2,1},{3,2},{4,3},{5,4},{6,5},{7,6},{8,7},{9,8},{10,9},{11,1... | collective-permute-start | bytes 1572872 | tf_op jit(solution)/shard_map/ppermute | solution.py:456
  11.9 1.3 %collective-permute-start.5 = (bf16[2,256,256]{2,1,0:T(8,128)(2,1)}, bf16[2,256,256]{2,1,0:T(8,128)(2,1)S(1)}, u32[]{:S(2)}, u32[]{:S(2)}) collective-permute-start(bf16[2,256,256]{2,1,0:T(8,128)(2,1)} %get-tuple-element.38), channel_id=1, source_target_pairs={{0,32},{32,0},{64,96},{96,64},{1,33},{33,1},{65,97},{97,65},{2,34}... | collective-permute-start | bytes 786440 | tf_op jit(solution)/shard_map/ppermute | solution.py:460
  13.2 2.6 %collective-permute-start.6 = (bf16[2,256,256]{2,1,0:T(8,128)(2,1)}, bf16[2,256,256]{2,1,0:T(8,128)(2,1)S(1)}, u32[]{:S(2)}, u32[]{:S(2)}) collective-permute-start(bf16[2,256,256]{2,1,0:T(8,128)(2,1)} %get-tuple-element.39), channel_id=1, source_target_pairs={{0,64},{32,96},{64,0},{96,32},{1,65},{33,97},{65,1},{97,33},{2,66}... | collective-permute-start | bytes 786440 | tf_op jit(solution)/shard_map/ppermute | solution.py:460
  15.8 0.6 mask_rights.1
  16.5 0.7 collective-permute-start.8
  17.1 2.1 %collective-permute-done.5.refs_1_ = bf16[2,256,256]{2,1,0:T(8,128)(2,1)S(1)} collective-permute-done((bf16[2,256,256]{2,1,0:T(8,128)(2,1)}, bf16[2,256,256]{2,1,0:T(8,128)(2,1)S(1)}, u32[]{:S(2)}, u32[]{:S(2)}) %collective-permute-start.5) | collective-permute-done | bytes 262176 | tf_op jit(solution)/shard_map/ppermute | solution.py:460
  19.3 2.9 %collective-permute-start.9 = (bf16[256,256]{1,0:T(8,128)(2,1)S(1)}, bf16[256,256]{1,0:T(8,128)(2,1)S(1)}, u32[]{:S(2)}, u32[]{:S(2)}) collective-permute-start(bf16[256,256]{1,0:T(8,128)(2,1)S(1)} %get-tuple-element.42), channel_id=1, source_target_pairs={{0,64},{32,96},{64,0},{96,32},{1,65},{33,97},{65,1},{97,33},{2,66}... | collective-permute-start | bytes 393224 | tf_op jit(solution)/shard_map/ppermute | solution.py:460
  22.2 1.5 %collective-permute-start.10 = (bf16[256,256]{1,0:T(8,128)(2,1)S(1)}, bf16[256,256]{1,0:T(8,128)(2,1)S(1)}, u32[]{:S(2)}, u32[]{:S(2)}) collective-permute-start(bf16[256,256]{1,0:T(8,128)(2,1)S(1)} %get-tuple-element.43), channel_id=1, source_target_pairs={{0,96},{32,64},{64,32},{96,0},{1,97},{33,65},{65,33},{97,1},{2,98}... | collective-permute-start | bytes 393224 | tf_op jit(solution)/shard_map/ppermute | solution.py:460
  23.8 2.9 %observable_weights.2.refs_3_.refs_5_ = bf16[2,4,64,1024]{3,2,1,0:T(8,128)(2,1)S(1)} custom-call(bf16[8,64,64]{2,1,0:T(8,128)(2,1)S(1)} %bitcast.20, bf16[288,1024]{1,0:T(8,128)(2,1)S(1)} %collective-permute-done.q_ref.refs_1_, bf16[2,8,16,16]{3,2,1,0:T(8,128)(2,1)S(1)} %copy-done.7, bf16[256,256]{1,0:T(8,128)(2,1)S(1)} %get-tuple-element.31.refs_3_.refs_4_, ...), custom_call_target="tpu_custom_call" | custom-call | flops 3000000000 | bytes 2097152 | tf_op jit(solution)/shard_map/observable_weights/pallas_call | solution.py:368
  26.7 2.3 %pack_second.1 = (bf16[3,256,256]{2,1,0:T(8,128)(2,1)S(1)}, bf16[3,256,256]{2,1,0:T(8,128)(2,1)S(1)}, bf16[3,256,256]{2,1,0:T(8,128)(2,1)S(1)}, bf16[3,256,256]{2,1,0:T(8,128)(2,1)S(1)}) custom-call(s32[1,8]{1,0:T(1,128)S(1)} %copy-done.3, bf16[8,64,1024]{2,1,0:T(8,128)(2,1)S(1)} %bitcast.15, bf16[8,256,256]{2,1,0:T(8,128)(2,1)S(1)} %bitcast.17, ...), custom_call_target="tpu_custom_call" | custom-call | flops 1000000 | bytes 2097152 | tf_op jit(solution)/shard_map/pack_second/pallas_call | solution.py:147
  29.0 0.1 collective-permute-start.2
  29.1 2.3 %collective-permute-start.3 = (bf16[3,256,256]{2,1,0:T(8,128)(2,1)S(1)}, bf16[3,256,256]{2,1,0:T(8,128)(2,1)S(1)}, u32[]{:S(2)}, u32[]{:S(2)}) collective-permute-start(bf16[3,256,256]{2,1,0:T(8,128)(2,1)S(1)} %get-tuple-element.35), channel_id=1, source_target_pairs={{0,64},{32,96},{64,0},{96,32},{1,65},{33,97},{65,1},{97,33},{2,66}... | collective-permute-start | bytes 1179656 | tf_op jit(solution)/shard_map/ppermute | solution.py:460
  31.4 1.5 %collective-permute-start.4 = (bf16[3,256,256]{2,1,0:T(8,128)(2,1)S(1)}, bf16[3,256,256]{2,1,0:T(8,128)(2,1)S(1)}, u32[]{:S(2)}, u32[]{:S(2)}) collective-permute-start(bf16[3,256,256]{2,1,0:T(8,128)(2,1)S(1)} %get-tuple-element.36), channel_id=1, source_target_pairs={{0,96},{32,64},{64,32},{96,0},{1,97},{33,65},{65,33},{97,1},{2,98}... | collective-permute-start | bytes 1179656 | tf_op jit(solution)/shard_map/ppermute | solution.py:460
  33.0 1.7 %collective-permute-done.10.refs_7_ = bf16[256,256]{1,0:T(8,128)(2,1)S(1)} collective-permute-done((bf16[256,256]{1,0:T(8,128)(2,1)S(1)}, bf16[256,256]{1,0:T(8,128)(2,1)S(1)}, u32[]{:S(2)}, u32[]{:S(2)}) %collective-permute-start.10) | collective-permute-done | bytes 131104 | tf_op jit(solution)/shard_map/ppermute | solution.py:460
  34.7 12.8 %chain_first.1 = (bf16[1,64,1024]{2,1,0:T(8,128)(2,1)S(1)}, bf16[1,64,1024]{2,1,0:T(8,128)(2,1)S(1)}, bf16[1,64,1024]{2,1,0:T(8,128)(2,1)S(1)}, bf16[1,64,1024]{2,1,0:T(8,128)(2,1)S(1)}, f32[8,128]{1,0:T(8,128)S(1)}) custom-call(bf16[2,256,256]{2,1,0:T(8,128)(2,1)S(1)} %copy-done.6, bf16[2,256,256]{2,1,0:T(8,128)(2,1)S(1)} %collective-permute-done.5.refs_1_, ...), custom_call_target="tpu_custom_call" | custom-call | flops 12000000000 | bytes 4194304 | tf_op jit(solution)/shard_map/chain_first/pallas_call | solution.py:293
  47.5 2.9 %observable_weights.3.refs_10_.refs_6_ = bf16[2,4,64,1024]{3,2,1,0:T(8,128)(2,1)S(1)} custom-call(bf16[8,64,64]{2,1,0:T(8,128)(2,1)S(1)} %bitcast.21, bf16[288,1024]{1,0:T(8,128)(2,1)S(1)} %collective-permute-done.q_ref.refs_1_, bf16[2,8,16,16]{3,2,1,0:T(8,128)(2,1)S(1)} %copy-done.7, f32[8,128]{1,0:T(8,128)S(1)} %get-tuple-element.44.refs_3_.refs_5_, ...), custom_call_target="tpu_custom_call" | custom-call | flops 3000000000 | bytes 2097152 | tf_op jit(solution)/shard_map/observable_weights/pallas_call | solution.py:368
  50.4 12.8 %chain_second.1 = (bf16[2,64,1024]{2,1,0:T(8,128)(2,1)S(1)}, bf16[2,64,1024]{2,1,0:T(8,128)(2,1)S(1)}, bf16[2,64,1024]{2,1,0:T(8,128)(2,1)S(1)}, bf16[2,64,1024]{2,1,0:T(8,128)(2,1)S(1)}, f32[128,128]{1,0:T(8,128)S(1)}) custom-call(bf16[3,256,256]{2,1,0:T(8,128)(2,1)S(1)} %get-tuple-element.33.refs_9_.refs_0_, ...), custom_call_target="tpu_custom_call" | custom-call | flops 12000000000 | bytes 4194304 | tf_op jit(solution)/shard_map/chain_second/pallas_call | solution.py:293
  63.3 0.1 collective-permute-start.11
  63.4 1.6 %collective-permute-start.12 = (bf16[2,64,1024]{2,1,0:T(8,128)(2,1)S(1)}, bf16[2,64,1024]{2,1,0:T(8,128)(2,1)S(1)}, u32[]{:S(2)}, u32[]{:S(2)}) collective-permute-start(bf16[2,64,1024]{2,1,0:T(8,128)(2,1)S(1)} %get-tuple-element.52), channel_id=1, source_target_pairs={{0,64},{32,96},{64,0},{96,32},{1,65},{33,97},{65,1},{97,33},{2,66}... | collective-permute-start | bytes 786440 | tf_op jit(solution)/shard_map/ppermute | solution.py:460
  65.0 2.3 %collective-permute-start.13 = (bf16[2,64,1024]{2,1,0:T(8,128)(2,1)S(1)}, bf16[2,64,1024]{2,1,0:T(8,128)(2,1)S(1)}, u32[]{:S(2)}, u32[]{:S(2)}) collective-permute-start(bf16[2,64,1024]{2,1,0:T(8,128)(2,1)S(1)} %get-tuple-element.53), channel_id=1, source_target_pairs={{0,96},{32,64},{64,32},{96,0},{1,97},{33,65},{65,33},{97,1},{2,98}... | collective-permute-start | bytes 786440 | tf_op jit(solution)/shard_map/ppermute | solution.py:460
  67.2 20.6 %all_to_all.11 = f32[128,1,128]{2,1,0:T(1,128)S(1)} all-to-all(f32[128,1,128]{2,1,0:T(1,128)S(1)} %bitcast.22), channel_id=1, replica_groups=mesh['row'=4,'col'=32] {'row','col'}, dimensions={0} | all-to-all | bytes 131072 | tf_op jit(solution)/shard_map/all_to_all | solution.py:493
  87.8 2.2 %finish.1 = (bf16[8,64,1024]{2,1,0:T(8,128)(2,1)}, f32[1,8]{1,0:T(1,128)}, f32[2,8]{1,0:T(2,128)}) custom-call(f32[128,128]{1,0:T(8,128)S(1)} %bitcast.18, bf16[2,64,1024]{2,1,0:T(8,128)(2,1)S(1)} %get-tuple-element.50.refs_1_, bf16[2,64,1024]{2,1,0:T(8,128)(2,1)S(1)} %collective-permute-done.11.refs_2_, ...), custom_call_target="tpu_custom_call" | custom-call | flops 2000000 | bytes 2097152 | tf_op jit(solution)/shard_map/finish/pallas_call | solution.py:434
  (31 shorter events, 0.2 us)
Async XLA Ops:
  0.6 15.2 %copy-start.3 = (s32[1,8]{1,0:T(1,128)S(1)}, s32[1,8]{1,0:T(1,128)}, u32[]{:S(2)}) copy-start(s32[1,8]{1,0:T(1,128)} %refs_0_.3) | copy-start | bytes 100
  0.6 23.1 %copy-start.2 = (bf16[1,1,8,64,64]{4,3,2,1,0:T(8,128)(2,1)S(1)}, bf16[1,1,8,64,64]{4,3,2,1,0:T(8,128)(2,1)}, u32[]{:S(2)}) copy-start(bf16[1,1,8,64,64]{4,3,2,1,0:T(8,128)(2,1)} %param.14) | copy-start | bytes 196612
  0.7 23.1 %copy-start.7 = (bf16[2,8,16,16]{3,2,1,0:T(8,128)(2,1)S(1)}, bf16[2,8,16,16]{3,2,1,0:T(8,128)(2,1)}, u32[]{:S(2)}) copy-start(bf16[2,8,16,16]{3,2,1,0:T(8,128)(2,1)} %refs_2_.3) | copy-start | bytes 24580
  0.7 23.1 %copy-start.4 = (bf16[1,1,8,64,1024]{4,3,2,1,0:T(8,128)(2,1)S(1)}, bf16[1,1,8,64,1024]{4,3,2,1,0:T(8,128)(2,1)}, u32[]{:S(2)}) copy-start(bf16[1,1,8,64,1024]{4,3,2,1,0:T(8,128)(2,1)} %param.13) | copy-start | bytes 3145732
  4.6 11.2 %collective-permute-start = (bf16[288,1024]{1,0:T(8,128)(2,1)}, bf16[288,1024]{1,0:T(8,128)(2,1)S(1)}, u32[]{:S(2)}, u32[]{:S(2)}) collective-permute-start(bf16[288,1024]{1,0:T(8,128)(2,1)} %get-tuple-element.30), channel_id=1, source_target_pairs={{1,0},{2,1},{3,2},{4,3},{5,4},{6,5},{7,6},{8,7},{9,8},{10,9},{11,1... | collective-permute-start | bytes 1769480 | tf_op jit(solution)/shard_map/ppermute | solution.py:456
  6.1 16.1 %collective-permute-start.1 = (bf16[256,1024]{1,0:T(8,128)(2,1)}, bf16[256,1024]{1,0:T(8,128)(2,1)S(1)}, u32[]{:S(2)}, u32[]{:S(2)}) collective-permute-start(bf16[256,1024]{1,0:T(8,128)(2,1)} %get-tuple-element.32), channel_id=1, source_target_pairs={{1,0},{2,1},{3,2},{4,3},{5,4},{6,5},{7,6},{8,7},{9,8},{10,9},{11,1... | collective-permute-start | bytes 1572872 | tf_op jit(solution)/shard_map/ppermute | solution.py:456
  11.9 7.4 %collective-permute-start.5 = (bf16[2,256,256]{2,1,0:T(8,128)(2,1)}, bf16[2,256,256]{2,1,0:T(8,128)(2,1)S(1)}, u32[]{:S(2)}, u32[]{:S(2)}) collective-permute-start(bf16[2,256,256]{2,1,0:T(8,128)(2,1)} %get-tuple-element.38), channel_id=1, source_target_pairs={{0,32},{32,0},{64,96},{96,64},{1,33},{33,1},{65,97},{97,65},{2,34}... | collective-permute-start | bytes 786440 | tf_op jit(solution)/shard_map/ppermute | solution.py:460
  13.2 15.8 %collective-permute-start.6 = (bf16[2,256,256]{2,1,0:T(8,128)(2,1)}, bf16[2,256,256]{2,1,0:T(8,128)(2,1)S(1)}, u32[]{:S(2)}, u32[]{:S(2)}) collective-permute-start(bf16[2,256,256]{2,1,0:T(8,128)(2,1)} %get-tuple-element.39), channel_id=1, source_target_pairs={{0,64},{32,96},{64,0},{96,32},{1,65},{33,97},{65,1},{97,33},{2,66}... | collective-permute-start | bytes 786440 | tf_op jit(solution)/shard_map/ppermute | solution.py:460
  15.8 13.3 %collective-permute-start.7 = (bf16[2,256,256]{2,1,0:T(8,128)(2,1)}, bf16[2,256,256]{2,1,0:T(8,128)(2,1)S(1)}, u32[]{:S(2)}, u32[]{:S(2)}) collective-permute-start(bf16[2,256,256]{2,1,0:T(8,128)(2,1)} %get-tuple-element.40), channel_id=1, source_target_pairs={{0,96},{32,64},{64,32},{96,0},{1,97},{33,65},{65,33},{97,1},{2,98}... | collective-permute-start | bytes 786440 | tf_op jit(solution)/shard_map/ppermute | solution.py:460
  16.5 14.9 %collective-permute-start.8 = (bf16[256,256]{1,0:T(8,128)(2,1)S(1)}, bf16[256,256]{1,0:T(8,128)(2,1)S(1)}, u32[]{:S(2)}, u32[]{:S(2)}) collective-permute-start(bf16[256,256]{1,0:T(8,128)(2,1)S(1)} %get-tuple-element.41), channel_id=1, source_target_pairs={{0,32},{32,0},{64,96},{96,64},{1,33},{33,1},{65,97},{97,65},{2,34}... | collective-permute-start | bytes 393224 | tf_op jit(solution)/shard_map/ppermute | solution.py:460
  19.3 13.7 %collective-permute-start.9 = (bf16[256,256]{1,0:T(8,128)(2,1)S(1)}, bf16[256,256]{1,0:T(8,128)(2,1)S(1)}, u32[]{:S(2)}, u32[]{:S(2)}) collective-permute-start(bf16[256,256]{1,0:T(8,128)(2,1)S(1)} %get-tuple-element.42), channel_id=1, source_target_pairs={{0,64},{32,96},{64,0},{96,32},{1,65},{33,97},{65,1},{97,33},{2,66}... | collective-permute-start | bytes 393224 | tf_op jit(solution)/shard_map/ppermute | solution.py:460
  22.2 12.5 %collective-permute-start.10 = (bf16[256,256]{1,0:T(8,128)(2,1)S(1)}, bf16[256,256]{1,0:T(8,128)(2,1)S(1)}, u32[]{:S(2)}, u32[]{:S(2)}) collective-permute-start(bf16[256,256]{1,0:T(8,128)(2,1)S(1)} %get-tuple-element.43), channel_id=1, source_target_pairs={{0,96},{32,64},{64,32},{96,0},{1,97},{33,65},{65,33},{97,1},{2,98}... | collective-permute-start | bytes 393224 | tf_op jit(solution)/shard_map/ppermute | solution.py:460
  23.7 2.9 %copy-start = (bf16[1,1,8,64,1024]{4,3,2,1,0:T(8,128)(2,1)S(1)}, bf16[1,1,8,64,1024]{4,3,2,1,0:T(8,128)(2,1)}, u32[]{:S(2)}) copy-start(bf16[1,1,8,64,1024]{4,3,2,1,0:T(8,128)(2,1)} %param.11) | copy-start | bytes 3145732
  23.8 2.9 %copy-start.1 = (bf16[1,1,8,256,256]{4,3,2,1,0:T(8,128)(2,1)S(1)}, bf16[1,1,8,256,256]{4,3,2,1,0:T(8,128)(2,1)}, u32[]{:S(2)}) copy-start(bf16[1,1,8,256,256]{4,3,2,1,0:T(8,128)(2,1)} %param.10) | copy-start | bytes 3145732
  26.7 8.1 %copy-start.5 = (bf16[1,8,64,1024]{3,2,1,0:T(8,128)(2,1)S(1)}, bf16[1,8,64,1024]{3,2,1,0:T(8,128)(2,1)}, u32[]{:S(2)}) copy-start(bf16[1,8,64,1024]{3,2,1,0:T(8,128)(2,1)} %param.9) | copy-start | bytes 3145732
  26.7 8.1 %copy-start.6 = (bf16[2,256,256]{2,1,0:T(8,128)(2,1)S(1)}, bf16[2,256,256]{2,1,0:T(8,128)(2,1)}, u32[]{:S(2)}) copy-start(bf16[2,256,256]{2,1,0:T(8,128)(2,1)} %get-tuple-element.37.refs_0_) | copy-start | bytes 786436
  26.7 8.1 %copy-start.8 = (bf16[1024,1024]{1,0:T(8,128)(2,1)S(1)}, bf16[1024,1024]{1,0:T(8,128)(2,1)}, u32[]{:S(2)}) copy-start(bf16[1024,1024]{1,0:T(8,128)(2,1)} %constant.2.clone.refs_8_.refs_4_) | copy-start | bytes 6291460
  29.0 21.4 %collective-permute-start.2 = (bf16[3,256,256]{2,1,0:T(8,128)(2,1)S(1)}, bf16[3,256,256]{2,1,0:T(8,128)(2,1)S(1)}, u32[]{:S(2)}, u32[]{:S(2)}) collective-permute-start(bf16[3,256,256]{2,1,0:T(8,128)(2,1)S(1)} %get-tuple-element.34), channel_id=1, source_target_pairs={{0,32},{32,0},{64,96},{96,64},{1,33},{33,1},{65,97},{97,65},{2,34}... | collective-permute-start | bytes 1179656 | tf_op jit(solution)/shard_map/ppermute | solution.py:460
  29.1 21.3 %collective-permute-start.3 = (bf16[3,256,256]{2,1,0:T(8,128)(2,1)S(1)}, bf16[3,256,256]{2,1,0:T(8,128)(2,1)S(1)}, u32[]{:S(2)}, u32[]{:S(2)}) collective-permute-start(bf16[3,256,256]{2,1,0:T(8,128)(2,1)S(1)} %get-tuple-element.35), channel_id=1, source_target_pairs={{0,64},{32,96},{64,0},{96,32},{1,65},{33,97},{65,1},{97,33},{2,66}... | collective-permute-start | bytes 1179656 | tf_op jit(solution)/shard_map/ppermute | solution.py:460
  31.4 19.0 %collective-permute-start.4 = (bf16[3,256,256]{2,1,0:T(8,128)(2,1)S(1)}, bf16[3,256,256]{2,1,0:T(8,128)(2,1)S(1)}, u32[]{:S(2)}, u32[]{:S(2)}) collective-permute-start(bf16[3,256,256]{2,1,0:T(8,128)(2,1)S(1)} %get-tuple-element.36), channel_id=1, source_target_pairs={{0,96},{32,64},{64,32},{96,0},{1,97},{33,65},{65,33},{97,1},{2,98}... | collective-permute-start | bytes 1179656 | tf_op jit(solution)/shard_map/ppermute | solution.py:460
  63.3 24.5 %collective-permute-start.11 = (bf16[2,64,1024]{2,1,0:T(8,128)(2,1)S(1)}, bf16[2,64,1024]{2,1,0:T(8,128)(2,1)S(1)}, u32[]{:S(2)}, u32[]{:S(2)}) collective-permute-start(bf16[2,64,1024]{2,1,0:T(8,128)(2,1)S(1)} %get-tuple-element.51), channel_id=1, source_target_pairs={{0,32},{32,0},{64,96},{96,64},{1,33},{33,1},{65,97},{97,65},{2,34}... | collective-permute-start | bytes 786440 | tf_op jit(solution)/shard_map/ppermute | solution.py:460
  63.4 24.4 %collective-permute-start.12 = (bf16[2,64,1024]{2,1,0:T(8,128)(2,1)S(1)}, bf16[2,64,1024]{2,1,0:T(8,128)(2,1)S(1)}, u32[]{:S(2)}, u32[]{:S(2)}) collective-permute-start(bf16[2,64,1024]{2,1,0:T(8,128)(2,1)S(1)} %get-tuple-element.52), channel_id=1, source_target_pairs={{0,64},{32,96},{64,0},{96,32},{1,65},{33,97},{65,1},{97,33},{2,66}... | collective-permute-start | bytes 786440 | tf_op jit(solution)/shard_map/ppermute | solution.py:460
  65.0 22.8 %collective-permute-start.13 = (bf16[2,64,1024]{2,1,0:T(8,128)(2,1)S(1)}, bf16[2,64,1024]{2,1,0:T(8,128)(2,1)S(1)}, u32[]{:S(2)}, u32[]{:S(2)}) collective-permute-start(bf16[2,64,1024]{2,1,0:T(8,128)(2,1)S(1)} %get-tuple-element.53), channel_id=1, source_target_pairs={{0,96},{32,64},{64,32},{96,0},{1,97},{33,65},{65,33},{97,1},{2,98}... | collective-permute-start | bytes 786440 | tf_op jit(solution)/shard_map/ppermute | solution.py:460
